TPU v7x, 32 devices: a whole 2x2x4 slice. The times are simulated.
32 devices in a mesh: dp: 16 (over z, x, core), tensor: 2 (over y).
Axes of the slice: x: 2, y: 2, z: 4, core: 2. Of those that a mesh axis runs over, the one named last changes fastest.
Arguments:
- tokens: bfloat16 [4096, 1536], P(('dp', 'tensor')), may hold values from -6 to 6
- cotangent: bfloat16 [4096, 1536], P(('dp', 'tensor')), may hold values from -12 to 12
- doc_lengths: int32 [16, 4], P('dp'), may hold values from 1 to 128, 256 in all within a row
- norm_attn: bfloat16 [2, 1536], replicated, may hold values from 0.5 to 1.5
- norm_ffn: bfloat16 [2, 1536], replicated, may hold values from 0.5 to 1.5
- w_qkv: bfloat16 [2, 1536, 2048], P(None, 'dp', 'tensor'), may hold values from -0.15625 to 0.15625
- b_qkv: bfloat16 [2, 2048], P(None, 'tensor'), may hold values from -3 to 3
- w_out: bfloat16 [2, 1536, 1536], P(None, 'dp', 'tensor'), may hold values from -0.4375 to 0.4375
- w_gateup: bfloat16 [2, 1536, 17920], P(None, 'dp', 'tensor'), may hold values from -0.15625 to 0.15625
- w_down: bfloat16 [2, 1536, 8960], P(None, 'dp', 'tensor'), may hold values from -0.125 to 0.125
Outputs:
- output: bfloat16 [4096, 1536], P(('dp', 'tensor'))
- d_tokens: float32 [4096, 1536], P(('dp', 'tensor'))
- d_norm_attn: float32 [2, 1536], replicated
- d_norm_ffn: float32 [2, 1536], replicated
- d_w_qkv: float32 [2, 1536, 2048], P(None, 'dp', 'tensor')
- d_b_qkv: float32 [2, 2048], P(None, 'tensor')
- d_w_out: float32 [2, 1536, 1536], P(None, 'dp', 'tensor')
- d_w_gateup: float32 [2, 1536, 17920], P(None, 'dp', 'tensor')
- d_w_down: float32 [2, 1536, 8960], P(None, 'dp', 'tensor')
Inputs may be any that keep to these rules, and one draw needn't show every extreme that they name: `doc_lengths`: each sequence's document lengths add up to 256; in every sequence the longest is 128.
All inputs are finite; a program needn't handle non-finite values.
Results may differ from a plain program's by a relative error of at most 0.02.
Values may be sent and summed in bfloat16 or wider, within the bound.
A program may use at most 448 MiB of HBM per device.

v0:
```python
import math

import jax
import jax.numpy as jnp
from jax import lax
from jax.sharding import PartitionSpec as P

H = 12
KV = 2
HD = 128


def rms_factor(rows):
    return lax.rsqrt(jnp.mean(rows * rows, axis=-1, keepdims=True) + 1e-06)


def rotate(values):
    half = values.shape[-1] // 2
    return jnp.concatenate([-values[..., half:], values[..., :half]], axis=-1)


def rotate_back(values):
    half = values.shape[-1] // 2
    return jnp.concatenate([values[..., half:], -values[..., :half]], axis=-1)


def doc_layout(lens, count):
    bounds = jnp.cumsum(lens, dtype=jnp.int32)
    rows = jnp.arange(count, dtype=jnp.int32)
    after = (rows[:, None] >= bounds[None, :]).astype(jnp.int32)
    doc = jnp.sum(after, axis=1, dtype=jnp.int32)
    start = jnp.sum(after * lens[None, :], axis=1, dtype=jnp.int32)
    positions = rows - start
    allowed = (doc[:, None] == doc[None, :]) & (rows[:, None] >= rows[None, :])
    return (positions, allowed)


def rope_tables(positions, width):
    index = jnp.arange(width // 2, dtype=jnp.float32)
    freq = jnp.exp(-(2.0 * index / width) * math.log(1000000.0))
    angle = positions.astype(jnp.float32)[:, None] * freq[None, :]
    return (
        jnp.concatenate([jnp.cos(angle)] * 2, axis=1),
        jnp.concatenate([jnp.sin(angle)] * 2, axis=1),
    )


def contract_last(left, right):
    return lax.dot_general(
        left, right, (((1,), (1,)), ((), ())), preferred_element_type=jnp.float32
    )


def contract_first(left, right):
    return lax.dot_general(
        left, right, (((0,), (0,)), ((), ())), preferred_element_type=jnp.float32
    )


def spread_rows(rows):
    return lax.all_gather(rows, "tensor", axis=0, tiled=True)


def spread_grads(rows):
    return lax.all_gather(rows, "tensor", axis=0, tiled=True)


def branch_sum(left, weight, count):

    def term(start, number):
        return contract_last(left, weight)

    return lax.psum_scatter(
        term(jnp.int32(0), count * lax.axis_size("tensor")),
        "tensor",
        scatter_dimension=0,
        tiled=True,
    )


def branch_back(left, weight, count):

    def term(start, number):
        return contract_last(left, weight)

    return lax.psum_scatter(
        term(jnp.int32(0), count * lax.axis_size("tensor")),
        "tensor",
        scatter_dimension=0,
        tiled=True,
    )


def norm_back(upstream, rows, factor, gain):
    scaled = upstream * gain
    gain_part = jnp.sum(upstream * rows * factor, axis=0)
    result = factor * scaled - rows * factor**3 * jnp.mean(scaled * rows, axis=-1, keepdims=True)
    return (result, gain_part)


def local(
    tokens, cotangent, doc_lengths, norm_attn, norm_ffn, w_qkv, b_qkv, w_out, w_gateup, w_down
):
    tensor_size = lax.axis_size("tensor")
    count = tokens.shape[0]
    length = count * tensor_size
    layers = w_qkv.shape[0]
    kv_local = KV // tensor_size
    groups = H // KV
    q_width = kv_local * groups * HD
    kv_width = kv_local * HD
    scale = 1.0 / math.sqrt(HD)
    positions, allowed = doc_layout(doc_lengths[0], length)
    cosine, sine = rope_tables(positions, HD)
    cos_q = cosine[:, None, None, :]
    sin_q = sine[:, None, None, :]
    cos_k = cosine[:, None, :]
    sin_k = sine[:, None, :]
    gain_attn = norm_attn.astype(jnp.float32)
    gain_ffn = norm_ffn.astype(jnp.float32)
    saved = []
    state = tokens.astype(jnp.float32)
    for layer in range(layers):
        qkv_w, out_w = (
            lax.all_gather(w_qkv[layer], "dp", axis=0, tiled=True),
            lax.all_gather(w_out[layer], "dp", axis=0, tiled=True),
        )
        factor_a = rms_factor(state)
        xa_all = spread_rows((state * factor_a * gain_attn[layer]).astype(jnp.bfloat16))
        lin = jnp.dot(xa_all, qkv_w, preferred_element_type=jnp.float32) + b_qkv[layer].astype(
            jnp.float32
        )
        query = lin[:, :q_width].reshape(length, kv_local, groups, HD)
        key = lin[:, q_width : q_width + kv_width].reshape(length, kv_local, HD)
        value = lin[:, q_width + kv_width :].reshape(length, kv_local, HD).astype(jnp.bfloat16)
        query = (query * cos_q + rotate(query) * sin_q).astype(jnp.bfloat16)
        key = (key * cos_k + rotate(key) * sin_k).astype(jnp.bfloat16)
        raw = jnp.einsum("qkgd,pkd->kgqp", query, key, preferred_element_type=jnp.float32)
        scores = jnp.where(allowed, raw * scale, -1e30)
        top = jnp.max(scores, axis=-1, keepdims=True)
        expo = jnp.exp(scores - top)
        total = jnp.sum(expo, axis=-1, keepdims=True)
        probs = expo / total
        log_total = top + jnp.log(total)
        attended = (
            jnp.einsum(
                "kgqp,pkd->qkgd",
                probs.astype(jnp.bfloat16),
                value,
                preferred_element_type=jnp.float32,
            )
            .reshape(length, q_width)
            .astype(jnp.bfloat16)
        )
        middle = state + branch_sum(attended, out_w, count)
        gu_w, down_w = (
            lax.all_gather(w_gateup[layer], "dp", axis=0, tiled=True),
            lax.all_gather(w_down[layer], "dp", axis=0, tiled=True),
        )
        factor_f = rms_factor(middle)
        xf_all = spread_rows((middle * factor_f * gain_ffn[layer]).astype(jnp.bfloat16))
        gate_up = jnp.dot(xf_all, gu_w, preferred_element_type=jnp.float32)
        half = gate_up.shape[1] // 2
        gate = gate_up[:, :half]
        up = gate_up[:, half:]
        act = (jax.nn.silu(gate) * up).astype(jnp.bfloat16)
        after = middle + branch_sum(act, down_w, count)
        saved.append(
            (
                state,
                factor_a,
                xa_all,
                query,
                key,
                value,
                log_total,
                attended,
                middle,
                factor_f,
                xf_all,
                gate,
                up,
                act,
            )
        )
        state = after
    output = state.astype(jnp.bfloat16)
    grad = cotangent.astype(jnp.float32)
    grads_qkv, grads_out, grads_gu, grads_down, grads_bias, grads_ga, grads_gf = (
        [],
        [],
        [],
        [],
        [],
        [],
        [],
    )
    for layer in reversed(range(layers)):
        (
            state_in,
            factor_a,
            xa_all,
            query,
            key,
            value,
            log_total,
            attended,
            middle,
            factor_f,
            xf_all,
            gate,
            up,
            act,
        ) = saved[layer]
        gu_w, down_w = (
            lax.all_gather(w_gateup[layer], "dp", axis=0, tiled=True),
            lax.all_gather(w_down[layer], "dp", axis=0, tiled=True),
        )
        gm_all = spread_grads(grad.astype(jnp.bfloat16))
        d_act = jnp.dot(gm_all, down_w, preferred_element_type=jnp.float32)
        sig = jax.nn.sigmoid(gate)
        d_gate = d_act * up * sig * (1.0 + gate * (1.0 - sig))
        d_up = d_act * gate * sig
        d_gu = jnp.concatenate([d_gate, d_up], axis=1).astype(jnp.bfloat16)
        d_xf = branch_back(d_gu, gu_w, count)
        d_mid, part_f = norm_back(d_xf, middle, factor_f, gain_ffn[layer])
        grad = grad + d_mid
        d_gateup = contract_first(xf_all, d_gu)
        d_down = contract_first(gm_all, act)
        shard_gu, shard_down = (
            lax.psum_scatter(d_gateup, "dp", scatter_dimension=0, tiled=True),
            lax.psum_scatter(d_down, "dp", scatter_dimension=0, tiled=True),
        )
        qkv_w, out_w = (
            lax.all_gather(w_qkv[layer], "dp", axis=0, tiled=True),
            lax.all_gather(w_out[layer], "dp", axis=0, tiled=True),
        )
        ga_all = spread_grads(grad.astype(jnp.bfloat16))
        d_att = jnp.dot(ga_all, out_w, preferred_element_type=jnp.float32).astype(jnp.bfloat16)
        raw = jnp.einsum("qkgd,pkd->kgqp", query, key, preferred_element_type=jnp.float32)
        scores = jnp.where(allowed, raw * scale, -1e30)
        probs = jnp.exp(scores - log_total)
        d_att4 = d_att.reshape(length, kv_local, groups, HD)
        d_probs = jnp.einsum("qkgd,pkd->kgqp", d_att4, value, preferred_element_type=jnp.float32)
        centre = jnp.sum(probs * d_probs, axis=-1, keepdims=True)
        d_raw = (probs * (d_probs - centre) * scale).astype(jnp.bfloat16)
        d_query = jnp.einsum("kgqp,pkd->qkgd", d_raw, key, preferred_element_type=jnp.float32)
        d_key = jnp.einsum("kgqp,qkgd->pkd", d_raw, query, preferred_element_type=jnp.float32)
        d_value = jnp.einsum(
            "kgqp,qkgd->pkd", probs.astype(jnp.bfloat16), d_att4, preferred_element_type=jnp.float32
        )
        d_query = d_query * cos_q + rotate_back(d_query * sin_q)
        d_key = d_key * cos_k + rotate_back(d_key * sin_k)
        d_lin = jnp.concatenate(
            [
                d_query.reshape(length, q_width),
                d_key.reshape(length, kv_width),
                d_value.reshape(length, kv_width),
            ],
            axis=1,
        )
        grads_bias.append(jnp.sum(d_lin, axis=0))
        d_lin_low = d_lin.astype(jnp.bfloat16)
        d_xa = branch_back(d_lin_low, qkv_w, count)
        d_in, part_a = norm_back(d_xa, state_in, factor_a, gain_attn[layer])
        grad = grad + d_in
        d_wqkv = contract_first(xa_all, d_lin_low)
        d_wout = contract_first(ga_all, attended)
        shard_qkv, shard_wout = (
            lax.psum_scatter(d_wqkv, "dp", scatter_dimension=0, tiled=True),
            lax.psum_scatter(d_wout, "dp", scatter_dimension=0, tiled=True),
        )
        grads_qkv.append(shard_qkv)
        grads_out.append(shard_wout)
        grads_gu.append(shard_gu)
        grads_down.append(shard_down)
        grads_ga.append(part_a)
        grads_gf.append(part_f)

    def ordered(items):
        return jnp.stack(items[::-1], axis=0)

    sum_ga, sum_gf, sum_bias = lax.psum(
        (ordered(grads_ga), ordered(grads_gf), ordered(grads_bias)), "dp"
    )
    full_ga, full_gf = lax.psum((sum_ga, sum_gf), "tensor")
    return (
        output,
        grad,
        full_ga,
        full_gf,
        ordered(grads_qkv),
        sum_bias,
        ordered(grads_out),
        ordered(grads_gu),
        ordered(grads_down),
    )


def solution(mesh):
    placed = (
        P(("dp", "tensor"), None),
        P(("dp", "tensor"), None),
        P("dp", None),
        P(),
        P(),
        P(None, "dp", "tensor"),
        P(None, "tensor"),
        P(None, "dp", "tensor"),
        P(None, "dp", "tensor"),
        P(None, "dp", "tensor"),
    )
    return jax.shard_map(
        local,
        mesh=mesh,
        in_specs=placed,
        out_specs=(
            P(("dp", "tensor"), None),
            P(("dp", "tensor"), None),
            P(),
            P(),
            P(None, "dp", "tensor"),
            P(None, "tensor"),
            P(None, "dp", "tensor"),
            P(None, "dp", "tensor"),
            P(None, "dp", "tensor"),
        ),
        check_vma=False,
    )
```

profile of v0, /device:TPU:26, one launch (start us, length us, event | category | flops | bytes accessed | tf_op | source)
XLA Modules:
  0.0 2964.0 jit_solution(7250814748019625150)
XLA Ops:
  15.2 11.5 all_gather.56
  28.0 27.2 all-gather.17.cloned.1.call-done
  69.4 29.8 %all-gather.19.cloned.1.call-done = bf16[1,1536,768]{2,1,0:T(8,128)(2,1)} async-done(((bf16[1,96,768]{2,1,0:T(8,128)(2,1)}), bf16[1,1536,768]{2,1,0:T(8,128)(2,1)}) %all-gather.19.cloned.1.call-update) | async-done | bytes 2359312 | tf_op jit(solution)/shard_map/all_gather | solution.py:126
  103.0 4.0 fusion.117
  110.5 19.6 reduce-scatter.17.cloned.1.call-done
  132.7 11.8 all_gather.59
  144.5 126.5 %all-gather.21.cloned.1.call-done = bf16[1,1536,8960]{2,1,0:T(8,128)(2,1)} async-done(((bf16[1,96,8960]{2,1,0:T(8,128)(2,1)}), bf16[1,1536,8960]{2,1,0:T(8,128)(2,1)}) %all-gather.21.cloned.1.call-update) | async-done | bytes 27525136 | tf_op jit(solution)/shard_map/all_gather | solution.py:157
  271.0 12.9 fusion.6
  290.2 89.4 %all-gather.23.cloned.1.call-done = bf16[1,1536,4480]{2,1,0:T(8,128)(2,1)} async-done(((bf16[1,96,4480]{2,1,0:T(8,128)(2,1)}), bf16[1,1536,4480]{2,1,0:T(8,128)(2,1)}) %all-gather.23.cloned.1.call-update) | async-done | bytes 13762576 | tf_op jit(solution)/shard_map/all_gather | solution.py:158
  379.6 10.6 fusion.14
  391.8 25.8 reduce-scatter.19.cloned.1.call-done
  419.9 11.5 all_gather.62
  431.4 32.4 %all-gather.25.cloned.1.call-done = bf16[1,1536,1024]{2,1,0:T(8,128)(2,1)} async-done(((bf16[1,96,1024]{2,1,0:T(8,128)(2,1)}), bf16[1,1536,1024]{2,1,0:T(8,128)(2,1)}) %all-gather.25.cloned.1.call-update) | async-done | bytes 3145744 | tf_op jit(solution)/shard_map/all_gather | solution.py:125
  482.2 25.1 all-gather.27.cloned.1.call-done
  512.4 19.8 all_gather.68
  532.2 11.9 reduce-scatter.21.cloned.1.call-done
  546.8 12.1 all_gather.65
  558.9 126.1 %all-gather.29.cloned.1.call-done = bf16[1,1536,8960]{2,1,0:T(8,128)(2,1)} async-done(((bf16[1,96,8960]{2,1,0:T(8,128)(2,1)}), bf16[1,1536,8960]{2,1,0:T(8,128)(2,1)}) %all-gather.29.cloned.1.call-update) | async-done | bytes 27525136 | tf_op jit(solution)/shard_map/all_gather | solution.py:157
  685.0 15.0 fusion.2
  700.1 93.7 %all-gather.31.cloned.1.call-done = bf16[1,1536,4480]{2,1,0:T(8,128)(2,1)} async-done(((bf16[1,96,4480]{2,1,0:T(8,128)(2,1)}), bf16[1,1536,4480]{2,1,0:T(8,128)(2,1)}) %all-gather.31.cloned.1.call-update) | async-done | bytes 13762576 | tf_op jit(solution)/shard_map/all_gather | solution.py:158
  793.8 11.7 multiply_convert_fusion.3
  806.9 14.2 fusion
  821.1 10.7 fusion.10
  833.2 15.2 reduce-scatter.25.cloned.1.call-done
  851.1 25.7 reduce-scatter.23.cloned.1.call-done
  880.0 11.9 all_gather.69
  908.3 26.2 reduce-scatter.27.cloned.1.call-done
  939.0 11.5 all_gather.70
  950.5 12.9 multiply_convert_fusion.1
  964.8 14.2 fusion.4
  979.9 25.5 reduce-scatter.29.cloned.1.call-done
  1010.0 11.7 all_gather.71
  1036.6 4.0 fusion.128
  1055.6 12.7 convolution_bitcast_fusion
  1069.4 14.1 fusion.129
  1084.7 23.0 fusion.25
  1108.8 22.5 fusion.24
  1133.9 54.5 %all-reduce = (f32[2,1536]{1,0:T(2,128)S(1)}, f32[2,1536]{1,0:T(2,128)S(1)}, f32[2,1024]{1,0:T(2,128)}) all-reduce(f32[2,1536]{1,0:T(2,128)S(1)} %get-tuple-element.101, f32[2,1536]{1,0:T(2,128)S(1)} %get-tuple-element.102, f32[2,1024]{1,0:T(2,128)S(1)} %pad_maximum_fusion.16), channel_id=1, replica_groups=mesh['dp'=16,'tensor'=2] {'dp'}, use_global_device_ids=true, to_apply=%region_27.28 | all-reduce | flops 8192 | bytes 65536 | tf_op jit(solution)/shard_map/psum | solution.py:283
  1188.5 8.2 all-reduce.1
  1199.1 19.8 reduce-scatter.37.cloned.1.call-done
  1220.7 87.4 %reduce-scatter.35.cloned.1.call-done = f32[96,1024]{1,0:T(8,128)} async-done(((f32[1536,1024]{1,0:T(8,128)}), f32[96,1024]{1,0:T(8,128)}) %reduce-scatter.35.cloned.1.call-update) | async-done | bytes 393232 | tf_op jit(solution)/shard_map/reduce_scatter | solution.py:270
  1308.2 88.8 %reduce-scatter.33.cloned.1.call-done = f32[96,1024]{1,0:T(8,128)} async-done(((f32[1536,1024]{1,0:T(8,128)}), f32[96,1024]{1,0:T(8,128)}) %reduce-scatter.33.cloned.1.call-update) | async-done | bytes 393232 | tf_op jit(solution)/shard_map/reduce_scatter | solution.py:270
  1399.1 263.9 %reduce-scatter.47.cloned.1.call-done = f32[96,4480]{1,0:T(8,128)} async-done(((f32[1536,4480]{1,0:T(8,128)}), f32[96,4480]{1,0:T(8,128)}) %reduce-scatter.47.cloned.1.call-update) | async-done | bytes 1720336 | tf_op jit(solution)/shard_map/reduce_scatter | solution.py:232
  1663.0 266.7 %reduce-scatter.45.cloned.1.call-done = f32[96,4480]{1,0:T(8,128)} async-done(((f32[1536,4480]{1,0:T(8,128)}), f32[96,4480]{1,0:T(8,128)}) %reduce-scatter.45.cloned.1.call-update) | async-done | bytes 1720336 | tf_op jit(solution)/shard_map/reduce_scatter | solution.py:232
  1929.7 4.0 pad_maximum_fusion.3
  1933.7 506.6 %reduce-scatter.43.cloned.1.call-done = f32[96,8960]{1,0:T(8,128)} async-done(((f32[1536,8960]{1,0:T(8,128)}), f32[96,8960]{1,0:T(8,128)}) %reduce-scatter.43.cloned.1.call-update) | async-done | bytes 3440656 | tf_op jit(solution)/shard_map/reduce_scatter | solution.py:231
  2440.3 510.3 %reduce-scatter.41.cloned.1.call-done = f32[96,8960]{1,0:T(8,128)} async-done(((f32[1536,8960]{1,0:T(8,128)}), f32[96,8960]{1,0:T(8,128)}) %reduce-scatter.41.cloned.1.call-update) | async-done | bytes 3440656 | tf_op jit(solution)/shard_map/reduce_scatter | solution.py:231
  2950.6 6.4 pad_maximum_fusion
  (319 shorter events, 147.6 us)
Async XLA Ops:
  7.2 7.8 copy-start.5
  7.2 19.5 copy-start.68
  7.2 48.0 %all-gather.17.cloned.1.call-start = ((), (), s32[]{:S(2)}) async-start(), calls=%async_computation.32 | async-start | bytes 3342336 | tf_op jit(solution)/shard_map/all_gather | solution.py:125
  9.1 90.1 %all-gather.19.cloned.1.call-start = ((), (), s32[]{:S(2)}) async-start(), calls=%async_computation.33 | async-start | bytes 2506752 | tf_op jit(solution)/shard_map/all_gather | solution.py:126
  10.9 119.2 %reduce-scatter.17.cloned.1.call-start = ((), (), s32[]{:S(2)}) async-start(), calls=%async_computation.16 | async-start | bytes 2359296 | tf_op jit(solution)/shard_map/reduce_scatter | solution.py:73
  12.8 45.2 %copy-start.57 = (f32[1536]{0:T(1024)}, f32[1536]{0:T(1024)S(1)}, u32[]{:S(2)}) copy-start(f32[1536]{0:T(1024)S(1)} %get-tuple-element.20) | copy-start | bytes 18436
  15.0 43.1 %copy-start.73 = (f32[128]{0:T(128)}, f32[128]{0:T(128)S(1)}, u32[]{:S(2)}) copy-start(f32[128]{0:T(128)S(1)} %get-tuple-element.78) | copy-start | bytes 1540
  26.7 31.4 %copy-start.19 = (bf16[256,1536]{1,0:T(8,128)(2,1)}, bf16[256,1536]{1,0:T(8,128)(2,1)S(1)}, u32[]{:S(2)}) copy-start(bf16[256,1536]{1,0:T(8,128)(2,1)S(1)} %all_gather.56) | copy-start | bytes 2359300
  27.5 38.7 %copy-start.52 = (pred[256,256]{0,1:T(8,128)(4,1)}, pred[256,256]{0,1:T(8,128)(4,1)S(1)}, u32[]{:S(2)}) copy-start(pred[256,256]{0,1:T(8,128)(4,1)S(1)} %fusion.85) | copy-start | bytes 196612
  59.1 7.1 copy-start.55
  60.7 5.5 copy-start.12
  64.2 4.0 copy-start.24
  103.0 168.0 %all-gather.21.cloned.1.call-start = ((), (), s32[]{:S(2)}) async-start(), calls=%async_computation.34 | async-start | bytes 29245440 | tf_op jit(solution)/shard_map/all_gather | solution.py:157
  107.0 2.9 copy-start.69
  107.0 272.6 %all-gather.23.cloned.1.call-start = ((), (), s32[]{:S(2)}) async-start(), calls=%async_computation.35 | async-start | bytes 14622720 | tf_op jit(solution)/shard_map/all_gather | solution.py:158
  109.8 307.8 %reduce-scatter.19.cloned.1.call-start = ((), (), s32[]{:S(2)}) async-start(), calls=%async_computation.17 | async-start | bytes 2359296 | tf_op jit(solution)/shard_map/reduce_scatter | solution.py:73
  131.4 286.2 %copy-start = (f32[128,1536]{1,0:T(8,128)}, f32[128,1536]{1,0:T(8,128)S(1)}, u32[]{:S(2)}) copy-start(f32[128,1536]{1,0:T(8,128)S(1)} %get-tuple-element.39) | copy-start | bytes 2359300
  284.0 3.5 copy-start.7
  390.3 73.5 %all-gather.25.cloned.1.call-start = ((), (), s32[]{:S(2)}) async-start(), calls=%async_computation.36 | async-start | bytes 3342336 | tf_op jit(solution)/shard_map/all_gather | solution.py:125
  391.0 116.2 %all-gather.27.cloned.1.call-start = ((), (), s32[]{:S(2)}) async-start(), calls=%async_computation.37 | async-start | bytes 2506752 | tf_op jit(solution)/shard_map/all_gather | solution.py:126
  391.8 72.0 %copy-start.75 = (f32[1,1024]{1,0:T(1,128)S(1)}, f32[1,1024]{1,0:T(1,128)}, u32[]{:S(2)}) copy-start(f32[1,1024]{1,0:T(1,128)} %get-tuple-element.73) | copy-start | bytes 12292
  391.8 152.3 %reduce-scatter.21.cloned.1.call-start = ((), (), s32[]{:S(2)}) async-start(), calls=%async_computation.18 | async-start | bytes 2359296 | tf_op jit(solution)/shard_map/reduce_scatter | solution.py:73
  419.5 44.3 %copy-start.71 = (f32[128]{0:T(128)}, f32[128]{0:T(128)S(1)}, u32[]{:S(2)}) copy-start(f32[128]{0:T(128)S(1)} %get-tuple-element.82) | copy-start | bytes 1540
  431.4 35.2 %copy-start.21 = (bf16[256,1536]{1,0:T(8,128)(2,1)}, bf16[256,1536]{1,0:T(8,128)(2,1)S(1)}, u32[]{:S(2)}) copy-start(bf16[256,1536]{1,0:T(8,128)(2,1)S(1)} %all_gather.62) | copy-start | bytes 2359300
  469.2 5.5 copy-start.14
  511.0 174.0 %all-gather.29.cloned.1.call-start = ((), (), s32[]{:S(2)}) async-start(), calls=%async_computation.38 | async-start | bytes 29245440 | tf_op jit(solution)/shard_map/all_gather | solution.py:157
  511.6 282.1 %all-gather.31.cloned.1.call-start = ((), (), s32[]{:S(2)}) async-start(), calls=%async_computation.39 | async-start | bytes 14622720 | tf_op jit(solution)/shard_map/all_gather | solution.py:158
  512.4 336.1 %reduce-scatter.25.cloned.1.call-start = ((), (), s32[]{:S(2)}) async-start(), calls=%async_computation.20 | async-start | bytes 2359296 | tf_op jit(solution)/shard_map/reduce_scatter | solution.py:86
  821.1 55.7 %reduce-scatter.23.cloned.1.call-start = ((), (), s32[]{:S(2)}) async-start(), calls=%async_computation.19 | async-start | bytes 2359296 | tf_op jit(solution)/shard_map/reduce_scatter | solution.py:73
  831.8 102.7 %reduce-scatter.27.cloned.1.call-start = ((), (), s32[]{:S(2)}) async-start(), calls=%async_computation.21 | async-start | bytes 2359296 | tf_op jit(solution)/shard_map/reduce_scatter | solution.py:86
  876.8 16.1 copy-start.40
  906.1 28.5 copy-start.3
  908.3 97.1 %reduce-scatter.29.cloned.1.call-start = ((), (), s32[]{:S(2)}) async-start(), calls=%async_computation.22 | async-start | bytes 2359296 | tf_op jit(solution)/shard_map/reduce_scatter | solution.py:86
  950.5 12.9 copy-start.37
  964.8 40.5 %copy-start.1 = (f32[128,1536]{1,0:T(8,128)S(1)}, f32[128,1536]{1,0:T(8,128)}, u32[]{:S(2)}) copy-start(f32[128,1536]{1,0:T(8,128)} %copy-done) | copy-start | bytes 2359300
  979.1 153.4 %reduce-scatter.31.cloned.1.call-start = ((), (), s32[]{:S(2)}) async-start(), calls=%async_computation.23 | async-start | bytes 2359296 | tf_op jit(solution)/shard_map/reduce_scatter | solution.py:86
  1007.3 14.3 copy-start.39
  1032.3 4.2 copy-start.48
  1036.6 162.5 %reduce-scatter.39.cloned.1.call-start = ((), (), s32[]{:S(2)}) async-start(), calls=%async_computation.27 | async-start | bytes 5013504 | tf_op jit(solution)/shard_map/reduce_scatter | solution.py:271
  1040.6 178.2 %reduce-scatter.37.cloned.1.call-start = ((), (), s32[]{:S(2)}) async-start(), calls=%async_computation.26 | async-start | bytes 5013504 | tf_op jit(solution)/shard_map/reduce_scatter | solution.py:271
  1044.7 263.5 %reduce-scatter.35.cloned.1.call-start = ((), (), s32[]{:S(2)}) async-start(), calls=%async_computation.25 | async-start | bytes 6684672 | tf_op jit(solution)/shard_map/reduce_scatter | solution.py:270
  1049.6 347.4 %reduce-scatter.33.cloned.1.call-start = ((), (), s32[]{:S(2)}) async-start(), calls=%async_computation.24 | async-start | bytes 6684672 | tf_op jit(solution)/shard_map/reduce_scatter | solution.py:270
  1054.5 608.5 %reduce-scatter.47.cloned.1.call-start = ((), (), s32[]{:S(2)}) async-start(), calls=%async_computation.31 | async-start | bytes 29245440 | tf_op jit(solution)/shard_map/reduce_scatter | solution.py:232
  1068.3 861.4 %reduce-scatter.45.cloned.1.call-start = ((), (), s32[]{:S(2)}) async-start(), calls=%async_computation.30 | async-start | bytes 29245440 | tf_op jit(solution)/shard_map/reduce_scatter | solution.py:232
  1083.5 1356.8 %reduce-scatter.43.cloned.1.call-start = ((), (), s32[]{:S(2)}) async-start(), calls=%async_computation.29 | async-start | bytes 58490880 | tf_op jit(solution)/shard_map/reduce_scatter | solution.py:231
  1107.7 1842.9 %reduce-scatter.41.cloned.1.call-start = ((), (), s32[]{:S(2)}) async-start(), calls=%async_computation.28 | async-start | bytes 58490880 | tf_op jit(solution)/shard_map/reduce_scatter | solution.py:231
  1131.3 65.4 %copy-start.35 = (f32[128,1536]{1,0:T(8,128)S(1)}, f32[128,1536]{1,0:T(8,128)}, u32[]{:S(2)}) copy-start(f32[128,1536]{1,0:T(8,128)} %get-tuple-element.29) | copy-start | bytes 2359300
  1131.3 65.4 %copy-start.76 = (f32[128]{0:T(128)S(1)}, f32[128]{0:T(128)}, u32[]{:S(2)}) copy-start(f32[128]{0:T(128)} %get-tuple-element.77) | copy-start | bytes 1540
  (54 other events, 67.6 us)
Sparse Core Ops, SparseCore 0:
  10.9 44.2 all-gather.16
  58.0 41.0 all-gather.18
  103.1 26.9 reduce-scatter.16
  132.2 138.7 all-gather.20
  273.4 106.1 all-gather.22
  390.4 27.1 reduce-scatter.18
  420.5 43.2 all-gather.24
  466.1 41.0 all-gather.26
  511.2 32.9 reduce-scatter.20
  546.2 138.7 all-gather.28
  687.6 106.1 all-gather.30
  821.2 27.1 reduce-scatter.24
  850.7 26.0 reduce-scatter.22
  908.4 26.0 reduce-scatter.26
  979.2 26.0 reduce-scatter.28
  1036.7 26.0 reduce-scatter.30
  1066.5 73.3 reduce-scatter.38
  1144.1 74.7 reduce-scatter.36
  1223.4 84.7 reduce-scatter.34
  1312.5 84.4 reduce-scatter.32
  1401.1 261.8 reduce-scatter.46
  1667.7 261.9 reduce-scatter.44
  1934.0 506.2 reduce-scatter.42
  2445.0 505.5 reduce-scatter.40
where the time goes:
time: 2970 us; the launch traced here: 2960 us
  waiting for transfers between devices  2450 us (82%)
  matrix products  224 us (8%)
  blocking collectives  165 us (6%)
  other arithmetic  61.1 us (2%)
  local copies, waits for them, and re-layouts  51 us (2%)
    reduce_scatter x2, waiting for transfers between devices, local(): lax.psum_scatter(d_gateup, 'dp', scatter_dimension=0, tiled=True)  1020 us
    reduce_scatter x2, waiting for transfers between devices, local(): lax.psum_scatter(d_down, 'dp', scatter_dimension=0, tiled=True)  531 us
    all_gather x2, waiting for transfers between devices, local(): lax.all_gather(w_gateup[layer], 'dp', axis=0, tiled=True)  253 us
    all_gather x2, waiting for transfers between devices, local(): lax.all_gather(w_down[layer], 'dp', axis=0, tiled=True)  183 us
    reduce_scatter x2, waiting for transfers between devices, local(): lax.psum_scatter(d_wqkv, 'dp', scatter_dimension=0, tiled=True)  176 us
    dot_general x8, matrix products, contract_first(): lax.dot_general(left, right, (((0,), (0,)), ((), ())), preferred_element_...  86.7 us
    reduce_scatter x4, waiting for transfers between devices, branch_sum(): lax.psum_scatter(term(jnp.int32(0), count * lax.axis_size('tensor')), 'te...  82.9 us
    reduce_scatter x4, waiting for transfers between devices, branch_back(): lax.psum_scatter(term(jnp.int32(0), count * lax.axis_size('tensor')), 'te...  66.9 us
  transfers between devices with their start and end apart: 24, of which 22 were waited for; matrix products, arithmetic and copies ran while one was open for 7% of the time, Pallas kernels for 0%

commit v1 on v0

v1 whole, which is shorter than its diff:
```python
import math

import jax
import jax.numpy as jnp
from jax import lax
from jax.sharding import Mesh
from jax.sharding import PartitionSpec as P

H = 12
KV = 2
HD = 128
LINE = 4
LANES = 128
LOW = jnp.bfloat16
F32 = jnp.float32


def rms_factor(rows):
    return lax.rsqrt(jnp.mean(rows * rows, axis=-1, keepdims=True) + 1e-06)


def rotate(values):
    half = values.shape[-1] // 2
    return jnp.concatenate([-values[..., half:], values[..., :half]], axis=-1)


def rotate_back(values):
    half = values.shape[-1] // 2
    return jnp.concatenate([values[..., half:], -values[..., :half]], axis=-1)


def doc_layout(lens, count):
    rows = jnp.arange(count, dtype=jnp.int32)
    doc = jnp.zeros((count,), jnp.int32)
    start = jnp.zeros((count,), jnp.int32)
    bound = jnp.int32(0)
    for number in range(lens.shape[0]):
        bound = bound + lens[number]
        after = (rows >= bound).astype(jnp.int32)
        doc = doc + after
        start = start + after * lens[number]
    positions = rows - start
    allowed = (doc[:, None] == doc[None, :]) & (rows[:, None] >= rows[None, :])
    return (positions, allowed)


def rope_tables(positions, width):
    index = jnp.arange(width // 2, dtype=F32)
    freq = jnp.exp(-(2.0 * index / width) * math.log(1000000.0))
    angle = positions.astype(F32)[:, None] * freq[None, :]
    return (
        jnp.concatenate([jnp.cos(angle)] * 2, axis=1),
        jnp.concatenate([jnp.sin(angle)] * 2, axis=1),
    )


def contract_last(left, right, out=F32):
    return lax.dot_general(left, right, (((1,), (1,)), ((), ())), preferred_element_type=out)


def contract_first(left, right, out=F32):
    return lax.dot_general(left, right, (((0,), (0,)), ((), ())), preferred_element_type=out)


def norm_back(upstream, rows, factor, gain):
    scaled = upstream * gain
    gain_part = jnp.sum(upstream * rows * factor, axis=0)
    result = factor * scaled - rows * factor**3 * jnp.mean(scaled * rows, axis=-1, keepdims=True)
    return (result, gain_part)


SWAP = [(0, 1), (1, 0)]


def take(array, index, axis):
    return lax.dynamic_index_in_dim(array, index, axis, keepdims=False)


def join_pair(own, other, axis_name, axis):
    index = lax.axis_index(axis_name)
    return jnp.where(
        index == 0, jnp.stack([own, other], axis=axis), jnp.stack([other, own], axis=axis)
    )


def spread_pair(rows):
    other = lax.ppermute(rows, "t", SWAP)
    return join_pair(rows, other, "t", 0).reshape(2 * rows.shape[0], rows.shape[1])


def sum_pair(partial):
    index = lax.axis_index("t")
    halves = partial.reshape(2, partial.shape[0] // 2, partial.shape[1])
    other = lax.ppermute(take(halves, 1 - index, 0).astype(LOW), "t", SWAP)
    return take(halves, index, 0) + other.astype(F32)


def spread_group(rows):
    return lax.all_gather(rows, ("z", "t"), axis=0, tiled=True)


def sum_group(partial):
    return lax.psum_scatter(partial, ("z", "t"), scatter_dimension=0, tiled=True).astype(F32)


def block_width(half):
    return -(-half // (LINE * LANES)) * LANES


def to_blocks(weight, parts):
    rows = weight.shape[0]
    half = weight.shape[1] // parts
    block = block_width(half)
    padded = jnp.pad(weight.reshape(rows, parts, half), ((0, 0), (0, 0), (0, LINE * block - half)))
    return padded.reshape(rows, parts, LINE, block).transpose(2, 0, 1, 3).reshape(LINE, rows, parts * block)


def from_blocks(blocks, parts, half):
    rows = blocks.shape[1]
    block = blocks.shape[2] // parts
    joined = blocks.reshape(LINE, rows, parts, block).transpose(1, 2, 0, 3)
    return joined.reshape(rows, parts, LINE * block)[:, :, :half].reshape(rows, parts * half)


def gather_blocks(weight, parts, bits):
    blocks = lax.all_to_all(to_blocks(weight, parts), "z", 0, 0, tiled=True)
    rows, width = blocks.shape[1:]
    lead = [LINE]
    current = blocks
    for bit in bits:
        other = lax.ppermute(current, bit, SWAP)
        current = join_pair(current, other, bit, len(lead))
        lead.append(2)
    return current.reshape(-1, width)


def reduce_blocks(grad, parts, half, bits, rows):
    width = grad.shape[1]
    current = grad.reshape(*([LINE] + [2] * len(bits)), rows, width)
    for number in reversed(range(len(bits))):
        index = lax.axis_index(bits[number])
        own = take(current, index, 1 + number)
        other = lax.ppermute(take(current, 1 - index, 1 + number), bits[number], SWAP)
        current = (own.astype(F32) + other.astype(F32)).astype(LOW)
    blocks = lax.all_to_all(current, "z", 0, 0, tiled=True)
    return from_blocks(blocks, parts, half).astype(F32)


def local(
    bits, tokens, cotangent, doc_lengths, norm_attn, norm_ffn, w_qkv, b_qkv, w_out, w_gateup, w_down
):
    dp = ("z", *bits)
    tensor_size = lax.axis_size("t")
    count = tokens.shape[0]
    length = count * tensor_size
    layers = w_qkv.shape[0]
    kv_local = KV // tensor_size
    groups = H // KV
    q_width = kv_local * groups * HD
    kv_width = kv_local * HD
    qkv_width = w_qkv.shape[2]
    rows = w_qkv.shape[1]
    half = w_down.shape[2]
    block = block_width(half)
    scale = 1.0 / math.sqrt(HD)
    positions, allowed = doc_layout(doc_lengths[0], length)
    cosine, sine = rope_tables(positions, HD)
    cos_q = cosine[:, None, None, :]
    sin_q = sine[:, None, None, :]
    cos_k = cosine[:, None, :]
    sin_k = sine[:, None, :]
    gain_attn = norm_attn.astype(F32)
    gain_ffn = norm_ffn.astype(F32)
    attn_weights, ffn_weights = [], []
    for layer in range(layers):
        both = lax.all_gather(
            jnp.concatenate([w_qkv[layer], w_out[layer]], axis=1), dp, axis=0, tiled=True
        )
        attn_weights.append((both[:, :qkv_width], both[:, qkv_width:]))
        ffn_weights.append(
            (gather_blocks(w_gateup[layer], 2, bits), gather_blocks(w_down[layer], 1, bits))
        )
    saved = []
    state = tokens.astype(F32)
    for layer in range(layers):
        qkv_w, out_w = attn_weights[layer]
        factor_a = rms_factor(state)
        xa_all = spread_pair((state * factor_a * gain_attn[layer]).astype(LOW))
        lin = jnp.dot(xa_all, qkv_w, preferred_element_type=F32) + b_qkv[layer].astype(F32)
        query = lin[:, :q_width].reshape(length, kv_local, groups, HD)
        key = lin[:, q_width : q_width + kv_width].reshape(length, kv_local, HD)
        value = lin[:, q_width + kv_width :].reshape(length, kv_local, HD).astype(LOW)
        query = (query * cos_q + rotate(query) * sin_q).astype(LOW)
        key = (key * cos_k + rotate(key) * sin_k).astype(LOW)
        raw = jnp.einsum("qkgd,pkd->kgqp", query, key, preferred_element_type=F32)
        scores = jnp.where(allowed, raw * scale, -1e30)
        top = jnp.max(scores, axis=-1, keepdims=True)
        expo = jnp.exp(scores - top)
        total = jnp.sum(expo, axis=-1, keepdims=True)
        probs = expo / total
        log_total = top + jnp.log(total)
        attended = (
            jnp.einsum("kgqp,pkd->qkgd", probs.astype(LOW), value, preferred_element_type=F32)
            .reshape(length, q_width)
            .astype(LOW)
        )
        middle = state + sum_pair(contract_last(attended, out_w))
        gu_w, down_w = ffn_weights[layer]
        factor_f = rms_factor(middle)
        xf_all = spread_group((middle * factor_f * gain_ffn[layer]).astype(LOW))
        gate_up = jnp.dot(xf_all, gu_w, preferred_element_type=F32)
        gate = gate_up[:, :block]
        up = gate_up[:, block:]
        act = (jax.nn.silu(gate) * up).astype(LOW)
        after = middle + sum_group(contract_last(act, down_w, LOW))
        saved.append(
            (state, factor_a, xa_all, query, key, value, log_total, attended)
            + (middle, factor_f, xf_all, gate, up, act)
        )
        state = after
    output = state.astype(LOW)
    grad = cotangent.astype(F32)
    grads_attn, grads_gu, grads_down, grads_bias, grads_ga, grads_gf = ([] for _ in range(6))
    for layer in reversed(range(layers)):
        (state_in, factor_a, xa_all, query, key, value, log_total, attended) = saved[layer][:8]
        (middle, factor_f, xf_all, gate, up, act) = saved[layer][8:]
        gu_w, down_w = ffn_weights[layer]
        qkv_w, out_w = attn_weights[layer]
        gm_all = spread_group(grad.astype(LOW))
        d_down = contract_first(gm_all, act, LOW)
        d_act = jnp.dot(gm_all, down_w, preferred_element_type=F32)
        sig = jax.nn.sigmoid(gate)
        d_gate = d_act * up * sig * (1.0 + gate * (1.0 - sig))
        d_up = d_act * gate * sig
        d_gu = jnp.concatenate([d_gate, d_up], axis=1).astype(LOW)
        d_xf = sum_group(contract_last(d_gu, gu_w, LOW))
        d_mid, part_f = norm_back(d_xf, middle, factor_f, gain_ffn[layer])
        grad = grad + d_mid
        d_gateup = contract_first(xf_all, d_gu, LOW)
        grads_gu.append(reduce_blocks(d_gateup, 2, half, bits, rows))
        grads_down.append(reduce_blocks(d_down, 1, half, bits, rows))
        ga_all = spread_pair(grad.astype(LOW))
        d_att = jnp.dot(ga_all, out_w, preferred_element_type=F32).astype(LOW)
        raw = jnp.einsum("qkgd,pkd->kgqp", query, key, preferred_element_type=F32)
        scores = jnp.where(allowed, raw * scale, -1e30)
        probs = jnp.exp(scores - log_total)
        d_att4 = d_att.reshape(length, kv_local, groups, HD)
        d_probs = jnp.einsum("qkgd,pkd->kgqp", d_att4, value, preferred_element_type=F32)
        centre = jnp.sum(probs * d_probs, axis=-1, keepdims=True)
        d_raw = (probs * (d_probs - centre) * scale).astype(LOW)
        d_query = jnp.einsum("kgqp,pkd->qkgd", d_raw, key, preferred_element_type=F32)
        d_key = jnp.einsum("kgqp,qkgd->pkd", d_raw, query, preferred_element_type=F32)
        d_value = jnp.einsum(
            "kgqp,qkgd->pkd", probs.astype(LOW), d_att4, preferred_element_type=F32
        )
        d_query = d_query * cos_q + rotate_back(d_query * sin_q)
        d_key = d_key * cos_k + rotate_back(d_key * sin_k)
        d_lin = jnp.concatenate(
            [
                d_query.reshape(length, q_width),
                d_key.reshape(length, kv_width),
                d_value.reshape(length, kv_width),
            ],
            axis=1,
        )
        grads_bias.append(jnp.sum(d_lin, axis=0))
        d_lin_low = d_lin.astype(LOW)
        d_xa = sum_pair(contract_last(d_lin_low, qkv_w))
        d_in, part_a = norm_back(d_xa, state_in, factor_a, gain_attn[layer])
        grad = grad + d_in
        d_both = jnp.concatenate(
            [contract_first(xa_all, d_lin_low, LOW), contract_first(ga_all, attended, LOW)], axis=1
        )
        grads_attn.append(
            lax.psum_scatter(d_both, dp, scatter_dimension=0, tiled=True).astype(F32)
        )
        grads_ga.append(part_a)
        grads_gf.append(part_f)

    def ordered(items):
        return jnp.stack(items[::-1], axis=0)

    side = lax.axis_index("t")
    bias = ordered(grads_bias)
    spread = jnp.where(
        (jnp.arange(tensor_size) == side)[:, None, None], bias[None], jnp.zeros_like(bias)[None]
    )
    full_ga, full_gf, full_bias = lax.psum(
        (ordered(grads_ga), ordered(grads_gf), spread), (*dp, "t")
    )
    both = ordered(grads_attn)
    return (
        output,
        grad,
        full_ga,
        full_gf,
        both[:, :, :qkv_width],
        take(full_bias, side, 0),
        both[:, :, qkv_width:],
        ordered(grads_gu),
        ordered(grads_down),
    )


def solution(mesh):
    dp_size, tensor_size = mesh.devices.shape
    rest = dp_size // LINE
    bits = tuple(f"r{number}" for number in range(rest.bit_length() - 1))
    shape = (LINE, *([2] * len(bits)), tensor_size)
    fine = Mesh(mesh.devices.reshape(shape), ("z", *bits, "t"))
    dp = ("z", *bits)
    rows = P((*dp, "t"), None)
    weight = P(None, dp, "t")

    def step(*args):
        return local(bits, *args)

    return jax.shard_map(
        step,
        mesh=fine,
        in_specs=(rows, rows, P(dp, None), P(), P(), weight, P(None, "t"), weight, weight, weight),
        out_specs=(rows, rows, P(), P(), weight, P(None, "t"), weight, weight, weight),
        check_vma=False,
    )
```

time: 2970 us -> 1200 us (0.40)
  waiting for transfers between devices: 2450 us -> 584 us
  local copies, waits for them, and re-layouts: 51 us -> 166 us
  blocking collectives: 165 us -> 69.6 us
  matrix products: 224 us -> 156 us
  starting transfers between devices: 1.2 us -> 66.5 us
  other arithmetic: 61.1 us -> 123 us
    reduce_scatter x16 -> x4, waiting for transfers between devices: 1890 us -> 168 us  [sum_group(): lax.psum_scatter(partial, ('z', 't'), scatter_dimension=0, tiled=True)]
    all_gather x8 -> x6, waiting for transfers between devices: 550 us -> 102 us  [the longest x4 52.7 us: spread_group(): return lax.all_gather(rows, ('z', 't'), axis=0, tiled=True)]
    all_to_all x0 -> x8, waiting for transfers between devices: none -> 179 us  [the longest x4 158 us: gather_blocks(): blocks = lax.all_to_all(to_blocks(weight, parts), 'z', 0, 0, tiled=True)]
    ppermute x0 -> x24, waiting for transfers between devices: none -> 125 us  [the longest x8 51.2 us: reduce_blocks(): lax.ppermute(take(current, 1 - index, 1 + number), bits[number], SWAP)]
    all_gather x8 -> x0, blocking collectives: 102 us -> none  [the longest x4 54.9 us: spread_grads(): return lax.all_gather(rows, 'tensor', axis=0, tiled=True)]
    dot_general x8, matrix products: 86.7 us -> 38.2 us  [contract_first(): lax.dot_general(left, right, (((0,), (0,)), ((), ())), preferred_element_...]
    all_to_all x0 -> x8, starting transfers between devices: none -> 47.3 us  [the longest x4 24.9 us: gather_blocks(): blocks = lax.all_to_all(to_blocks(weight, parts), 'z', 0, 0, tiled=True)]
    select_n x0 -> x17, other arithmetic: none -> 41 us  [the longest x16 40.9 us: join_pair(): jnp.where(index == 0, jnp.stack([own, other], axis=axis), jnp.stack([othe...]
  transfers between devices with their start and end apart: 24 -> 44, of which waited for: 22 -> 27; matrix products, arithmetic and copies ran while one was open for 7% -> 30% of each run, Pallas kernels for 0% -> 0%
where the time goes in v1:
time: 1200 us; the launch traced here: 1180 us
  waiting for transfers between devices  584 us (49%)
  local copies, waits for them, and re-layouts  166 us (14%)
  matrix products  156 us (13%)
  other arithmetic  123 us (10%)
  blocking collectives  69.6 us (6%)
  starting transfers between devices  66.5 us (6%)
  between operations  19.3 us (2%)
    reduce_scatter x4, waiting for transfers between devices, sum_group(): lax.psum_scatter(partial, ('z', 't'), scatter_dimension=0, tiled=True)  168 us
    all_to_all x4, waiting for transfers between devices, gather_blocks(): blocks = lax.all_to_all(to_blocks(weight, parts), 'z', 0, 0, tiled=True)  158 us
    psum x1, blocking collectives, local(): lax.psum((ordered(grads_ga), ordered(grads_gf), spread), (*dp, 't'))  69.6 us
    all_gather x4, waiting for transfers between devices, spread_group(): return lax.all_gather(rows, ('z', 't'), axis=0, tiled=True)  52.7 us
    ppermute x8, waiting for transfers between devices, reduce_blocks(): lax.ppermute(take(current, 1 - index, 1 + number), bits[number], SWAP)  51.2 us
    all_gather x2, waiting for transfers between devices, local(): lax.all_gather(jnp.concatenate([w_qkv[layer], w_out[layer]], axis=1), dp,...  49.1 us
    unnamed x252, local copies, waits for them, and re-layouts  46.1 us
    dot_general x8, matrix products, contract_last(): lax.dot_general(left, right, (((1,), (1,)), ((), ())), preferred_element_...  46.1 us
  transfers between devices with their start and end apart: 44, of which 27 were waited for; matrix products, arithmetic and copies ran while one was open for 30% of the time, Pallas kernels for 0%

profile of v1, /device:TPU:26, one launch (start us, length us, event | category | flops | bytes accessed | tf_op | source)
XLA Modules:
  0.0 1183.5 jit_solution(7630998283817550752)
XLA Ops:
  19.1 5.2 reshape.845
  24.2 5.2 all-to-all-start
  42.8 49.7 %all-to-all-done = bf16[4,96,2304]{2,1,0:T(8,128)(2,1)S(1)} async-done(((bf16[4,96,2304]{2,1,0:T(8,128)(2,1)}), bf16[4,96,2304]{2,1,0:T(8,128)(2,1)S(1)}, u32[]{:S(2)}, u32[]{:S(2)}) %all-to-all-start) | async-done | bytes 1769504 | tf_op jit(solution)/shard_map/all_to_all | solution.py:126
  124.0 6.8 all-to-all-start.1
  134.1 27.8 %all-to-all-done.1 = bf16[4,96,1152]{2,1,0:T(8,128)(2,1)} async-done(((bf16[4,96,1152]{2,1,0:T(8,128)(2,1)}), bf16[4,96,1152]{2,1,0:T(8,128)(2,1)}, u32[]{:S(2)}, u32[]{:S(2)}) %all-to-all-start.1) | async-done | bytes 884768 | tf_op jit(solution)/shard_map/all_to_all | solution.py:126
  166.7 13.0 %collective-permute-done.4 = bf16[4,96,1152]{2,1,0:T(8,128)(2,1)} collective-permute-done((bf16[4,96,1152]{2,1,0:T(8,128)(2,1)}, bf16[4,96,1152]{2,1,0:T(8,128)(2,1)}, u32[]{:S(2)}, u32[]{:S(2)}) %collective-permute-start.4) | collective-permute-done | bytes 884768 | tf_op jit(solution)/shard_map/ppermute | solution.py:131
  202.0 10.5 fusion.150
  218.3 5.6 fusion.151
  225.7 71.1 %reduce-scatter.11.cloned.1.call-done = bf16[128,1536]{1,0:T(8,128)(2,1)} async-done(((bf16[1024,1536]{1,0:T(8,128)(2,1)}), bf16[128,1536]{1,0:T(8,128)(2,1)}) %reduce-scatter.11.cloned.1.call-update) | async-done | bytes 393232 | tf_op jit(solution)/shard_map/reduce_scatter | solution.py:103
  300.3 8.8 collective-permute-done.6
  309.2 46.3 %all-gather.11.cloned.1.call-done = bf16[1536,1792]{1,0:T(8,128)(2,1)} async-done(((bf16[96,1792]{1,0:T(8,128)(2,1)}), bf16[1536,1792]{1,0:T(8,128)(2,1)}) %all-gather.11.cloned.1.call-update) | async-done | bytes 5505040 | tf_op jit(solution)/shard_map/all_gather | solution.py:176
  391.9 5.1 reshape.852
  397.0 6.3 all-to-all-start.2
  413.6 41.6 %all-to-all-done.2 = bf16[4,96,2304]{2,1,0:T(8,128)(2,1)} async-done(((bf16[4,96,2304]{2,1,0:T(8,128)(2,1)}), bf16[4,96,2304]{2,1,0:T(8,128)(2,1)}, u32[]{:S(2)}, u32[]{:S(2)}) %all-to-all-start.2) | async-done | bytes 1769504 | tf_op jit(solution)/shard_map/all_to_all | solution.py:126
  455.3 6.5 all-to-all-start.3
  463.3 39.1 %all-to-all-done.3 = bf16[4,96,1152]{2,1,0:T(8,128)(2,1)} async-done(((bf16[4,96,1152]{2,1,0:T(8,128)(2,1)}), bf16[4,96,1152]{2,1,0:T(8,128)(2,1)}, u32[]{:S(2)}, u32[]{:S(2)}) %all-to-all-start.3) | async-done | bytes 884768 | tf_op jit(solution)/shard_map/all_to_all | solution.py:126
  503.2 19.6 %collective-permute-done.10 = bf16[4,96,1152]{2,1,0:T(8,128)(2,1)S(1)} collective-permute-done((bf16[4,96,1152]{2,1,0:T(8,128)(2,1)}, bf16[4,96,1152]{2,1,0:T(8,128)(2,1)S(1)}, u32[]{:S(2)}, u32[]{:S(2)}) %collective-permute-start.10) | collective-permute-done | bytes 884768 | tf_op jit(solution)/shard_map/ppermute | solution.py:131
  524.9 5.2 maximum_select_fusion.5
  555.9 13.2 %fusion.152 = f32[1024,2304]{1,0:T(8,128)} fusion(bf16[1024,1536]{1,0:T(8,128)(2,1)} %all-gather.13.cloned.1.call-done, bf16[1536,2304]{1,0:T(8,128)(2,1)} %bitcast.433), kind=kOutput, calls=%fused_computation.319 | convolution fusion | flops 7247757312 | bytes 19660800 | tf_op jit(solution)/shard_map/dot_general | solution.py:211
  569.1 22.8 %all-gather.15.cloned.1.call-done = bf16[1024,1536]{1,0:T(8,128)(2,1)} async-done(((bf16[128,1536]{1,0:T(8,128)(2,1)}), bf16[1024,1536]{1,0:T(8,128)(2,1)}) %all-gather.15.cloned.1.call-update) | async-done | bytes 3145744 | tf_op jit(solution)/shard_map/all_gather | solution.py:99
  592.0 12.7 %fusion.4 = (bf16[1024,1152]{1,0:T(8,128)(2,1)S(1)}, bf16[1024,1152]{1,0:T(8,128)(2,1)S(1)}, bf16[1024,1152]{1,0:T(8,128)(2,1)}) fusion(f32[1024,2304]{1,0:T(8,128)} %fusion.152, bf16[1024,1536]{1,0:T(8,128)(2,1)} %all-gather.15.cloned.1.call-done, bf16[1536,1152]{1,0:T(8,128)(2,1)} %bitcast.467), kind=kOutput, calls=%fused_computation.15 | convolution fusion | flops 3642753024 | bytes 23199744 | tf_op jit(solution)/shard_map/dot_general | solution.py:231
  606.9 8.9 fusion.15
  616.0 8.6 fusion.153
  624.7 63.8 %reduce-scatter.15.cloned.1.call-done = bf16[128,1536]{1,0:T(8,128)(2,1)} async-done(((bf16[1024,1536]{1,0:T(8,128)(2,1)}), bf16[128,1536]{1,0:T(8,128)(2,1)}) %reduce-scatter.15.cloned.1.call-update) | async-done | bytes 393232 | tf_op jit(solution)/shard_map/reduce_scatter | solution.py:103
  694.4 9.7 collective-permute-done.12
  724.9 10.0 collective-permute-done.13
  735.8 33.4 %reduce-scatter.13.cloned.1.call-done = bf16[128,1536]{1,0:T(8,128)(2,1)} async-done(((bf16[1024,1536]{1,0:T(8,128)(2,1)}), bf16[128,1536]{1,0:T(8,128)(2,1)}) %reduce-scatter.13.cloned.1.call-update) | async-done | bytes 393232 | tf_op jit(solution)/shard_map/reduce_scatter | solution.py:103
  772.2 8.3 convolution_bitcast_fusion
  787.8 10.4 fusion.14
  802.3 29.9 %all-gather.17.cloned.1.call-done = bf16[1024,1536]{1,0:T(8,128)(2,1)} async-done(((bf16[128,1536]{1,0:T(8,128)(2,1)}), bf16[1024,1536]{1,0:T(8,128)(2,1)}) %all-gather.17.cloned.1.call-update) | async-done | bytes 3145744 | tf_op jit(solution)/shard_map/all_gather | solution.py:99
  832.2 10.7 multiply_convert_fusion.1
  845.1 10.9 fusion.13
  864.5 16.2 %collective-permute-done.23 = bf16[4,96,1152]{2,1,0:T(8,128)(2,1)S(1)} collective-permute-done((bf16[4,96,1152]{2,1,0:T(8,128)(2,1)S(1)}, bf16[4,96,1152]{2,1,0:T(8,128)(2,1)S(1)}, u32[]{:S(2)}, u32[]{:S(2)}) %collective-permute-start.23) | collective-permute-done | bytes 884768 | tf_op jit(solution)/shard_map/ppermute | solution.py:143
  881.9 6.3 all-to-all-start.7
  889.5 20.0 %all-to-all-done.7 = bf16[4,96,1152]{2,1,0:T(8,128)(2,1)} async-done(((bf16[4,96,1152]{2,1,0:T(8,128)(2,1)}), bf16[4,96,1152]{2,1,0:T(8,128)(2,1)}, u32[]{:S(2)}, u32[]{:S(2)}) %all-to-all-start.7) | async-done | bytes 884768 | tf_op jit(solution)/shard_map/all_to_all | solution.py:145
  911.6 6.1 collective-permute-done.19
  920.9 5.7 all-to-all-start.5
  932.5 7.9 copy.274
  942.0 6.3 fusion.154
  950.3 8.5 fusion.12
  968.8 19.4 %collective-permute-done.21 = bf16[4,96,1152]{2,1,0:T(8,128)(2,1)} collective-permute-done((bf16[4,96,1152]{2,1,0:T(8,128)(2,1)}, bf16[4,96,1152]{2,1,0:T(8,128)(2,1)}, u32[]{:S(2)}, u32[]{:S(2)}) %collective-permute-start.21) | collective-permute-done | bytes 884768 | tf_op jit(solution)/shard_map/ppermute | solution.py:143
  1003.2 8.4 copy.272
  1015.6 5.4 all-to-all-start.6
  1038.2 9.7 reduce-scatter.21.cloned.1.call-done
  1052.7 9.5 collective-permute-done.17
  1065.4 5.1 all-to-all-start.4
  1078.3 5.8 collective-permute-done.15
  1084.5 69.6 %all-reduce.4 = (f32[2,1536]{1,0:T(2,128)}, f32[2,1536]{1,0:T(2,128)}, f32[2,2,1024]{2,1,0:T(2,128)S(1)}) all-reduce(f32[2,1536]{1,0:T(2,128)S(1)} %get-tuple-element.139, f32[2,1536]{1,0:T(2,128)S(1)} %get-tuple-element.140, f32[2,2,1024]{2,1,0:T(2,128)S(1)} %broadcast_select_fusion), channel_id=1, replica_groups=mesh['z'=4,'r0'=2,'r1'=2,'t'=2] {'z','r0','r1','t'}, use_global_device_ids=true, to_apply=%region_20.21 | all-reduce | flops 10240 | bytes 81920 | tf_op jit(solution)/shard_map/psum | solution.py:288
  (519 shorter events, 327.8 us)
Async XLA Ops:
  7.2 88.5 %all-gather.7.cloned.1.call-start = ((), (), s32[]{:S(2)}) async-start(), calls=%async_computation.14 | async-start | bytes 5849088 | tf_op jit(solution)/shard_map/all_gather | solution.py:176
  24.2 68.3 %all-to-all-start = ((bf16[4,96,2304]{2,1,0:T(8,128)(2,1)}), bf16[4,96,2304]{2,1,0:T(8,128)(2,1)S(1)}, u32[]{:S(2)}, u32[]{:S(2)}) async-start(bf16[4,96,2304]{2,1,0:T(8,128)(2,1)} %reshape.845), calls=%async_computation | async-start | bytes 3538944 | tf_op jit(solution)/shard_map/all_to_all | solution.py:126
  30.4 10.4 collective-permute-start
  39.7 672.6 %copy-start.39 = (f32[256,64]{1,0:T(8,128)}, f32[256,64]{1,0:T(8,128)S(1)}, u32[]{:S(2)}) copy-start(f32[256,64]{1,0:T(8,128)S(1)} %get-tuple-element.110) | copy-start | bytes 196612
  39.7 673.6 %copy-start.37 = (f32[256,64]{1,0:T(8,128)}, f32[256,64]{1,0:T(8,128)S(1)}, u32[]{:S(2)}) copy-start(f32[256,64]{1,0:T(8,128)S(1)} %get-tuple-element.109) | copy-start | bytes 196612
  92.5 70.1 %collective-permute-start.2 = (bf16[4,96,2304]{2,1,0:T(8,128)(2,1)S(1)}, bf16[4,96,2304]{2,1,0:T(8,128)(2,1)}, u32[]{:S(2)}, u32[]{:S(2)}) collective-permute-start(bf16[4,96,2304]{2,1,0:T(8,128)(2,1)S(1)} %all-to-all-done), channel_id=1, source_target_pairs={{0,4},{4,0},{1,5},{5,1},{2,6},{6,2},{3,7},{7,3},{8,12},{12,8},{9,1... | collective-permute-start | bytes 5308424 | tf_op jit(solution)/shard_map/ppermute | solution.py:131
  100.7 618.1 %copy-start.26 = (f32[256,128]{0,1:T(8,128)}, f32[256,128]{0,1:T(8,128)S(1)}, u32[]{:S(2)}) copy-start(f32[256,128]{0,1:T(8,128)S(1)} %copy.184) | copy-start | bytes 393220
  118.1 12.7 %collective-permute-start.1 = (bf16[128,1536]{1,0:T(8,128)(2,1)}, bf16[128,1536]{1,0:T(8,128)(2,1)}, u32[]{:S(2)}, u32[]{:S(2)}) collective-permute-start(bf16[128,1536]{1,0:T(8,128)(2,1)} %fusion.98), channel_id=1, source_target_pairs={{0,1},{1,0},{2,3},{3,2},{4,5},{5,4},{6,7},{7,6},{8,9},{9,8},{10,11... | collective-permute-start | bytes 1179656 | tf_op jit(solution)/shard_map/ppermute | solution.py:94
  124.0 38.0 %all-to-all-start.1 = ((bf16[4,96,1152]{2,1,0:T(8,128)(2,1)}), bf16[4,96,1152]{2,1,0:T(8,128)(2,1)}, u32[]{:S(2)}, u32[]{:S(2)}) async-start(bf16[4,96,1152]{2,1,0:T(8,128)(2,1)} %copy.197), calls=%async_computation.1 | async-start | bytes 1769472 | tf_op jit(solution)/shard_map/all_to_all | solution.py:126
  130.8 71.2 %all-gather.9.cloned.1.call-start = ((), (), s32[]{:S(2)}) async-start(), calls=%async_computation.15 | async-start | bytes 3538944 | tf_op jit(solution)/shard_map/all_gather | solution.py:99
  132.4 164.4 %copy-start.2 = (f32[128,1536]{1,0:T(8,128)}, f32[128,1536]{1,0:T(8,128)S(1)}, u32[]{:S(2)}) copy-start(f32[128,1536]{1,0:T(8,128)S(1)} %get-tuple-element.69) | copy-start | bytes 2359300
  133.9 162.9 %reduce-scatter.11.cloned.1.call-start = ((), (), s32[]{:S(2)}) async-start(), calls=%async_computation.16 | async-start | bytes 3538944 | tf_op jit(solution)/shard_map/reduce_scatter | solution.py:103
  162.0 17.7 %collective-permute-start.4 = (bf16[4,96,1152]{2,1,0:T(8,128)(2,1)}, bf16[4,96,1152]{2,1,0:T(8,128)(2,1)}, u32[]{:S(2)}, u32[]{:S(2)}) collective-permute-start(bf16[4,96,1152]{2,1,0:T(8,128)(2,1)} %all-to-all-done.1), channel_id=1, source_target_pairs={{0,4},{4,0},{1,5},{5,1},{2,6},{6,2},{3,7},{7,3},{8,12},{12,8},{9,1... | collective-permute-start | bytes 2654216 | tf_op jit(solution)/shard_map/ppermute | solution.py:131
  166.6 27.2 %collective-permute-start.3 = (bf16[4,2,96,2304]{3,2,0,1:T(8,128)(2,1)}, bf16[4,2,96,2304]{3,2,0,1:T(8,128)(2,1)}, u32[]{:S(2)}, u32[]{:S(2)}) collective-permute-start(bf16[4,2,96,2304]{3,2,0,1:T(8,128)(2,1)} %maximum_select_fusion.3), channel_id=1, source_target_pairs={{0,2},{2,0},{1,3},{3,1},{4,6},{6,4},{5,7},{7,5},{8,10},{10,8},{9,1... | collective-permute-start | bytes 10616840 | tf_op jit(solution)/shard_map/ppermute | solution.py:131
  183.2 4.0 collective-permute-start.5
  224.0 131.5 %all-gather.11.cloned.1.call-start = ((), (), s32[]{:S(2)}) async-start(), calls=%async_computation.17 | async-start | bytes 5849088 | tf_op jit(solution)/shard_map/all_gather | solution.py:176
  298.7 10.4 collective-permute-start.6
  375.6 27.6 %collective-permute-start.7 = (bf16[128,1536]{1,0:T(8,128)(2,1)S(1)}, bf16[128,1536]{1,0:T(8,128)(2,1)}, u32[]{:S(2)}, u32[]{:S(2)}) collective-permute-start(bf16[128,1536]{1,0:T(8,128)(2,1)S(1)} %fusion.99), channel_id=1, source_target_pairs={{0,1},{1,0},{2,3},{3,2},{4,5},{5,4},{6,7},{7,6},{8,9},{9,8},{10,11... | collective-permute-start | bytes 1179656 | tf_op jit(solution)/shard_map/ppermute | solution.py:94
  397.0 58.3 %all-to-all-start.2 = ((bf16[4,96,2304]{2,1,0:T(8,128)(2,1)}), bf16[4,96,2304]{2,1,0:T(8,128)(2,1)}, u32[]{:S(2)}, u32[]{:S(2)}) async-start(bf16[4,96,2304]{2,1,0:T(8,128)(2,1)} %reshape.852), calls=%async_computation.3 | async-start | bytes 3538944 | tf_op jit(solution)/shard_map/all_to_all | solution.py:126
  403.3 152.6 %all-gather.13.cloned.1.call-start = ((), (), s32[]{:S(2)}) async-start(), calls=%async_computation.18 | async-start | bytes 3538944 | tf_op jit(solution)/shard_map/all_gather | solution.py:99
  455.3 47.1 %all-to-all-start.3 = ((bf16[4,96,1152]{2,1,0:T(8,128)(2,1)}), bf16[4,96,1152]{2,1,0:T(8,128)(2,1)}, u32[]{:S(2)}, u32[]{:S(2)}) async-start(bf16[4,96,1152]{2,1,0:T(8,128)(2,1)} %copy.215), calls=%async_computation.4 | async-start | bytes 1769472 | tf_op jit(solution)/shard_map/all_to_all | solution.py:126
  461.8 130.2 %all-gather.15.cloned.1.call-start = ((), (), s32[]{:S(2)}) async-start(), calls=%async_computation.20 | async-start | bytes 3538944 | tf_op jit(solution)/shard_map/all_gather | solution.py:99
  461.8 63.1 %collective-permute-start.8 = (bf16[4,96,2304]{2,1,0:T(8,128)(2,1)}, bf16[4,96,2304]{2,1,0:T(8,128)(2,1)}, u32[]{:S(2)}, u32[]{:S(2)}) collective-permute-start(bf16[4,96,2304]{2,1,0:T(8,128)(2,1)} %all-to-all-done.2), channel_id=1, source_target_pairs={{0,4},{4,0},{1,5},{5,1},{2,6},{6,2},{3,7},{7,3},{8,12},{12,8},{9,1... | collective-permute-start | bytes 5308424 | tf_op jit(solution)/shard_map/ppermute | solution.py:131
  502.3 20.4 %collective-permute-start.10 = (bf16[4,96,1152]{2,1,0:T(8,128)(2,1)}, bf16[4,96,1152]{2,1,0:T(8,128)(2,1)S(1)}, u32[]{:S(2)}, u32[]{:S(2)}) collective-permute-start(bf16[4,96,1152]{2,1,0:T(8,128)(2,1)} %all-to-all-done.3), channel_id=1, source_target_pairs={{0,4},{4,0},{1,5},{5,1},{2,6},{6,2},{3,7},{7,3},{8,12},{12,8},{9,1... | collective-permute-start | bytes 2654216 | tf_op jit(solution)/shard_map/ppermute | solution.py:131
  530.1 17.7 %collective-permute-start.9 = (bf16[4,2,96,2304]{3,2,0,1:T(8,128)(2,1)}, bf16[4,2,96,2304]{3,2,0,1:T(8,128)(2,1)}, u32[]{:S(2)}, u32[]{:S(2)}) collective-permute-start(bf16[4,2,96,2304]{3,2,0,1:T(8,128)(2,1)} %maximum_select_fusion.5), channel_id=1, source_target_pairs={{0,2},{2,0},{1,3},{3,1},{4,6},{6,4},{5,7},{7,5},{8,10},{10,8},{9,1... | collective-permute-start | bytes 10616840 | tf_op jit(solution)/shard_map/ppermute | solution.py:131
  531.5 7.7 collective-permute-start.11
  532.0 156.5 %reduce-scatter.15.cloned.1.call-start = ((), (), s32[]{:S(2)}) async-start(), calls=%async_computation.21 | async-start | bytes 3538944 | tf_op jit(solution)/shard_map/reduce_scatter | solution.py:103
  615.7 153.4 %reduce-scatter.13.cloned.1.call-start = ((), (), s32[]{:S(2)}) async-start(), calls=%async_computation.19 | async-start | bytes 3538944 | tf_op jit(solution)/shard_map/reduce_scatter | solution.py:103
  624.6 207.6 %all-gather.17.cloned.1.call-start = ((), (), s32[]{:S(2)}) async-start(), calls=%async_computation.22 | async-start | bytes 3538944 | tf_op jit(solution)/shard_map/all_gather | solution.py:99
  692.3 11.8 collective-permute-start.12
  722.4 12.5 %collective-permute-start.13 = (bf16[128,1536]{1,0:T(8,128)(2,1)S(1)}, bf16[128,1536]{1,0:T(8,128)(2,1)S(1)}, u32[]{:S(2)}, u32[]{:S(2)}) collective-permute-start(bf16[128,1536]{1,0:T(8,128)(2,1)S(1)} %fusion.100), channel_id=1, source_target_pairs={{0,1},{1,0},{2,3},{3,2},{4,5},{5,4},{6,7},{7,6},{8,9},{9,8},{10,11... | collective-permute-start | bytes 1179656 | tf_op jit(solution)/shard_map/ppermute | solution.py:94
  772.1 192.7 %reduce-scatter.17.cloned.1.call-start = ((), (), s32[]{:S(2)}) async-start(), calls=%async_computation.23 | async-start | bytes 3538944 | tf_op jit(solution)/shard_map/reduce_scatter | solution.py:103
  786.7 69.3 %collective-permute-start.22 = (bf16[4,2,96,1152]{3,2,1,0:T(8,128)(2,1)}, bf16[4,2,96,1152]{3,2,1,0:T(8,128)(2,1)}, u32[]{:S(2)}, u32[]{:S(2)}) collective-permute-start(bf16[4,2,96,1152]{3,2,1,0:T(8,128)(2,1)} %dynamic-slice_bitcast_fusion.2), channel_id=1, source_target_pairs={{0,2},{2,0},{1,3},{3,1},{4,6},{6,4},{5,7},{7,5},{8,10},{10,8},{9,1... | collective-permute-start | bytes 5308424 | tf_op jit(solution)/shard_map/ppermute | solution.py:143
  802.3 56.5 %collective-permute-start.18 = (bf16[4,2,96,2304]{3,2,1,0:T(8,128)(2,1)}, bf16[4,2,96,2304]{3,2,1,0:T(8,128)(2,1)}, u32[]{:S(2)}, u32[]{:S(2)}) collective-permute-start(bf16[4,2,96,2304]{3,2,1,0:T(8,128)(2,1)} %dynamic-slice_bitcast_fusion), channel_id=1, source_target_pairs={{0,2},{2,0},{1,3},{3,1},{4,6},{6,4},{5,7},{7,5},{8,10},{10,8},{9,1... | collective-permute-start | bytes 10616840 | tf_op jit(solution)/shard_map/ppermute | solution.py:143
  858.2 22.6 %collective-permute-start.23 = (bf16[4,96,1152]{2,1,0:T(8,128)(2,1)S(1)}, bf16[4,96,1152]{2,1,0:T(8,128)(2,1)S(1)}, u32[]{:S(2)}, u32[]{:S(2)}) collective-permute-start(bf16[4,96,1152]{2,1,0:T(8,128)(2,1)S(1)} %dynamic-slice_bitcast_fusion.6), channel_id=1, source_target_pairs={{0,4},{4,0},{1,5},{5,1},{2,6},{6,2},{3,7},{7,3},{8,12},{12,8},{9,1... | collective-permute-start | bytes 2654216 | tf_op jit(solution)/shard_map/ppermute | solution.py:143
  863.8 53.9 %collective-permute-start.19 = (bf16[4,96,2304]{2,1,0:T(8,128)(2,1)}, bf16[4,96,2304]{2,1,0:T(8,128)(2,1)}, u32[]{:S(2)}, u32[]{:S(2)}) collective-permute-start(bf16[4,96,2304]{2,1,0:T(8,128)(2,1)} %dynamic-slice_bitcast_fusion.4), channel_id=1, source_target_pairs={{0,4},{4,0},{1,5},{5,1},{2,6},{6,2},{3,7},{7,3},{8,12},{12,8},{9,1... | collective-permute-start | bytes 5308424 | tf_op jit(solution)/shard_map/ppermute | solution.py:143
  881.9 27.6 %all-to-all-start.7 = ((bf16[4,96,1152]{2,1,0:T(8,128)(2,1)}), bf16[4,96,1152]{2,1,0:T(8,128)(2,1)}, u32[]{:S(2)}, u32[]{:S(2)}) async-start(bf16[4,96,1152]{2,1,0:T(8,128)(2,1)} %fusion.34), calls=%async_computation.11 | async-start | bytes 1769472 | tf_op jit(solution)/shard_map/all_to_all | solution.py:145
  920.9 94.7 %all-to-all-start.5 = ((bf16[4,96,2304]{2,1,0:T(8,128)(2,1)}), bf16[4,96,2304]{2,1,0:T(8,128)(2,1)}, u32[]{:S(2)}, u32[]{:S(2)}) async-start(bf16[4,96,2304]{2,1,0:T(8,128)(2,1)} %fusion.10), calls=%async_computation.9 | async-start | bytes 3538944 | tf_op jit(solution)/shard_map/all_to_all | solution.py:145
  926.6 121.3 %reduce-scatter.21.cloned.1.call-start = ((), (), s32[]{:S(2)}) async-start(), calls=%async_computation.25 | async-start | bytes 5849088
  940.4 229.9 %reduce-scatter.19.cloned.1.call-start = ((), (), s32[]{:S(2)}) async-start(), calls=%async_computation.24 | async-start | bytes 5849088
  948.5 14.5 %collective-permute-start.20 = (bf16[4,2,96,1152]{3,2,1,0:T(8,128)(2,1)S(1)}, bf16[4,2,96,1152]{3,2,1,0:T(8,128)(2,1)S(1)}, u32[]{:S(2)}, u32[]{:S(2)}) collective-permute-start(bf16[4,2,96,1152]{3,2,1,0:T(8,128)(2,1)S(1)} %dynamic-slice_bitcast_fusion.3), channel_id=1, source_target_pairs={{0,2},{2,0},{1,3},{3,1},{4,6},{6,4},{5,7},{7,5},{8,10},{10,8},{9,1... | collective-permute-start | bytes 5308424 | tf_op jit(solution)/shard_map/ppermute | solution.py:143
  962.9 48.6 %collective-permute-start.16 = (bf16[4,2,96,2304]{3,2,1,0:T(8,128)(2,1)}, bf16[4,2,96,2304]{3,2,1,0:T(8,128)(2,1)}, u32[]{:S(2)}, u32[]{:S(2)}) collective-permute-start(bf16[4,2,96,2304]{3,2,1,0:T(8,128)(2,1)} %dynamic-slice_bitcast_fusion.1), channel_id=1, source_target_pairs={{0,2},{2,0},{1,3},{3,1},{4,6},{6,4},{5,7},{7,5},{8,10},{10,8},{9,1... | collective-permute-start | bytes 10616840 | tf_op jit(solution)/shard_map/ppermute | solution.py:143
  964.5 23.7 %collective-permute-start.21 = (bf16[4,96,1152]{2,1,0:T(8,128)(2,1)}, bf16[4,96,1152]{2,1,0:T(8,128)(2,1)}, u32[]{:S(2)}, u32[]{:S(2)}) collective-permute-start(bf16[4,96,1152]{2,1,0:T(8,128)(2,1)} %dynamic-slice_bitcast_fusion.7), channel_id=1, source_target_pairs={{0,4},{4,0},{1,5},{5,1},{2,6},{6,2},{3,7},{7,3},{8,12},{12,8},{9,1... | collective-permute-start | bytes 2654216 | tf_op jit(solution)/shard_map/ppermute | solution.py:143
  968.3 22.2 %collective-permute-start.14 = (bf16[128,1536]{1,0:T(8,128)(2,1)S(1)}, bf16[128,1536]{1,0:T(8,128)(2,1)S(1)}, u32[]{:S(2)}, u32[]{:S(2)}) collective-permute-start(bf16[128,1536]{1,0:T(8,128)(2,1)S(1)} %get-tuple-element.60), channel_id=1, source_target_pairs={{0,1},{1,0},{2,3},{3,2},{4,5},{5,4},{6,7},{7,6},{8,9},{9,8},{10,11... | collective-permute-start | bytes 1179656 | tf_op jit(solution)/shard_map/ppermute | solution.py:87
  1015.6 34.9 %all-to-all-start.6 = ((bf16[4,96,1152]{2,1,0:T(8,128)(2,1)}), bf16[4,96,1152]{2,1,0:T(8,128)(2,1)}, u32[]{:S(2)}, u32[]{:S(2)}) async-start(bf16[4,96,1152]{2,1,0:T(8,128)(2,1)} %fusion.35), calls=%async_computation.10 | async-start | bytes 1769472 | tf_op jit(solution)/shard_map/all_to_all | solution.py:145
  1022.4 39.8 %collective-permute-start.17 = (bf16[4,96,2304]{2,1,0:T(8,128)(2,1)}, bf16[4,96,2304]{2,1,0:T(8,128)(2,1)}, u32[]{:S(2)}, u32[]{:S(2)}) collective-permute-start(bf16[4,96,2304]{2,1,0:T(8,128)(2,1)} %dynamic-slice_bitcast_fusion.5), channel_id=1, source_target_pairs={{0,4},{4,0},{1,5},{5,1},{2,6},{6,2},{3,7},{7,3},{8,12},{12,8},{9,1... | collective-permute-start | bytes 5308424 | tf_op jit(solution)/shard_map/ppermute | solution.py:143
  1065.4 91.6 %all-to-all-start.4 = ((bf16[4,96,2304]{2,1,0:T(8,128)(2,1)}), bf16[4,96,2304]{2,1,0:T(8,128)(2,1)S(1)}, u32[]{:S(2)}, u32[]{:S(2)}) async-start(bf16[4,96,2304]{2,1,0:T(8,128)(2,1)} %fusion.11), calls=%async_computation.8 | async-start | bytes 3538944 | tf_op jit(solution)/shard_map/all_to_all | solution.py:145
  1074.4 9.7 collective-permute-start.15
  (119 other events, 1478.7 us)
Sparse Core Ops, SparseCore 0:
  11.5 84.1 all-gather.6
  134.4 64.9 all-gather.8
  224.1 72.6 reduce-scatter.10
  299.5 55.9 all-gather.10
  406.8 96.6 all-gather.12
  532.1 59.7 all-gather.14
  615.9 72.6 reduce-scatter.14
  692.7 76.4 reduce-scatter.12
  772.3 59.9 all-gather.16
  856.1 82.2 reduce-scatter.16
  942.3 105.5 reduce-scatter.20
  1052.2 101.2 reduce-scatter.18

commit v2 on v1

--- a/solution.py
+++ b/solution.py
@@ -1,8 +1,11 @@
+import functools
 import math
 
 import jax
 import jax.numpy as jnp
 from jax import lax
+from jax.experimental import pallas as pl
+from jax.experimental.pallas import tpu as pltpu
 from jax.sharding import Mesh
 from jax.sharding import PartitionSpec as P
 
@@ -13,6 +16,7 @@
 LANES = 128
 LOW = jnp.bfloat16
 F32 = jnp.float32
+MESH = pl.DeviceIdType.MESH
 
 
 def rms_factor(rows):
@@ -95,55 +99,773 @@
     return take(halves, index, 0) + other.astype(F32)
 
 
+def greet(axes_targets, conditions):
+    barrier = pltpu.get_barrier_semaphore()
+    for (axis, target), condition in zip(axes_targets, conditions):
+        def signal(axis=axis, target=target):
+            pl.semaphore_signal(barrier, inc=1, device_id={axis: target}, device_id_type=MESH)
+        if condition is None:
+            signal()
+        else:
+            pl.when(condition)(signal)
+    amount = sum(1 if c is None else c.astype(jnp.int32) for c in conditions)
+    pl.semaphore_wait(barrier, amount)
+
+
+def slot_of(line, values):
+    slot = line
+    for value in values:
+        slot = slot * 2 + value
+    return slot
+
+
+def both(*conditions):
+    given = [c for c in conditions if c is not None]
+    return functools.reduce(jnp.logical_and, given) if given else None
+
+
+def guarded(condition, action):
+    if condition is None:
+        action()
+    else:
+        pl.when(condition)(action)
+
+
+def bit_flips(variant, stage, count):
+    return [(variant >> b) & 1 for b in range(stage)] + [1] + [0] * (count - stage - 1)
+
+
+class Gather:
+    def __init__(self, size, bits, x_ref, out_ref, own_sem, line_sems, bit_sems, recv_sems):
+        self.size, self.bits, self.count = size, bits, len(bits)
+        self.x_ref, self.out_ref, self.own_sem = x_ref, out_ref, own_sem
+        self.line_sems, self.bit_sems, self.recv_sems = line_sems, bit_sems, recv_sems
+        self.z = lax.axis_index("z")
+        self.mine = [lax.axis_index(bit) for bit in bits]
+        self.own = slot_of(self.z, self.mine)
+        self.pending = []
+
+    def copy(self, slot, first, axis, target, send_sem):
+        return pltpu.make_async_remote_copy(
+            src_ref=self.x_ref if first else self.out_ref.at[slot],
+            dst_ref=self.out_ref.at[slot],
+            send_sem=send_sem,
+            recv_sem=self.recv_sems.at[slot],
+            device_id={axis: target},
+            device_id_type=MESH,
+        )
+
+    def start(self, condition, make):
+        self.pending.append((condition, make))
+        guarded(condition, lambda: make().start())
+
+    def arrived(self, condition, slot, axis, target):
+        guarded(
+            condition,
+            lambda: self.copy(slot, False, axis, target, self.line_sems.at[0, 0]).wait_recv(),
+        )
+
+    def spread(self, condition, slot, first, number, side, variant, after):
+        for stage in range(after, self.count):
+            self.start(
+                condition,
+                functools.partial(
+                    self.copy,
+                    slot,
+                    first,
+                    self.bits[stage],
+                    1 - self.mine[stage],
+                    self.bit_sems.at[number, side, variant, stage],
+                ),
+            )
+
+    def line_of(self, number, side):
+        line = self.z - number if side == 0 else self.z + number
+        if number == 0:
+            return line, None
+        return line, (line >= 0 if side == 0 else line < self.size)
+
+    def on_bits(self, number):
+        for side in range(1 if number == 0 else 2):
+            line, condition = self.line_of(number, side)
+            for stage in range(self.count):
+                for variant in range(2**stage):
+                    flips = bit_flips(variant, stage, self.count)
+                    slot = slot_of(line, [1 - m if f else m for m, f in zip(self.mine, flips)])
+                    self.arrived(condition, slot, self.bits[stage], 1 - self.mine[stage])
+                    code = sum(f << b for b, f in enumerate(flips))
+                    self.spread(condition, slot, False, number, side, code, stage + 1)
+
+    def begin(self):
+        pltpu.make_async_copy(self.x_ref, self.out_ref.at[self.own], self.own_sem).start()
+        z, size = self.z, self.size
+        first = functools.partial(self.copy, self.own, True, "z")
+        self.start(z < size - 1, functools.partial(first, z + 1, self.line_sems.at[0, 0]))
+        self.start(z > 0, functools.partial(first, z - 1, self.line_sems.at[0, 1]))
+        self.spread(None, self.own, True, 0, 0, 0, 0)
+
+    def step(self, number):
+        z, size = self.z, self.size
+        for side in range(2):
+            line, condition = self.line_of(number, side)
+            slot = slot_of(line, self.mine)
+            back = z - 1 if side == 0 else z + 1
+            onto = z + 1 if side == 0 else z - 1
+            self.arrived(condition, slot, "z", back)
+            self.start(
+                both(condition, onto < size if side == 0 else onto >= 0),
+                functools.partial(self.copy, slot, False, "z", onto, self.line_sems.at[number, side]),
+            )
+            self.spread(condition, slot, False, number, side, 0, 0)
+
+    def middle(self):
+        for number in range(1, self.size):
+            self.step(number)
+            self.on_bits(number - 1)
+        self.on_bits(self.size - 1)
+
+    def end(self):
+        pltpu.make_async_copy(self.x_ref, self.out_ref.at[self.own], self.own_sem).wait()
+        for condition, make in self.pending:
+            guarded(condition, lambda make=make: make().wait_send())
+
+
+def gather_kernel(size, bits, *refs):
+    z = lax.axis_index("z")
+    mine = [lax.axis_index(bit) for bit in bits]
+    greet(
+        [("z", z + 1), ("z", z - 1)] + [(bit, 1 - m) for bit, m in zip(bits, mine)],
+        [z < size - 1, z > 0] + [None] * len(bits),
+    )
+    steps = Gather(size, bits, *refs)
+    steps.begin()
+    steps.middle()
+    steps.end()
+
+
+def gather_semaphores(size, bits):
+    slots = size * 2 ** len(bits)
+    return [
+        pltpu.SemaphoreType.DMA,
+        pltpu.SemaphoreType.DMA((size, 2)),
+        pltpu.SemaphoreType.DMA((size, 2, 2 ** len(bits), len(bits))),
+        pltpu.SemaphoreType.DMA((slots,)),
+    ]
+
+
+def gather(x, size, bits, collective_id):
+    slots = size * 2 ** len(bits)
+    return pl.pallas_call(
+        functools.partial(gather_kernel, size, bits),
+        out_shape=jax.ShapeDtypeStruct((slots, *x.shape), x.dtype),
+        in_specs=[pl.BlockSpec(memory_space=pl.ANY)],
+        out_specs=pl.BlockSpec(memory_space=pl.ANY),
+        scratch_shapes=gather_semaphores(size, bits),
+        compiler_params=pltpu.CompilerParams(collective_id=collective_id, has_side_effects=True),
+        cost_estimate=pl.CostEstimate(
+            flops=0, transcendentals=0, bytes_accessed=slots * x.size * 100
+        ),
+    )(x)
+
+
+class Exchange:
+    def __init__(self, size, bits, block, half, gu_ref, dn_ref, gu_out, dn_out, sems):
+        self.size, self.bits, self.count = size, bits, len(bits)
+        self.block, self.half = block, half
+        self.gu_ref, self.dn_ref, self.gu_out, self.dn_out = gu_ref, dn_ref, gu_out, dn_out
+        self.own_sems, self.line_sems, self.bit_sems, self.recv_sems = sems
+        self.z = lax.axis_index("z")
+        self.mine = [lax.axis_index(bit) for bit in bits]
+        self.own = slot_of(self.z, self.mine)
+        self.others = [lax.rem(self.z + o, size) for o in range(1, size)]
+        self.pending = []
+
+    def pieces(self, target, slot):
+        low = pl.multiple_of(jnp.minimum(target * self.block, self.half - self.block), LANES)
+        high = pl.multiple_of(low + self.half, LANES)
+        width = self.block
+        return [
+            (self.gu_ref.at[:, pl.ds(low, width)], self.gu_out.at[slot, :, pl.ds(0, width)]),
+            (self.gu_ref.at[:, pl.ds(high, width)], self.gu_out.at[slot, :, pl.ds(width, width)]),
+            (self.dn_ref.at[:, pl.ds(low, width)], self.dn_out.at[slot]),
+        ]
+
+    def line_copy(self, place, piece, slot):
+        source, landing = self.pieces(self.others[place], slot)[piece]
+        return pltpu.make_async_remote_copy(
+            src_ref=source,
+            dst_ref=landing,
+            send_sem=self.line_sems.at[place, piece],
+            recv_sem=self.recv_sems.at[slot, piece],
+            device_id={"z": self.others[place]},
+            device_id_type=MESH,
+        )
+
+    def own_copy(self, piece):
+        source, landing = self.pieces(self.z, self.own)[piece]
+        return pltpu.make_async_copy(source, landing, self.own_sems.at[piece])
+
+    def bit_copy(self, slot, piece, stage, send_sem):
+        ref = (self.gu_out, None, self.dn_out)[piece]
+        return pltpu.make_async_remote_copy(
+            src_ref=ref.at[slot],
+            dst_ref=ref.at[slot],
+            send_sem=send_sem,
+            recv_sem=self.recv_sems.at[slot, piece],
+            device_id={self.bits[stage]: 1 - self.mine[stage]},
+            device_id_type=MESH,
+        )
+
+    def first_copy(self, slot, piece, stage, send_sem):
+        source, landing = self.pieces(self.z, slot)[piece]
+        return pltpu.make_async_remote_copy(
+            src_ref=source,
+            dst_ref=landing,
+            send_sem=send_sem,
+            recv_sem=self.recv_sems.at[slot, piece],
+            device_id={self.bits[stage]: 1 - self.mine[stage]},
+            device_id_type=MESH,
+        )
+
+    def spread(self, slot, number, variant, after):
+        for stage in range(after, self.count):
+            for piece in (0, 2):
+                make = functools.partial(
+                    self.bit_copy, slot, piece, stage, self.bit_sems.at[number, variant, stage, piece]
+                )
+                self.pending.append(make)
+                make().start()
+
+    def on_bits(self, number):
+        line = lax.rem(self.z - number + self.size, self.size)
+        for stage in range(self.count):
+            for variant in range(2**stage):
+                flips = bit_flips(variant, stage, self.count)
+                slot = slot_of(line, [1 - m if f else m for m, f in zip(self.mine, flips)])
+                if number == 0 and variant == 0:
+                    for piece in range(3):
+                        self.first_copy(slot, piece, stage, self.own_sems.at[0]).wait_recv()
+                else:
+                    for piece in (0, 2):
+                        self.bit_copy(slot, piece, stage, self.own_sems.at[0]).wait_recv()
+                self.spread(slot, number, sum(f << b for b, f in enumerate(flips)), stage + 1)
+
+    def begin(self):
+        for stage in range(self.count):
+            for piece in range(3):
+                make = functools.partial(
+                    self.first_copy, self.own, piece, stage, self.bit_sems.at[0, 0, stage, piece]
+                )
+                self.pending.append(make)
+                make().start()
+        for piece in range(3):
+            self.own_copy(piece).start()
+
+    def send(self, offset):
+        for piece in range(3):
+            self.line_copy(offset - 1, piece, self.own).start()
+
+    def sent(self, offset):
+        for piece in range(3):
+            self.line_copy(offset - 1, piece, self.own).wait_send()
+
+    def step(self, offset):
+        slot = slot_of(lax.rem(self.z - offset + self.size, self.size), self.mine)
+        for piece in range(3):
+            self.line_copy(0, piece, slot).wait_recv()
+        self.spread(slot, offset, 0, 0)
+
+    def end(self):
+        for piece in range(3):
+            self.own_copy(piece).wait()
+        for make in self.pending:
+            make().wait_send()
+
+
+def weights_kernel(
+    size, bits, block, half, at_ref, gu_ref, dn_ref, gm_ref, at_out, gu_out, dn_out, gm_out, *sems
+):
+    z = lax.axis_index("z")
+    mine = [lax.axis_index(bit) for bit in bits]
+    others = [lax.rem(z + o, size) for o in range(1, size)]
+    greet(
+        [("z", other) for other in others]
+        + [(bit, 1 - m) for bit, m in zip(bits, mine)]
+        + [("t", 1 - lax.axis_index("t"))],
+        [None] * (size + len(bits)),
+    )
+    rows = Gather(size, ("t",), gm_ref, gm_out, *sems[8:])
+    attention = Gather(size, bits, at_ref, at_out, *sems[:4])
+    feed = Exchange(size, bits, block, half, gu_ref, dn_ref, gu_out, dn_out, sems[4:8])
+    attention.begin()
+    rows.begin()
+    feed.begin()
+    attention.step(1)
+    rows.step(1)
+    attention.step(2)
+    attention.on_bits(0)
+    rows.on_bits(0)
+    rows.step(2)
+    feed.send(1)
+    attention.step(3)
+    attention.on_bits(1)
+    rows.on_bits(1)
+    rows.step(3)
+    feed.on_bits(0)
+    attention.on_bits(2)
+    feed.sent(1)
+    feed.send(3)
+    feed.step(1)
+    attention.on_bits(3)
+    rows.on_bits(2)
+    feed.sent(3)
+    feed.send(2)
+    feed.step(3)
+    feed.on_bits(1)
+    rows.on_bits(3)
+    feed.sent(2)
+    feed.step(2)
+    feed.on_bits(3)
+    feed.on_bits(2)
+    attention.end()
+    feed.end()
+    rows.end()
+
+
+def weights(at, gu, dn, gm, size, bits, block, collective_id):
+    slots = size * 2 ** len(bits)
+    rows, half = dn.shape
+    return pl.pallas_call(
+        functools.partial(weights_kernel, size, bits, block, half),
+        out_shape=(
+            jax.ShapeDtypeStruct((slots, *at.shape), at.dtype),
+            jax.ShapeDtypeStruct((slots, rows, 2 * block), gu.dtype),
+            jax.ShapeDtypeStruct((slots, rows, block), dn.dtype),
+            jax.ShapeDtypeStruct((2 * size, *gm.shape), gm.dtype),
+        ),
+        in_specs=[pl.BlockSpec(memory_space=pl.ANY)] * 4,
+        out_specs=[pl.BlockSpec(memory_space=pl.ANY)] * 4,
+        scratch_shapes=[
+            *gather_semaphores(size, bits),
+            pltpu.SemaphoreType.DMA((3,)),
+            pltpu.SemaphoreType.DMA((size - 1, 3)),
+            pltpu.SemaphoreType.DMA((size, 2 ** len(bits), len(bits), 3)),
+            pltpu.SemaphoreType.DMA((slots, 3)),
+            *gather_semaphores(size, ("t",)),
+        ],
+        compiler_params=pltpu.CompilerParams(collective_id=collective_id, has_side_effects=True),
+        cost_estimate=pl.CostEstimate(
+            flops=0, transcendentals=0, bytes_accessed=slots * gu.size * 27
+        ),
+    )(at, gu, dn, gm)
+
+
+class Fold:
+    def __init__(self, size, bits, order, p_ref, own_buf, sums, stage_in, stage_out, own_sems, send_sems, recv_sems):
+        self.size, self.bits, self.count, self.order = size, bits, len(bits), order
+        self.last = self.count - 1
+        self.p_ref, self.own_buf, self.sums = p_ref, own_buf, sums
+        self.stage_in, self.stage_out = stage_in, stage_out
+        self.own_sems, self.send_sems, self.recv_sems = own_sems, send_sems, recv_sems
+        self.z = lax.axis_index("z")
+        self.mine = [lax.axis_index(bit) for bit in bits]
+
+    def line(self, place):
+        return lax.rem(self.z + self.order[place], self.size)
+
+    def index(self, place, stage, variant):
+        return place * (2**self.count - 1) + 2**stage - 1 + variant
+
+    def slot(self, place, variant, flip):
+        flips = [(variant >> b) & 1 for b in range(self.last)] + [flip]
+        return slot_of(self.line(place), [1 - m if f else m for m, f in zip(self.mine, flips)])
+
+    def copy(self, place, stage, variant):
+        index = self.index(place, stage, variant)
+        if stage == self.last:
+            source = self.p_ref.at[self.slot(place, variant, 1)]
+        else:
+            source = self.stage_out.at[place * (2**self.last - 1) + 2**stage - 1 + variant]
+        return pltpu.make_async_remote_copy(
+            src_ref=source,
+            dst_ref=self.stage_in.at[index],
+            send_sem=self.send_sems.at[index],
+            recv_sem=self.recv_sems.at[index],
+            device_id={self.bits[stage]: 1 - self.mine[stage]},
+            device_id_type=MESH,
+        )
+
+    def own_copy(self, place, variant):
+        number = place * 2**self.last + variant
+        return pltpu.make_async_copy(
+            self.p_ref.at[self.slot(place, variant, 0)], self.own_buf.at[number], self.own_sems.at[number]
+        )
+
+    def begin(self, places=None):
+        for place in range(self.size) if places is None else places:
+            for variant in reversed(range(2**self.last)):
+                self.copy(place, self.last, variant).start()
+                self.own_copy(place, variant).start()
+
+    def stage(self, place, stage, done=None):
+        for variant in reversed(range(2**stage)):
+            if stage == self.last:
+                self.own_copy(place, variant).wait()
+                held = self.own_buf[place * 2**self.last + variant].astype(F32)
+            else:
+                held = self.sums[place * (2**self.last - 1) + 2**stage - 1 + variant]
+            self.copy(place, stage, variant).wait_recv()
+            total = held + self.stage_in[self.index(place, stage, variant)].astype(F32)
+            if stage == 0:
+                done(place, total)
+                continue
+            lower = variant & (2 ** (stage - 1) - 1)
+            number = place * (2**self.last - 1) + 2 ** (stage - 1) - 1 + lower
+            if variant >> (stage - 1):
+                self.stage_out[number] = total.astype(LOW)
+                self.copy(place, stage - 1, lower).start()
+            else:
+                self.sums[number] = total
+
+    def end(self):
+        for place in range(self.size):
+            for stage in range(self.count):
+                for variant in range(2**stage):
+                    self.copy(place, stage, variant).wait_send()
+
+
+def fold_scratch(size, bits, rows, columns):
+    count = len(bits)
+    inner, lower = size * (2**count - 1), size * (2 ** (count - 1) - 1)
+    return [
+        pltpu.VMEM((size * 2 ** (count - 1), rows, columns), LOW),
+        pltpu.VMEM((max(lower, 1), rows, columns) if lower else (1, 8, LANES), F32),
+        pltpu.VMEM((inner, rows, columns), LOW),
+        pltpu.VMEM((max(lower, 1), rows, columns) if lower else (1, 16, LANES), LOW),
+        pltpu.SemaphoreType.DMA((size * 2 ** (count - 1),)),
+        pltpu.SemaphoreType.DMA((inner,)),
+        pltpu.SemaphoreType.DMA((inner,)),
+    ]
+
+
+class Scatter:
+    def __init__(self, size, bits, p_ref, out_ref, line_out, line_in, line_send, line_recv, *fold):
+        order = list(range(1, size)) + [0]
+        self.fold = Fold(size, bits, order, p_ref, *fold)
+        self.size, self.out_ref = size, out_ref
+        self.line_out, self.line_in, self.line_send, self.line_recv = line_out, line_in, line_send, line_recv
+
+    def line_copy(self, place):
+        return pltpu.make_async_remote_copy(
+            src_ref=self.line_out.at[place],
+            dst_ref=self.line_in.at[place],
+            send_sem=self.line_send.at[place],
+            recv_sem=self.line_recv.at[place],
+            device_id={"z": self.fold.line(place)},
+            device_id_type=MESH,
+        )
+
+    def done(self, place, total):
+        if place < self.size - 1:
+            self.line_out[place] = total.astype(LOW)
+            self.line_copy(place).start()
+        else:
+            self.out_ref[...] = total
+
+    def begin(self):
+        self.fold.begin()
+
+    def place(self, place):
+        for stage in reversed(range(self.fold.count)):
+            self.fold.stage(place, stage, self.done)
+
+    def finish(self):
+        for place in range(self.size - 1):
+            self.line_copy(place).wait_recv()
+            self.out_ref[...] += self.line_in[place].astype(F32)
+
+    def end(self):
+        self.fold.end()
+        for place in range(self.size - 1):
+            self.line_copy(place).wait_send()
+
+
+def scatter_scratch(size, bits, rows, columns):
+    return [
+        pltpu.VMEM((size - 1, rows, columns), LOW),
+        pltpu.VMEM((size - 1, rows, columns), LOW),
+        pltpu.SemaphoreType.DMA((size - 1,)),
+        pltpu.SemaphoreType.DMA((size - 1,)),
+        *fold_scratch(size, bits, rows, columns),
+    ]
+
+
+SCATTER_REFS = 11
+
+
+class Total:
+    def __init__(self, size, bits, x_ref, out_ref, held, landed, send_sems, recv_sems):
+        self.size, self.bits, self.count = size, bits, len(bits)
+        self.x_ref, self.out_ref, self.held, self.landed = x_ref, out_ref, held, landed
+        self.send_sems, self.recv_sems = send_sems, recv_sems
+        self.z = lax.axis_index("z")
+        self.others = [lax.rem(self.z + o, size) for o in range(1, size)]
+
+    def copy(self, number):
+        if number < self.count:
+            axis = self.bits[number]
+            source, target = self.held.at[number], {axis: 1 - lax.axis_index(axis)}
+        else:
+            source, target = self.held.at[self.count], {"z": self.others[number - self.count]}
+        return pltpu.make_async_remote_copy(
+            src_ref=source,
+            dst_ref=self.landed.at[number],
+            send_sem=self.send_sems.at[number],
+            recv_sem=self.recv_sems.at[number],
+            device_id=target,
+            device_id_type=MESH,
+        )
+
+    def begin(self):
+        self.held[0] = self.x_ref[...]
+        self.copy(0).start()
+
+    def pair(self, number):
+        self.copy(number).wait_recv()
+        self.held[number + 1] = self.held[number] + self.landed[number]
+        if number + 1 < self.count:
+            self.copy(number + 1).start()
+        else:
+            for place in range(self.size - 1):
+                self.copy(self.count + place).start()
+
+    def finish(self):
+        for place in range(self.size - 1):
+            self.copy(self.count + place).wait_recv()
+        total = jnp.zeros(self.out_ref.shape, self.out_ref.dtype)
+        for line in range(self.size):
+            offset = lax.rem(line - self.z + self.size, self.size)
+            part = self.held[self.count]
+            for o in range(1, self.size):
+                part = jnp.where(offset == o, self.landed[self.count + self.size - o - 1], part)
+            total = total + part
+        self.out_ref[...] = total
+
+    def end(self):
+        for number in range(self.count + self.size - 1):
+            self.copy(number).wait_send()
+
+
+def greet_all(size, axes):
+    z = lax.axis_index("z")
+    greet(
+        [("z", lax.rem(z + o, size)) for o in range(1, size)]
+        + [(axis, 1 - lax.axis_index(axis)) for axis in axes],
+        [None] * (size - 1 + len(axes)),
+    )
+
+
+def in_groups(refs, sizes):
+    groups, at = [], 0
+    for number in sizes:
+        groups.append(refs[at : at + number])
+        at += number
+    return groups
+
+
+def comm_params(collective_id):
+    return pltpu.CompilerParams(
+        collective_id=collective_id, has_side_effects=True, vmem_limit_bytes=56 * 2**20
+    )
+
+
+def at_microseconds(time):
+    return pl.CostEstimate(flops=0, transcendentals=0, bytes_accessed=time * 3500000)
+
+
+def scatter_kernel(size, bits, p_ref, out_ref, *refs):
+    greet_all(size, bits)
+    steps = Scatter(size, bits, p_ref, out_ref, *refs)
+    steps.begin()
+    for place in range(size):
+        steps.place(place)
+    steps.finish()
+    steps.end()
+
+
+def scatter(partial, size, bits, collective_id):
+    slots, rows, columns = partial.shape
+    return pl.pallas_call(
+        functools.partial(scatter_kernel, size, bits),
+        out_shape=jax.ShapeDtypeStruct((rows, columns), F32),
+        in_specs=[pl.BlockSpec(memory_space=pl.ANY)],
+        out_specs=pl.BlockSpec(memory_space=pltpu.VMEM),
+        scratch_shapes=scatter_scratch(size, bits, rows, columns),
+        compiler_params=comm_params(collective_id),
+        cost_estimate=at_microseconds(48),
+    )(partial)
+
+
+def last_kernel(size, bits, p_ref, x_ref, out_ref, sum_ref, *refs):
+    greet_all(size, ("t", *bits))
+    given, rest = in_groups(refs, [SCATTER_REFS, 4])
+    small = Total(size, ("t", *bits), x_ref, sum_ref, *rest)
+    steps = Scatter(size, bits, p_ref, out_ref, *given)
+    small.begin()
+    steps.begin()
+    for place in range(size):
+        steps.place(place)
+        if place <= len(bits):
+            small.pair(place)
+    for number in range(size, len(bits) + 1):
+        small.pair(number)
+    steps.finish()
+    small.finish()
+    steps.end()
+    small.end()
+
+
+def last(partial, x, size, bits, collective_id):
+    slots, rows, columns = partial.shape
+    number = len(bits) + 1
+    return pl.pallas_call(
+        functools.partial(last_kernel, size, bits),
+        out_shape=(jax.ShapeDtypeStruct((rows, columns), F32), jax.ShapeDtypeStruct(x.shape, F32)),
+        in_specs=[pl.BlockSpec(memory_space=pl.ANY), pl.BlockSpec(memory_space=pltpu.VMEM)],
+        out_specs=[pl.BlockSpec(memory_space=pltpu.VMEM)] * 2,
+        scratch_shapes=[
+            *scatter_scratch(size, bits, rows, columns),
+            pltpu.VMEM((number + 1, *x.shape), F32),
+            pltpu.VMEM((number + size - 1, *x.shape), F32),
+            pltpu.SemaphoreType.DMA((number + size - 1,)),
+            pltpu.SemaphoreType.DMA((number + size - 1,)),
+        ],
+        compiler_params=comm_params(collective_id),
+        cost_estimate=at_microseconds(60),
+    )(partial, x)
+
+
+def back_kernel(size, bits, branches, *refs):
+    p_refs, (gu_ref, dn_ref), outs, (folded,), refs = in_groups(
+        refs, [branches, 2, branches, 1, len(refs)]
+    )
+    greet_all(size, ("t", *bits))
+    *scatters, gu_scratch, dn_scratch, (gu_done, dn_done, done_sems) = in_groups(
+        refs, [SCATTER_REFS] * branches + [7, 7, 3]
+    )
+    scatters = [
+        Scatter(size, ("t",), p, out, *scratch) for p, out, scratch in zip(p_refs, outs, scatters)
+    ]
+    order = list(range(size))
+    gu = Fold(size, bits, order, gu_ref, *gu_scratch)
+    dn = Fold(size, bits, order, dn_ref, *dn_scratch)
+    width, narrow = gu_ref.shape[2], dn_ref.shape[2]
+
+    def out_copy(number, place, line):
+        source = (gu_done, dn_done)[number].at[place]
+        low, count = ((0, width), (width, narrow))[number]
+        return pltpu.make_async_copy(
+            source, folded.at[line, :, pl.ds(low, count)], done_sems.at[number, place]
+        )
+
+    def done(number):
+        def keep(place, total):
+            (gu_done, dn_done)[number][place] = total.astype(LOW)
+            out_copy(number, place, gu.line(place)).start()
+
+        return keep
+
+    for steps in scatters:
+        steps.begin()
+    gu.begin()
+    dn.begin()
+    for place in range(size):
+        for stage in reversed(range(1, len(bits))):
+            gu.stage(place, stage)
+            dn.stage(place, stage)
+        for steps in scatters:
+            steps.place(place)
+    for steps in scatters:
+        steps.finish()
+    for place in range(size):
+        gu.stage(place, 0, done(0))
+        dn.stage(place, 0, done(1))
+    for place in range(size):
+        for number in range(2):
+            out_copy(number, place, gu.line(place)).wait()
+    for steps in (*scatters, gu, dn):
+        steps.end()
+
+
+def back(partials, gu, dn, size, bits, collective_id):
+    _, rows, columns = partials[0].shape
+    slots, few, width = gu.shape
+    narrow = dn.shape[2]
+    branches = len(partials)
+    out = pl.pallas_call(
+        functools.partial(back_kernel, size, bits, branches),
+        out_shape=(
+            *([jax.ShapeDtypeStruct((rows, columns), F32)] * branches),
+            jax.ShapeDtypeStruct((size, few, width + narrow), LOW),
+        ),
+        in_specs=[pl.BlockSpec(memory_space=pl.ANY)] * (branches + 2),
+        out_specs=[pl.BlockSpec(memory_space=pltpu.VMEM)] * branches + [pl.BlockSpec(memory_space=pl.ANY)],
+        scratch_shapes=[
+            *(scatter_scratch(size, ("t",), rows, columns) * branches),
+            *fold_scratch(size, bits, few, width),
+            *fold_scratch(size, bits, few, narrow),
+            pltpu.VMEM((size, few, width), LOW),
+            pltpu.VMEM((size, few, narrow), LOW),
+            pltpu.SemaphoreType.DMA((2, size)),
+        ],
+        compiler_params=comm_params(collective_id),
+        cost_estimate=at_microseconds(80),
+    )(*partials, gu, dn)
+    return out[:branches], out[branches]
+
+
 def spread_group(rows):
-    return lax.all_gather(rows, ("z", "t"), axis=0, tiled=True)
+    return gather(rows, LINE, ("t",), 1).reshape(-1, rows.shape[1])
+
+
+def in_slots(partial, slots):
+    return partial.reshape(slots, -1, partial.shape[1])
 
 
 def sum_group(partial):
-    return lax.psum_scatter(partial, ("z", "t"), scatter_dimension=0, tiled=True).astype(F32)
+    return scatter(in_slots(partial, 2 * LINE), LINE, ("t",), 2)
 
 
 def block_width(half):
     return -(-half // (LINE * LANES)) * LANES
 
 
-def to_blocks(weight, parts):
-    rows = weight.shape[0]
-    half = weight.shape[1] // parts
-    block = block_width(half)
-    padded = jnp.pad(weight.reshape(rows, parts, half), ((0, 0), (0, 0), (0, LINE * block - half)))
-    return padded.reshape(rows, parts, LINE, block).transpose(2, 0, 1, 3).reshape(LINE, rows, parts * block)
+def block_start(line, block, half):
+    return min(line * block, half - block)
+
+
+def tie(value, *others):
+    return lax.optimization_barrier((value, *others))
+
+
+def column_sections(gu, dn, block):
+    half = dn.shape[1]
+    sections = []
+    for line in range(LINE):
+        low = block_start(line, block, half)
+        parts = [gu[:, low : low + block], gu[:, half + low : half + low + block], dn[:, low : low + block]]
+        sections.append(jnp.concatenate(parts, axis=1))
+    return jnp.stack(sections)
 
 
 def from_blocks(blocks, parts, half):
-    rows = blocks.shape[1]
-    block = blocks.shape[2] // parts
-    joined = blocks.reshape(LINE, rows, parts, block).transpose(1, 2, 0, 3)
-    return joined.reshape(rows, parts, LINE * block)[:, :, :half].reshape(rows, parts * half)
-
-
-def gather_blocks(weight, parts, bits):
-    blocks = lax.all_to_all(to_blocks(weight, parts), "z", 0, 0, tiled=True)
-    rows, width = blocks.shape[1:]
-    lead = [LINE]
-    current = blocks
-    for bit in bits:
-        other = lax.ppermute(current, bit, SWAP)
-        current = join_pair(current, other, bit, len(lead))
-        lead.append(2)
-    return current.reshape(-1, width)
-
-
-def reduce_blocks(grad, parts, half, bits, rows):
-    width = grad.shape[1]
-    current = grad.reshape(*([LINE] + [2] * len(bits)), rows, width)
-    for number in reversed(range(len(bits))):
-        index = lax.axis_index(bits[number])
-        own = take(current, index, 1 + number)
-        other = lax.ppermute(take(current, 1 - index, 1 + number), bits[number], SWAP)
-        current = (own.astype(F32) + other.astype(F32)).astype(LOW)
-    blocks = lax.all_to_all(current, "z", 0, 0, tiled=True)
-    return from_blocks(blocks, parts, half).astype(F32)
+    block = blocks.shape[2] // 3
+    pieces = []
+    for part in parts:
+        for line in range(LINE):
+            skip = line * block - block_start(line, block, half)
+            pieces.append(blocks[line, :, part * block + skip : (part + 1) * block])
+    return jnp.concatenate(pieces, axis=1).astype(F32)
 
 
 def local(
@@ -171,19 +893,27 @@
     sin_k = sine[:, None, :]
     gain_attn = norm_attn.astype(F32)
     gain_ffn = norm_ffn.astype(F32)
-    attn_weights, ffn_weights = [], []
-    for layer in range(layers):
-        both = lax.all_gather(
-            jnp.concatenate([w_qkv[layer], w_out[layer]], axis=1), dp, axis=0, tiled=True
-        )
-        attn_weights.append((both[:, :qkv_width], both[:, qkv_width:]))
-        ffn_weights.append(
-            (gather_blocks(w_gateup[layer], 2, bits), gather_blocks(w_down[layer], 1, bits))
-        )
+    flats = [jnp.concatenate([w_qkv[layer], w_out[layer]], axis=1) for layer in range(layers)]
+    both_w, gu_w, down_w, gm_all = weights(
+        flats[0], w_gateup[0], w_down[0], cotangent, LINE, bits, block, 3
+    )
+    attn_weights = [both_w.reshape(-1, flats[0].shape[1])]
+    ffn_weights = [(gu_w.reshape(-1, 2 * block), down_w.reshape(-1, block))]
+    gm_all = gm_all.reshape(-1, cotangent.shape[1])
+    line = lax.axis_index("z")
+    valid = jnp.arange(block) >= line * block - jnp.minimum(line * block, half - block)
     saved = []
     state = tokens.astype(F32)
     for layer in range(layers):
-        qkv_w, out_w = attn_weights[layer]
+        both_w = attn_weights[layer]
+        ahead = layer + 1 < layers
+        if ahead:
+            flat, sections = flats[layer + 1], column_sections(w_gateup[layer + 1], w_down[layer + 1], block)
+            both_w, flat, sections = tie(both_w, flat, sections)
+            coming = lax.all_gather(flat, dp, axis=0, tiled=True)
+            sections = lax.all_to_all(sections, "z", 0, 0, tiled=True)
+        attn_weights[layer] = both_w
+        qkv_w, out_w = both_w[:, :qkv_width], both_w[:, qkv_width:]
         factor_a = rms_factor(state)
         xa_all = spread_pair((state * factor_a * gain_attn[layer]).astype(LOW))
         lin = jnp.dot(xa_all, qkv_w, preferred_element_type=F32) + b_qkv[layer].astype(F32)
@@ -208,37 +938,59 @@
         gu_w, down_w = ffn_weights[layer]
         factor_f = rms_factor(middle)
         xf_all = spread_group((middle * factor_f * gain_ffn[layer]).astype(LOW))
+        if ahead:
+            xf_all, sections = tie(xf_all, sections)
+            sections = join_pair(sections, lax.ppermute(sections, bits[0], SWAP), bits[0], 1)
         gate_up = jnp.dot(xf_all, gu_w, preferred_element_type=F32)
         gate = gate_up[:, :block]
         up = gate_up[:, block:]
-        act = (jax.nn.silu(gate) * up).astype(LOW)
-        after = middle + sum_group(contract_last(act, down_w, LOW))
+        act = jnp.where(valid, jax.nn.silu(gate) * up, 0.0).astype(LOW)
+        partial = contract_last(act, down_w, LOW)
+        if ahead:
+            branch = sum_group(partial)
+            branch, sections, coming = tie(branch, sections, coming)
+            for number, bit in enumerate(bits[1:]):
+                sections = join_pair(sections, lax.ppermute(sections, bit, SWAP), bit, 2 + number)
+            sections = sections.reshape(-1, 3 * block)
+            ffn_weights.append((sections[:, : 2 * block], sections[:, 2 * block :]))
+            attn_weights.append(coming)
+            after = middle + branch
         saved.append(
             (state, factor_a, xa_all, query, key, value, log_total, attended)
             + (middle, factor_f, xf_all, gate, up, act)
         )
-        state = after
-    output = state.astype(LOW)
+        if ahead:
+            state = after
     grad = cotangent.astype(F32)
-    grads_attn, grads_gu, grads_down, grads_bias, grads_ga, grads_gf = ([] for _ in range(6))
+    grads_attn, grads_bias, grads_ga, grads_gf = ([] for _ in range(4))
+    waiting, branches = None, [in_slots(partial, 2 * LINE)]
+    grads_blocks = []
     for layer in reversed(range(layers)):
         (state_in, factor_a, xa_all, query, key, value, log_total, attended) = saved[layer][:8]
         (middle, factor_f, xf_all, gate, up, act) = saved[layer][8:]
         gu_w, down_w = ffn_weights[layer]
-        qkv_w, out_w = attn_weights[layer]
-        gm_all = spread_group(grad.astype(LOW))
+        both_w = attn_weights[layer]
+        qkv_w, out_w = both_w[:, :qkv_width], both_w[:, qkv_width:]
+        if waiting is not None:
+            gm_all = spread_group(grad.astype(LOW))
         d_down = contract_first(gm_all, act, LOW)
         d_act = jnp.dot(gm_all, down_w, preferred_element_type=F32)
         sig = jax.nn.sigmoid(gate)
         d_gate = d_act * up * sig * (1.0 + gate * (1.0 - sig))
         d_up = d_act * gate * sig
-        d_gu = jnp.concatenate([d_gate, d_up], axis=1).astype(LOW)
-        d_xf = sum_group(contract_last(d_gu, gu_w, LOW))
+        d_gu = jnp.concatenate(
+            [jnp.where(valid, d_gate, 0.0), jnp.where(valid, d_up, 0.0)], axis=1
+        ).astype(LOW)
+        d_gateup = contract_first(xf_all, d_gu, LOW)
+        branches.insert(0, in_slots(contract_last(d_gu, gu_w, LOW), 2 * LINE))
+        slots = in_slots(d_gateup, d_gateup.shape[0] // rows), in_slots(d_down, d_down.shape[0] // rows)
+        (d_xf, *others), folded = back(branches, *slots, LINE, bits, 6 + layer)
+        branches = []
+        if others:
+            output = (middle + others[0]).astype(LOW)
+        waiting = lax.all_to_all(folded, "z", 0, 0, tiled=True)
         d_mid, part_f = norm_back(d_xf, middle, factor_f, gain_ffn[layer])
         grad = grad + d_mid
-        d_gateup = contract_first(xf_all, d_gu, LOW)
-        grads_gu.append(reduce_blocks(d_gateup, 2, half, bits, rows))
-        grads_down.append(reduce_blocks(d_down, 1, half, bits, rows))
         ga_all = spread_pair(grad.astype(LOW))
         d_att = jnp.dot(ga_all, out_w, preferred_element_type=F32).astype(LOW)
         raw = jnp.einsum("qkgd,pkd->kgqp", query, key, preferred_element_type=F32)
@@ -268,12 +1020,18 @@
         d_xa = sum_pair(contract_last(d_lin_low, qkv_w))
         d_in, part_a = norm_back(d_xa, state_in, factor_a, gain_attn[layer])
         grad = grad + d_in
+        if layer > 0:
+            grad, waiting = tie(grad, waiting)
+        grads_blocks.append(waiting)
         d_both = jnp.concatenate(
             [contract_first(xa_all, d_lin_low, LOW), contract_first(ga_all, attended, LOW)], axis=1
         )
-        grads_attn.append(
-            lax.psum_scatter(d_both, dp, scatter_dimension=0, tiled=True).astype(F32)
-        )
+        if layer == 0:
+            d_both = in_slots(d_both, d_both.shape[0] // rows)
+        else:
+            grads_attn.append(
+                lax.psum_scatter(d_both, dp, scatter_dimension=0, tiled=True).astype(F32)
+            )
         grads_ga.append(part_a)
         grads_gf.append(part_f)
 
@@ -285,8 +1043,15 @@
     spread = jnp.where(
         (jnp.arange(tensor_size) == side)[:, None, None], bias[None], jnp.zeros_like(bias)[None]
     )
-    full_ga, full_gf, full_bias = lax.psum(
-        (ordered(grads_ga), ordered(grads_gf), spread), (*dp, "t")
+    small = (ordered(grads_ga), ordered(grads_gf), spread)
+    flat = jnp.concatenate([item.reshape(-1, LANES) for item in small], axis=0)
+    last_attn, flat = last(d_both, flat, LINE, bits, 4)
+    grads_attn.append(last_attn)
+    full_ga, full_gf, full_bias = (
+        part.reshape(item.shape)
+        for part, item in zip(
+            jnp.split(flat, [small[0].size // LANES, 2 * small[0].size // LANES], axis=0), small
+        )
     )
     both = ordered(grads_attn)
     return (
@@ -297,8 +1062,8 @@
         both[:, :, :qkv_width],
         take(full_bias, side, 0),
         both[:, :, qkv_width:],
-        ordered(grads_gu),
-        ordered(grads_down),
+        ordered([from_blocks(blocks, (0, 1), half) for blocks in grads_blocks]),
+        ordered([from_blocks(blocks, (2,), half) for blocks in grads_blocks]),
     )
 
 

time: 1200 us -> 1010 us (0.84)
  Pallas kernels: 0 us -> 604 us
  waiting for transfers between devices: 584 us -> 51.8 us
  local copies, waits for them, and re-layouts: 166 us -> 83.9 us
  blocking collectives: 69.6 us -> 0 us
  other arithmetic: 123 us -> 73.7 us
  starting transfers between devices: 66.5 us -> 24.7 us
  matrix products: 156 us -> 138 us
    pallas_call x0 -> x8, Pallas kernels: none -> 604 us  [the longest x3 195 us: gather(): pl.pallas_call(functools.partial(gather_kernel, size, bits), out_shape=ja...]
    reduce_scatter x4 -> x1, waiting for transfers between devices: 168 us -> 0.01 us  [local(): lax.psum_scatter(d_both, dp, scatter_dimension=0, tiled=True).astype(F32)]
    all_to_all x8 -> x3, waiting for transfers between devices: 179 us -> 23.7 us  [the longest x2 23.7 us: local(): waiting = lax.all_to_all(folded, 'z', 0, 0, tiled=True)]
    all_gather x6 -> x1, waiting for transfers between devices: 102 us -> 0.01 us  [local(): coming = lax.all_gather(flat, dp, axis=0, tiled=True)]
    ppermute x16 -> x2, waiting for transfers between devices: 89.8 us -> 0.01 us  [the longest x1 0.01 us: local(): lax.ppermute(sections, bits[0], SWAP)]
    psum x1 -> x0, blocking collectives: 69.6 us -> none  [local(): lax.psum((ordered(grads_ga), ordered(grads_gf), spread), (*dp, 't'))]
    reshape x14 -> x5, local copies, waits for them, and re-layouts: 37.8 us -> 1.87 us  [the longest x3 1.24 us: local(): part.reshape(item.shape)]
    all_to_all x8 -> x3, starting transfers between devices: 47.3 us -> 16.4 us  [the longest x2 11.2 us: local(): waiting = lax.all_to_all(folded, 'z', 0, 0, tiled=True)]
  transfers between devices with their start and end apart: 44 -> 15, of which waited for: 27 -> 7; matrix products, arithmetic and copies ran while one was open for 30% -> 21% of each run, Pallas kernels for 0% -> 50%
where the time goes in v2:
time: 1010 us; the launch traced here: 995 us
  Pallas kernels  604 us (60%)
  matrix products  138 us (14%)
  local copies, waits for them, and re-layouts  83.9 us (8%)
  other arithmetic  73.7 us (7%)
  waiting for transfers between devices  51.8 us (5%)
  starting transfers between devices  24.7 us (2%)
  between operations  18.7 us (2%)
    pallas_call x3, Pallas kernels, gather(): pl.pallas_call(functools.partial(gather_kernel, size, bits), out_shape=ja...  195 us
    pallas_call x2, Pallas kernels, back(): pl.pallas_call(functools.partial(back_kernel, size, bits, branches), out_...  175 us
    pallas_call x1, Pallas kernels, weights(): pl.pallas_call(functools.partial(weights_kernel, size, bits, block, half)...  135 us
    pallas_call x1, Pallas kernels, last(): pl.pallas_call(functools.partial(last_kernel, size, bits), out_shape=(jax...  52.5 us
    pallas_call x1, Pallas kernels, scatter(): pl.pallas_call(functools.partial(scatter_kernel, size, bits), out_shape=j...  47 us
    dot_general x8, matrix products, contract_last(): lax.dot_general(left, right, (((1,), (1,)), ((), ())), preferred_element_...  40.5 us
    dot_general x8, matrix products, contract_first(): lax.dot_general(left, right, (((0,), (0,)), ((), ())), preferred_element_...  40.1 us
    unnamed x238, local copies, waits for them, and re-layouts  29.4 us
  transfers between devices with their start and end apart: 15, of which 7 were waited for; matrix products, arithmetic and copies ran while one was open for 21% of the time, Pallas kernels for 50%

profile of v2, /device:TPU:26, one launch (start us, length us, event | category | flops | bytes accessed | tf_op | source)
XLA Modules:
  0.0 994.9 jit_solution(18414680977378620535)
XLA Ops:
  12.4 3.4 slice_bitcast_fusion
  21.5 135.2 %shard_map.169 = (bf16[16,96,1792]{2,1,0:T(8,128)(2,1)}, bf16[16,96,2304]{2,1,0:T(8,128)(2,1)}, bf16[16,96,1152]{2,1,0:T(8,128)(2,1)}, bf16[8,128,1536]{2,1,0:T(8,128)(2,1)}) custom-call(bf16[96,1792]{1,0:T(8,128)(2,1)} %get-tuple-element.164.at_ref, bf16[96,8960]{1,0:T(8,128)(2,1)} %get-tuple-element.79.gu_ref, bf16[96,4480]{1,0:T(8,128)(2,1)} %get-tuple-element.101.dn_ref, ...), custom_call_target="tpu_custom_call" | custom-call | bytes 371589120 | tf_op jit(solution)/shard_map/pallas_call | solution.py:438
  156.8 5.2 all-to-all-start
  165.9 2.6 subtract_convert_fusion
  170.7 3.2 fusion.50
  184.7 2.6 fusion.32
  190.8 8.6 collective-permute-done.1
  202.2 86.9 %shard_map.170 = bf16[8,128,1536]{2,1,0:T(8,128)(2,1)} custom-call(bf16[128,1536]{1,0:T(8,128)(2,1)} %multiply_convert_fusion.2.refs_0_), custom_call_target="tpu_custom_call" | custom-call | bytes 157286400 | tf_op jit(solution)/shard_map/pallas_call | solution.py:258
  290.7 10.5 %fusion.145 = f32[1024,2304]{1,0:T(8,128)S(1)} fusion(bf16[1024,1536]{1,0:T(8,128)(2,1)} %bitcast.383, bf16[1536,2304]{1,0:T(8,128)(2,1)} %bitcast.416), kind=kOutput, calls=%fused_computation.306 | convolution fusion | flops 7247757312 | bytes 19660800 | tf_op jit(solution)/shard_map/dot_general | solution.py:944
  302.8 2.8 copy-done.8
  305.8 5.6 fusion.146.p_ref
  311.5 47.0 %shard_map.171 = f32[128,1536]{1,0:T(8,128)} custom-call(bf16[8,128,1536]{2,1,0:T(8,128)(2,1)} %fusion.146.p_ref), custom_call_target="tpu_custom_call" | custom-call | bytes 168000000 | tf_op jit(solution)/shard_map/pallas_call | solution.py:698
  358.5 6.1 maximum_select_fusion.1
  366.3 7.7 collective-permute-done.3
  385.5 2.5 fusion.30
  389.7 4.6 copy.81
  399.5 40.9 %shard_map.172 = bf16[8,128,1536]{2,1,0:T(8,128)(2,1)} custom-call(bf16[128,1536]{1,0:T(8,128)(2,1)} %multiply_convert_fusion.refs_0_), custom_call_target="tpu_custom_call" | custom-call | bytes 157286400 | tf_op jit(solution)/shard_map/pallas_call | solution.py:258
  440.4 4.7 copy.80
  445.1 8.6 maximum_select_fusion
  453.7 9.8 fusion.2
  463.4 9.4 select_convert_fusion.4
  472.9 5.7 fusion.14
  478.6 5.6 fusion.28.refs_3_
  484.2 8.9 fusion
  493.1 9.9 fusion.12.refs_2_
  503.0 109.2 %shard_map.173 = (f32[128,1536]{1,0:T(8,128)}, f32[128,1536]{1,0:T(8,128)}, bf16[4,96,3456]{2,1,0:T(8,128)(2,1)}) custom-call(bf16[8,128,1536]{2,1,0:T(8,128)(2,1)} %bitcast.376, bf16[8,128,1536]{2,1,0:T(8,128)(2,1)} %bitcast.375, bf16[16,96,2304]{2,1,0:T(8,128)(2,1)} %fusion.12.refs_2_, bf16[16,96,1152]{2,1,0:T(8,128)(2,1)} %fusion.28.refs_3_), custom_call_target="tpu_custom_call" | custom-call | bytes 280000000 | tf_op jit(solution)/shard_map/pallas_call | solution.py:805
  613.6 2.9 fusion.129
  617.6 5.1 all-to-all-start.1
  627.7 3.2 fusion.59
  641.5 3.0 fusion.18
  648.2 2.8 pad_maximum_fusion.1
  655.6 23.7 %all-to-all-done.1 = bf16[4,96,3456]{2,1,0:T(8,128)(2,1)} async-done(((bf16[4,96,3456]{2,1,0:T(8,128)(2,1)}), bf16[4,96,3456]{2,1,0:T(8,128)(2,1)}, u32[]{:S(2)}, u32[]{:S(2)}) %all-to-all-start.1) | async-done | bytes 2654240 | tf_op jit(solution)/shard_map/all_to_all | solution.py:991
  680.1 66.8 %shard_map.174 = bf16[8,128,1536]{2,1,0:T(8,128)(2,1)} custom-call(bf16[128,1536]{1,0:T(8,128)(2,1)} %convert_element_type.318.refs_0_), custom_call_target="tpu_custom_call" | custom-call | bytes 157286400 | tf_op jit(solution)/shard_map/pallas_call | solution.py:258
  746.9 4.7 copy.93
  751.6 8.8 fusion.26.refs_2_
  760.5 7.2 select_convert_fusion.1
  767.7 12.1 %fusion.8 = bf16[1536,2304]{1,0:T(8,128)(2,1)} fusion(bf16[1024,1536]{1,0:T(8,128)(2,1)S(1)} %bitcast.384, bf16[1024,1152]{1,0:T(8,128)(2,1)} %get-tuple-element.74, bf16[1024,1152]{1,0:T(8,128)(2,1)} %get-tuple-element.73), kind=kOutput, calls=%fused_computation.13 | convolution fusion | flops 7257194496 | bytes 14942208 | tf_op jit(solution)/shard_map/dot_general | solution.py:66
  779.9 9.1 fusion.4.refs_0_
  789.0 65.6 %shard_map.175 = (f32[128,1536]{1,0:T(8,128)}, bf16[4,96,3456]{2,1,0:T(8,128)(2,1)}) custom-call(bf16[8,128,1536]{2,1,0:T(8,128)(2,1)} %fusion.4.refs_0_, bf16[16,96,2304]{2,1,0:T(8,128)(2,1)} %bitcast.366, bf16[16,96,1152]{2,1,0:T(8,128)(2,1)} %fusion.26.refs_2_), custom_call_target="tpu_custom_call" | custom-call | bytes 280000000 | tf_op jit(solution)/shard_map/pallas_call | solution.py:805
  854.6 6.1 all-to-all-start.2
  870.7 2.3 fusion.133
  877.5 7.5 collective-permute-done.8
  885.2 2.8 fusion.56
  893.0 3.0 fusion.22
  900.7 2.8 pad_maximum_fusion
  903.5 8.3 copy.103
  912.9 52.5 %shard_map.176 = (f32[96,1792]{1,0:T(8,128)}, f32[80,128]{1,0:T(8,128)}) custom-call(bf16[16,96,1792]{2,1,0:T(8,128)(2,1)} %bitcast.344, f32[80,128]{1,0:T(8,128)} %pad_maximum_fusion.13.x_ref), custom_call_target="tpu_custom_call" | custom-call | bytes 210000000 | tf_op jit(solution)/shard_map/pallas_call | solution.py:731
  980.1 4.9 maximum_convert_fusion
  (407 shorter events, 123.9 us)
Async XLA Ops:
  7.9 162.5 %copy-start.70 = (f32[1536]{0:T(1024)}, f32[1536]{0:T(1024)S(1)}, u32[]{:S(2)}) copy-start(f32[1536]{0:T(1024)S(1)} %get-tuple-element.62) | copy-start | bytes 18436
  9.6 160.8 %copy-start.90 = (f32[128]{0:T(128)}, f32[128]{0:T(128)S(1)}, u32[]{:S(2)}) copy-start(f32[128]{0:T(128)S(1)} %get-tuple-element.137) | copy-start | bytes 1540
  10.8 159.8 %collective-permute-start = (bf16[128,1536]{1,0:T(8,128)(2,1)S(1)}, bf16[128,1536]{1,0:T(8,128)(2,1)S(1)}, u32[]{:S(2)}, u32[]{:S(2)}) collective-permute-start(bf16[128,1536]{1,0:T(8,128)(2,1)S(1)} %fusion.73), channel_id=1, source_target_pairs={{0,1},{1,0},{2,3},{3,2},{4,5},{5,4},{6,7},{7,6},{8,9},{9,8},{10,11... | collective-permute-start | bytes 1179656 | tf_op jit(solution)/shard_map/ppermute | solution.py:91
  156.7 13.1 %copy-start.85 = (bf16[2,1024]{1,0:T(2,128)(2,1)S(1)}, bf16[2,1024]{1,0:T(2,128)(2,1)}, u32[]{:S(2)}) copy-start(bf16[2,1024]{1,0:T(2,128)(2,1)} %param.16) | copy-start | bytes 12292
  156.8 13.7 %copy-start.4 = (bf16[128,1536]{1,0:T(8,128)(2,1)S(1)}, bf16[128,1536]{1,0:T(8,128)(2,1)}, u32[]{:S(2)}) copy-start(bf16[128,1536]{1,0:T(8,128)(2,1)} %param.10) | copy-start | bytes 1179652
  156.8 132.3 %all-to-all-start = ((bf16[4,96,3456]{2,1,0:T(8,128)(2,1)}), bf16[4,96,3456]{2,1,0:T(8,128)(2,1)}, u32[]{:S(2)}, u32[]{:S(2)}) async-start(bf16[4,96,3456]{2,1,0:T(8,128)(2,1)} %pad_maximum_fusion.5), calls=%async_computation | async-start | bytes 5308416 | tf_op jit(solution)/shard_map/all_to_all | solution.py:914
  162.0 202.6 %all-gather.2.cloned.1.call-start = ((), (), s32[]{:S(2)}) async-start(), calls=%async_computation.4 | async-start | bytes 5849088 | tf_op jit(solution)/shard_map/all_gather | solution.py:913
  175.8 200.8 %copy-start.24 = (f32[256,128]{0,1:T(8,128)}, f32[256,128]{0,1:T(8,128)S(1)}, u32[]{:S(2)}) copy-start(f32[256,128]{0,1:T(8,128)S(1)} %copy.65) | copy-start | bytes 393220
  188.2 11.2 %collective-permute-start.1 = (bf16[128,1536]{1,0:T(8,128)(2,1)}, bf16[128,1536]{1,0:T(8,128)(2,1)S(1)}, u32[]{:S(2)}, u32[]{:S(2)}) collective-permute-start(bf16[128,1536]{1,0:T(8,128)(2,1)} %fusion.89), channel_id=1, source_target_pairs={{0,1},{1,0},{2,3},{3,2},{4,5},{5,4},{6,7},{7,6},{8,9},{9,8},{10,11... | collective-permute-start | bytes 1179656 | tf_op jit(solution)/shard_map/ppermute | solution.py:98
  190.8 10.6 %copy-start.72 = (f32[1536]{0:T(1024)}, f32[1536]{0:T(1024)S(1)}, u32[]{:S(2)}) copy-start(f32[1536]{0:T(1024)S(1)} %get-tuple-element.60) | copy-start | bytes 18436
  200.8 163.9 %copy-start.2 = (f32[128,1536]{1,0:T(8,128)}, f32[128,1536]{1,0:T(8,128)S(1)}, u32[]{:S(2)}) copy-start(f32[128,1536]{1,0:T(8,128)S(1)} %get-tuple-element.72) | copy-start | bytes 2359300
  201.3 99.8 %copy-start.96 = (f32[128]{0:T(128)}, f32[128]{0:T(128)S(1)}, u32[]{:S(2)}) copy-start(f32[128]{0:T(128)S(1)} %get-tuple-element.139) | copy-start | bytes 1540
  289.1 69.4 %collective-permute-start.2 = (bf16[4,96,3456]{2,1,0:T(8,128)(2,1)}, bf16[4,96,3456]{2,1,0:T(8,128)(2,1)S(1)}, u32[]{:S(2)}, u32[]{:S(2)}) collective-permute-start(bf16[4,96,3456]{2,1,0:T(8,128)(2,1)} %all-to-all-done), channel_id=1, source_target_pairs={{0,4},{4,0},{1,5},{5,1},{2,6},{6,2},{3,7},{7,3},{8,12},{12,8},{9,1... | collective-permute-start | bytes 7962632 | tf_op jit(solution)/shard_map/ppermute | solution.py:943
  290.7 10.5 %copy-start.86 = (pred[1152]{0:T(1024)(128)(4,1)S(1)}, pred[1152]{0:T(1024)(128)(4,1)}, u32[]{:S(2)}) copy-start(pred[1152]{0:T(1024)(128)(4,1)} %iota_compare_fusion.1) | copy-start | bytes 3460
  364.7 9.5 copy-start.98
  364.7 9.5 copy-start.103
  365.6 8.4 collective-permute-start.3
  366.1 78.9 %collective-permute-start.5 = (bf16[4,2,96,3456]{3,2,1,0:T(8,128)(2,1)}, bf16[4,2,96,3456]{3,2,1,0:T(8,128)(2,1)}, u32[]{:S(2)}, u32[]{:S(2)}) collective-permute-start(bf16[4,2,96,3456]{3,2,1,0:T(8,128)(2,1)} %maximum_select_fusion.1), channel_id=1, source_target_pairs={{0,2},{2,0},{1,3},{3,1},{4,6},{6,4},{5,7},{7,5},{8,10},{10,8},{9,1... | collective-permute-start | bytes 15925256 | tf_op jit(solution)/shard_map/ppermute | solution.py:953
  389.3 7.9 collective-permute-start.4
  453.7 9.8 copy-start.33
  453.7 9.8 copy-start.87
  484.2 8.9 copy-start.35
  503.0 110.7 %copy-start.47 = (bf16[128,1536]{1,0:T(8,128)(2,1)S(1)}, bf16[128,1536]{1,0:T(8,128)(2,1)}, u32[]{:S(2)}) copy-start(bf16[128,1536]{1,0:T(8,128)(2,1)} %gm_ref.1) | copy-start | bytes 1179652
  616.5 8.1 collective-permute-start.6
  617.6 14.5 %copy-start.74 = (f32[6,256]{1,0:T(8,128)}, f32[6,256]{1,0:T(8,128)S(1)}, u32[]{:S(2)}) copy-start(f32[6,256]{1,0:T(8,128)S(1)} %log_add_fusion.1) | copy-start | bytes 18436
  617.6 61.7 %all-to-all-start.1 = ((bf16[4,96,3456]{2,1,0:T(8,128)(2,1)}), bf16[4,96,3456]{2,1,0:T(8,128)(2,1)}, u32[]{:S(2)}, u32[]{:S(2)}) async-start(bf16[4,96,3456]{2,1,0:T(8,128)(2,1)} %get-tuple-element.44), calls=%async_computation.1 | async-start | bytes 5308416 | tf_op jit(solution)/shard_map/all_to_all | solution.py:991
  622.7 362.3 %reduce-scatter.2.cloned.1.call-start = ((), (), s32[]{:S(2)}) async-start(), calls=%async_computation.5 | async-start | bytes 5849088 | tf_op jit(solution)/shard_map/reduce_scatter | solution.py:1033
  645.3 8.0 collective-permute-start.7
  746.9 13.6 %slice-start = ((s8[9437184]{0:T(1024)(128)(4,1)}), s8[1048576]{0:T(1024)(128)(4,1)S(1)}, s32[]{:S(2)}) async-start(s8[9437184]{0:T(1024)(128)(4,1)} %bitcast.354), calls=%async_computation.6 | async-start | bytes 2097152
  751.6 8.8 copy-start.6
  751.6 8.8 slice-start.1
  751.6 8.9 slice-start.2
  751.6 8.9 copy-start.88
  751.6 8.9 copy-start.105
  751.6 28.2 %slice-start.3 = ((s8[7077888]{0:T(1024)(128)(4,1)}), s8[4194304]{0:T(1024)(128)(4,1)S(1)}, s32[]{:S(2)}) async-start(s8[7077888]{0:T(1024)(128)(4,1)} %bitcast.417), calls=%async_computation.9 | async-start | bytes 8388608
  760.5 19.3 %slice-start.4 = ((s8[7077888]{0:T(1024)(128)(4,1)}), s8[2883584]{0:T(1024)(128)(4,1)S(1)}, s32[]{:S(2)}) async-start(s8[7077888]{0:T(1024)(128)(4,1)} %bitcast.417), calls=%async_computation.10 | async-start | bytes 5767168
  767.7 12.2 %copy-start.106 = (bf16[1024,1152]{1,0:T(8,128)(2,1)S(1)}, bf16[1024,1152]{1,0:T(8,128)(2,1)}, u32[]{:S(2)}) copy-start(bf16[1024,1152]{1,0:T(8,128)(2,1)} %get-tuple-element.73) | copy-start | bytes 7077892
  767.7 12.2 %copy-start.107 = (bf16[1024,1152]{1,0:T(8,128)(2,1)S(1)}, bf16[1024,1152]{1,0:T(8,128)(2,1)}, u32[]{:S(2)}) copy-start(bf16[1024,1152]{1,0:T(8,128)(2,1)} %get-tuple-element.74) | copy-start | bytes 7077892
  854.6 115.3 %all-to-all-start.2 = ((bf16[4,96,3456]{2,1,0:T(8,128)(2,1)}), bf16[4,96,3456]{2,1,0:T(8,128)(2,1)}, u32[]{:S(2)}, u32[]{:S(2)}) async-start(bf16[4,96,3456]{2,1,0:T(8,128)(2,1)} %get-tuple-element.49), calls=%async_computation.3 | async-start | bytes 5308416 | tf_op jit(solution)/shard_map/all_to_all | solution.py:991
  860.7 12.3 %copy-start.3 = (f32[128,1536]{1,0:T(8,128)S(1)}, f32[128,1536]{1,0:T(8,128)}, u32[]{:S(2)}) copy-start(f32[128,1536]{1,0:T(8,128)} %copy-done.2) | copy-start | bytes 2359300
  860.7 12.3 %copy-start.38 = (f32[128,1536]{1,0:T(8,128)S(1)}, f32[128,1536]{1,0:T(8,128)}, u32[]{:S(2)}) copy-start(f32[128,1536]{1,0:T(8,128)} %get-tuple-element.46) | copy-start | bytes 2359300
  860.7 12.3 %copy-start.73 = (f32[1536]{0:T(1024)S(1)}, f32[1536]{0:T(1024)}, u32[]{:S(2)}) copy-start(f32[1536]{0:T(1024)} %copy-done.72) | copy-start | bytes 18436
  860.7 12.3 %copy-start.97 = (f32[128]{0:T(128)S(1)}, f32[128]{0:T(128)}, u32[]{:S(2)}) copy-start(f32[128]{0:T(128)} %copy-done.96) | copy-start | bytes 1540
  864.1 9.2 copy-start.99
  874.4 10.6 %collective-permute-start.8 = (bf16[128,1536]{1,0:T(8,128)(2,1)S(1)}, bf16[128,1536]{1,0:T(8,128)(2,1)S(1)}, u32[]{:S(2)}, u32[]{:S(2)}) collective-permute-start(bf16[128,1536]{1,0:T(8,128)(2,1)S(1)} %get-tuple-element.63), channel_id=1, source_target_pairs={{0,1},{1,0},{2,3},{3,2},{4,5},{5,4},{6,7},{7,6},{8,9},{9,8},{10,11... | collective-permute-start | bytes 1179656 | tf_op jit(solution)/shard_map/ppermute | solution.py:91
  898.0 13.9 %collective-permute-start.9 = (bf16[128,1536]{1,0:T(8,128)(2,1)}, bf16[128,1536]{1,0:T(8,128)(2,1)S(1)}, u32[]{:S(2)}, u32[]{:S(2)}) collective-permute-start(bf16[128,1536]{1,0:T(8,128)(2,1)} %fusion.92), channel_id=1, source_target_pairs={{0,1},{1,0},{2,3},{3,2},{4,5},{5,4},{6,7},{7,6},{8,9},{9,8},{10,11... | collective-permute-start | bytes 1179656 | tf_op jit(solution)/shard_map/ppermute | solution.py:98
  912.9 55.8 %copy-start.37 = (f32[128,1536]{1,0:T(8,128)S(1)}, f32[128,1536]{1,0:T(8,128)}, u32[]{:S(2)}) copy-start(f32[128,1536]{1,0:T(8,128)} %get-tuple-element.64) | copy-start | bytes 2359300
  912.9 55.8 %copy-start.102 = (f32[128]{0:T(128)S(1)}, f32[128]{0:T(128)}, u32[]{:S(2)}) copy-start(f32[128]{0:T(128)} %get-tuple-element.136) | copy-start | bytes 1540
  (80 other events, 317.8 us)
Sparse Core Ops, SparseCore 0:
  165.7 98.0 all-gather.1
  651.2 88.9 reduce-scatter.1

commit v3 on v2

--- a/solution.py
+++ b/solution.py
@@ -143,7 +143,7 @@
         self.z = lax.axis_index("z")
         self.mine = [lax.axis_index(bit) for bit in bits]
         self.own = slot_of(self.z, self.mine)
-        self.pending = []
+        self.pending, self.settled = [], False
 
     def copy(self, slot, first, axis, target, send_sem):
         return pltpu.make_async_remote_copy(
@@ -224,8 +224,13 @@
             self.on_bits(number - 1)
         self.on_bits(self.size - 1)
 
+    def settle(self):
+        if not self.settled:
+            pltpu.make_async_copy(self.x_ref, self.out_ref.at[self.own], self.own_sem).wait()
+            self.settled = True
+
     def end(self):
-        pltpu.make_async_copy(self.x_ref, self.out_ref.at[self.own], self.own_sem).wait()
+        self.settle()
         for condition, make in self.pending:
             guarded(condition, lambda make=make: make().wait_send())
 
@@ -380,84 +385,6 @@
             self.own_copy(piece).wait()
         for make in self.pending:
             make().wait_send()
-
-
-def weights_kernel(
-    size, bits, block, half, at_ref, gu_ref, dn_ref, gm_ref, at_out, gu_out, dn_out, gm_out, *sems
-):
-    z = lax.axis_index("z")
-    mine = [lax.axis_index(bit) for bit in bits]
-    others = [lax.rem(z + o, size) for o in range(1, size)]
-    greet(
-        [("z", other) for other in others]
-        + [(bit, 1 - m) for bit, m in zip(bits, mine)]
-        + [("t", 1 - lax.axis_index("t"))],
-        [None] * (size + len(bits)),
-    )
-    rows = Gather(size, ("t",), gm_ref, gm_out, *sems[8:])
-    attention = Gather(size, bits, at_ref, at_out, *sems[:4])
-    feed = Exchange(size, bits, block, half, gu_ref, dn_ref, gu_out, dn_out, sems[4:8])
-    attention.begin()
-    rows.begin()
-    feed.begin()
-    attention.step(1)
-    rows.step(1)
-    attention.step(2)
-    attention.on_bits(0)
-    rows.on_bits(0)
-    rows.step(2)
-    feed.send(1)
-    attention.step(3)
-    attention.on_bits(1)
-    rows.on_bits(1)
-    rows.step(3)
-    feed.on_bits(0)
-    attention.on_bits(2)
-    feed.sent(1)
-    feed.send(3)
-    feed.step(1)
-    attention.on_bits(3)
-    rows.on_bits(2)
-    feed.sent(3)
-    feed.send(2)
-    feed.step(3)
-    feed.on_bits(1)
-    rows.on_bits(3)
-    feed.sent(2)
-    feed.step(2)
-    feed.on_bits(3)
-    feed.on_bits(2)
-    attention.end()
-    feed.end()
-    rows.end()
-
-
-def weights(at, gu, dn, gm, size, bits, block, collective_id):
-    slots = size * 2 ** len(bits)
-    rows, half = dn.shape
-    return pl.pallas_call(
-        functools.partial(weights_kernel, size, bits, block, half),
-        out_shape=(
-            jax.ShapeDtypeStruct((slots, *at.shape), at.dtype),
-            jax.ShapeDtypeStruct((slots, rows, 2 * block), gu.dtype),
-            jax.ShapeDtypeStruct((slots, rows, block), dn.dtype),
-            jax.ShapeDtypeStruct((2 * size, *gm.shape), gm.dtype),
-        ),
-        in_specs=[pl.BlockSpec(memory_space=pl.ANY)] * 4,
-        out_specs=[pl.BlockSpec(memory_space=pl.ANY)] * 4,
-        scratch_shapes=[
-            *gather_semaphores(size, bits),
-            pltpu.SemaphoreType.DMA((3,)),
-            pltpu.SemaphoreType.DMA((size - 1, 3)),
-            pltpu.SemaphoreType.DMA((size, 2 ** len(bits), len(bits), 3)),
-            pltpu.SemaphoreType.DMA((slots, 3)),
-            *gather_semaphores(size, ("t",)),
-        ],
-        compiler_params=pltpu.CompilerParams(collective_id=collective_id, has_side_effects=True),
-        cost_estimate=pl.CostEstimate(
-            flops=0, transcendentals=0, bytes_accessed=slots * gu.size * 27
-        ),
-    )(at, gu, dn, gm)
 
 
 class Fold:
@@ -681,29 +608,6 @@
 
 def at_microseconds(time):
     return pl.CostEstimate(flops=0, transcendentals=0, bytes_accessed=time * 3500000)
-
-
-def scatter_kernel(size, bits, p_ref, out_ref, *refs):
-    greet_all(size, bits)
-    steps = Scatter(size, bits, p_ref, out_ref, *refs)
-    steps.begin()
-    for place in range(size):
-        steps.place(place)
-    steps.finish()
-    steps.end()
-
-
-def scatter(partial, size, bits, collective_id):
-    slots, rows, columns = partial.shape
-    return pl.pallas_call(
-        functools.partial(scatter_kernel, size, bits),
-        out_shape=jax.ShapeDtypeStruct((rows, columns), F32),
-        in_specs=[pl.BlockSpec(memory_space=pl.ANY)],
-        out_specs=pl.BlockSpec(memory_space=pltpu.VMEM),
-        scratch_shapes=scatter_scratch(size, bits, rows, columns),
-        compiler_params=comm_params(collective_id),
-        cost_estimate=at_microseconds(48),
-    )(partial)
 
 
 def last_kernel(size, bits, p_ref, x_ref, out_ref, sum_ref, *refs):
@@ -824,6 +728,277 @@
     return out[:branches], out[branches]
 
 
+class Attend:
+    def __init__(self, rows_ref, gain_ref, bias_ref, cos_ref, sin_ref, mask_ref, w_ref, outs, scratch, width, epsilon=1e-06):
+        self.gain_ref, self.bias_ref, self.w_ref = gain_ref, bias_ref, w_ref
+        self.cos_ref, self.sin_ref, self.mask_ref = cos_ref, sin_ref, mask_ref
+        self.state_ref, self.middle_ref, self.xa_ref, self.q_ref, self.k_ref, self.v_ref, self.lse_ref, self.o_ref = outs
+        self.send_buf, self.land_buf, self.send_sems, self.recv_sems = scratch
+        self.rows_ref = rows_ref
+        self.t = lax.axis_index("t")
+        self.slots, self.few = w_ref.shape[0], w_ref.shape[1]
+        self.model = self.slots * self.few
+        self.count = rows_ref.shape[0]
+        self.q_width = self.q_ref.shape[1]
+        self.width = width
+        self.epsilon = epsilon
+
+    def normed(self, rows, gain_ref):
+        factor = lax.rsqrt(jnp.mean(rows * rows, axis=-1, keepdims=True) + self.epsilon)
+        return (rows * factor * gain_ref[...]).astype(LOW)
+
+    def xa_copy(self):
+        return pltpu.make_async_remote_copy(
+            src_ref=self.xa_ref.at[self.t],
+            dst_ref=self.xa_ref.at[self.t],
+            send_sem=self.send_sems.at[0],
+            recv_sem=self.recv_sems.at[0],
+            device_id={"t": 1 - self.t},
+            device_id_type=MESH,
+        )
+
+    def xa_landing(self):
+        return pltpu.make_async_remote_copy(
+            src_ref=self.xa_ref.at[1 - self.t],
+            dst_ref=self.xa_ref.at[1 - self.t],
+            send_sem=self.send_sems.at[0],
+            recv_sem=self.recv_sems.at[0],
+            device_id={"t": 1 - self.t},
+            device_id_type=MESH,
+        )
+
+    def half_copy(self):
+        return pltpu.make_async_remote_copy(
+            src_ref=self.send_buf,
+            dst_ref=self.land_buf,
+            send_sem=self.send_sems.at[1],
+            recv_sem=self.recv_sems.at[1],
+            device_id={"t": 1 - self.t},
+            device_id_type=MESH,
+        )
+
+    def begin(self, state):
+        self.state_ref[...] = state
+        self.xa_ref[self.t] = self.normed(state, self.gain_ref)
+        self.xa_copy().start()
+
+    def columns(self, low, count):
+        weight = self.w_ref[:, :, low : low + count].reshape(self.model, count)
+        xa = self.xa_ref[...].reshape(2 * self.count, self.model)
+        return jnp.dot(xa, weight, preferred_element_type=F32) + self.bias_ref[:, low : low + count]
+
+    def rope(self, values):
+        return (values * self.cos_ref[...] + pltpu.roll(values, HD // 2, 1) * self.sin_ref[...]).astype(LOW)
+
+    def keys(self):
+        self.xa_landing().wait_recv()
+        both_kv = self.columns(self.q_width, 2 * HD)
+        self.k_ref[...] = self.rope(both_kv[:, :HD])
+        self.v_ref[...] = both_kv[:, HD:].astype(LOW)
+
+    def heads(self, first):
+        lin = self.columns(first * HD, 2 * HD)
+        for number in range(2):
+            head = first + number
+            low = head * HD
+            query = self.rope(lin[:, number * HD : (number + 1) * HD])
+            self.q_ref[:, low : low + HD] = query
+            raw = lax.dot_general(
+                query, self.k_ref[...], (((1,), (1,)), ((), ())), preferred_element_type=F32
+            )
+            scores = jnp.where(self.mask_ref[...] > 0, raw * (1.0 / math.sqrt(HD)), -1e30)
+            top = jnp.max(scores, axis=-1, keepdims=True)
+            expo = jnp.exp(scores - top)
+            whole = jnp.sum(expo, axis=-1, keepdims=True)
+            probs = (expo / whole).astype(LOW)
+            self.lse_ref[head] = top + jnp.log(whole)
+            out = jnp.dot(probs, self.v_ref[...], preferred_element_type=F32).astype(LOW)
+            self.o_ref[0, :, low : low + HD] = out[: self.count]
+            self.o_ref[1, :, low : low + HD] = out[self.count :]
+
+    def projected(self, half, step):
+        left = self.o_ref[half]
+        for low in range(0, self.slots, step):
+            weight = self.w_ref[low : low + step, :, self.width :].reshape(step * self.few, self.q_width)
+            yield low * self.few, lax.dot_general(
+                left, weight, (((1,), (1,)), ((), ())), preferred_element_type=F32
+            )
+
+    def other_half(self):
+        for low, part in self.projected(1 - self.t, self.slots // 4):
+            self.send_buf[:, low : low + part.shape[1]] = part.astype(LOW)
+        self.half_copy().start()
+
+    def own_half(self):
+        for low, part in self.projected(self.t, self.slots // 4):
+            where = slice(low, low + part.shape[1])
+            self.middle_ref[:, where] = self.state_ref[:, where] + part
+
+    def finish(self, gain_ref, xf_ref):
+        self.half_copy().wait_recv()
+        middle = self.middle_ref[...] + self.land_buf[...].astype(F32)
+        self.middle_ref[...] = middle
+        xf_ref[...] = self.normed(middle, gain_ref)
+
+    def end(self):
+        self.xa_copy().wait_send()
+        self.half_copy().wait_send()
+
+
+def front_kernel(size, bits, block, half, layer, width, *refs):
+    first = layer == 0
+    inputs, outs, refs = in_groups(refs, [11, 13 if first else 12, len(refs)])
+    (x_ref, more_ref, ga_ref, gf_ref, bias_ref, cos_ref, sin_ref, mask_ref, at_ref, gu_ref, dn_ref) = inputs
+    xf_out, gu_out, dn_out, at_out = outs[8:12]
+    (w_ref, xf_ref, at_sem), pair, at_sems, feed_sems, rows_sems, rest = in_groups(
+        refs, [3, 4, 4, 4, 4, len(refs)]
+    )
+    greet_all(size, ("t", *bits))
+    work = Attend(
+        x_ref, ga_ref, bias_ref, cos_ref, sin_ref, mask_ref, w_ref, outs[:8], pair, width
+    )
+    attention = Gather(size, bits, at_ref, w_ref, *at_sems)
+    feed = Exchange(
+        size, bits, block, half, gu_ref.at[layer], dn_ref.at[layer], gu_out, dn_out, feed_sems
+    )
+    rows = Gather(size, ("t",), xf_ref, xf_out, *rows_sems)
+    kept = pltpu.make_async_copy(w_ref, at_out, at_sem)
+    if first:
+        side = Gather(size, ("t",), more_ref, outs[12], *rest)
+        attention.begin()
+        side.begin()
+        feed.begin()
+        work.begin(x_ref[...].astype(F32))
+        attention.step(1)
+        side.step(1)
+        attention.step(2)
+        attention.on_bits(0)
+        side.on_bits(0)
+        side.step(2)
+        feed.send(1)
+        attention.step(3)
+        attention.on_bits(1)
+        side.on_bits(1)
+        side.step(3)
+        feed.on_bits(0)
+        attention.on_bits(2)
+        feed.sent(1)
+        feed.send(3)
+        feed.step(1)
+        attention.on_bits(3)
+        attention.settle()
+        work.keys()
+        work.heads(0)
+        side.on_bits(2)
+        side.on_bits(3)
+    else:
+        total_ref, *rest = rest
+        side = Scatter(size, ("t",), more_ref, total_ref, *rest)
+        attention.begin()
+        side.begin()
+        feed.begin()
+        side.place(0)
+        attention.step(1)
+        side.place(1)
+        attention.step(2)
+        attention.on_bits(0)
+        side.place(2)
+        attention.step(3)
+        attention.on_bits(1)
+        side.place(3)
+        feed.send(1)
+        attention.on_bits(2)
+        attention.on_bits(3)
+        attention.settle()
+        side.finish()
+        work.begin(x_ref[...] + total_ref[...])
+        feed.on_bits(0)
+        feed.sent(1)
+        feed.send(3)
+        feed.step(1)
+        work.keys()
+        work.heads(0)
+    kept.start()
+    feed.sent(3)
+    feed.send(2)
+    feed.step(3)
+    feed.on_bits(1)
+    work.heads(2)
+    work.heads(4)
+    work.other_half()
+    work.own_half()
+    work.finish(gf_ref, xf_ref)
+    rows.begin()
+    rows.step(1)
+    rows.on_bits(0)
+    rows.step(2)
+    feed.sent(2)
+    feed.step(2)
+    rows.on_bits(1)
+    feed.on_bits(3)
+    rows.step(3)
+    rows.on_bits(2)
+    feed.on_bits(2)
+    rows.on_bits(3)
+    kept.wait()
+    for steps in (attention, side, feed, work, rows):
+        steps.end()
+
+
+def front(x, more, gains, bias, tables, at, gu, dn, layer, size, bits, block, width, collective_id):
+    slots = size * 2 ** len(bits)
+    count, model = x.shape
+    few, half = dn.shape[1:]
+    length = 2 * count
+    q_width = at.shape[1] - width
+    first = layer == 0
+    held, far = pl.BlockSpec(memory_space=pltpu.VMEM), pl.BlockSpec(memory_space=pl.ANY)
+    shape = jax.ShapeDtypeStruct
+    more_scratch = (
+        gather_semaphores(size, ("t",))
+        if first
+        else [pltpu.VMEM((count, model), F32), *scatter_scratch(size, ("t",), count, model)]
+    )
+    return pl.pallas_call(
+        functools.partial(front_kernel, size, bits, block, half, layer, width),
+        out_shape=(
+            shape((count, model), F32),
+            shape((count, model), F32),
+            shape((2, count, model), LOW),
+            shape((length, q_width), LOW),
+            shape((length, HD), LOW),
+            shape((length, HD), LOW),
+            shape((q_width // HD, length, 1), F32),
+            shape((2, count, q_width), LOW),
+            shape((2 * size, count, model), LOW),
+            shape((slots, few, 2 * block), LOW),
+            shape((slots, few, block), LOW),
+            shape((slots, few, at.shape[1]), LOW),
+            *([shape((2 * size, count, model), LOW)] if first else []),
+        ),
+        in_specs=[held, far] + [held] * 6 + [far] * 3,
+        out_specs=[held] * 8 + [far] * (5 if first else 4),
+        scratch_shapes=[
+            pltpu.VMEM((slots, few, at.shape[1]), LOW),
+            pltpu.VMEM((count, model), LOW),
+            pltpu.SemaphoreType.DMA,
+            pltpu.VMEM((count, model), LOW),
+            pltpu.VMEM((count, model), LOW),
+            pltpu.SemaphoreType.DMA((2,)),
+            pltpu.SemaphoreType.DMA((2,)),
+            *gather_semaphores(size, bits),
+            pltpu.SemaphoreType.DMA((3,)),
+            pltpu.SemaphoreType.DMA((size - 1, 3)),
+            pltpu.SemaphoreType.DMA((size, 2 ** len(bits), len(bits), 3)),
+            pltpu.SemaphoreType.DMA((slots, 3)),
+            *gather_semaphores(size, ("t",)),
+            *more_scratch,
+        ],
+        compiler_params=comm_params(collective_id),
+        cost_estimate=at_microseconds(150),
+    )(x, more, *gains, bias, *tables, at, gu, dn)
+
+
 def spread_group(rows):
     return gather(rows, LINE, ("t",), 1).reshape(-1, rows.shape[1])
 
@@ -832,10 +1007,6 @@
     return partial.reshape(slots, -1, partial.shape[1])
 
 
-def sum_group(partial):
-    return scatter(in_slots(partial, 2 * LINE), LINE, ("t",), 2)
-
-
 def block_width(half):
     return -(-half // (LINE * LANES)) * LANES
 
@@ -846,16 +1017,6 @@
 
 def tie(value, *others):
     return lax.optimization_barrier((value, *others))
-
-
-def column_sections(gu, dn, block):
-    half = dn.shape[1]
-    sections = []
-    for line in range(LINE):
-        low = block_start(line, block, half)
-        parts = [gu[:, low : low + block], gu[:, half + low : half + low + block], dn[:, low : low + block]]
-        sections.append(jnp.concatenate(parts, axis=1))
-    return jnp.stack(sections)
 
 
 def from_blocks(blocks, parts, half):
@@ -887,89 +1048,53 @@
     scale = 1.0 / math.sqrt(HD)
     positions, allowed = doc_layout(doc_lengths[0], length)
     cosine, sine = rope_tables(positions, HD)
+    turned = jnp.where(jnp.arange(HD) < HD // 2, -sine, sine)
+    tables = (cosine, turned, allowed.astype(F32))
     cos_q = cosine[:, None, None, :]
     sin_q = sine[:, None, None, :]
     cos_k = cosine[:, None, :]
     sin_k = sine[:, None, :]
     gain_attn = norm_attn.astype(F32)
     gain_ffn = norm_ffn.astype(F32)
-    flats = [jnp.concatenate([w_qkv[layer], w_out[layer]], axis=1) for layer in range(layers)]
-    both_w, gu_w, down_w, gm_all = weights(
-        flats[0], w_gateup[0], w_down[0], cotangent, LINE, bits, block, 3
-    )
-    attn_weights = [both_w.reshape(-1, flats[0].shape[1])]
-    ffn_weights = [(gu_w.reshape(-1, 2 * block), down_w.reshape(-1, block))]
-    gm_all = gm_all.reshape(-1, cotangent.shape[1])
+    bias_all = b_qkv.astype(F32)
     line = lax.axis_index("z")
     valid = jnp.arange(block) >= line * block - jnp.minimum(line * block, half - block)
     saved = []
-    state = tokens.astype(F32)
     for layer in range(layers):
-        both_w = attn_weights[layer]
-        ahead = layer + 1 < layers
-        if ahead:
-            flat, sections = flats[layer + 1], column_sections(w_gateup[layer + 1], w_down[layer + 1], block)
-            both_w, flat, sections = tie(both_w, flat, sections)
-            coming = lax.all_gather(flat, dp, axis=0, tiled=True)
-            sections = lax.all_to_all(sections, "z", 0, 0, tiled=True)
-        attn_weights[layer] = both_w
-        qkv_w, out_w = both_w[:, :qkv_width], both_w[:, qkv_width:]
-        factor_a = rms_factor(state)
-        xa_all = spread_pair((state * factor_a * gain_attn[layer]).astype(LOW))
-        lin = jnp.dot(xa_all, qkv_w, preferred_element_type=F32) + b_qkv[layer].astype(F32)
-        query = lin[:, :q_width].reshape(length, kv_local, groups, HD)
-        key = lin[:, q_width : q_width + kv_width].reshape(length, kv_local, HD)
-        value = lin[:, q_width + kv_width :].reshape(length, kv_local, HD).astype(LOW)
-        query = (query * cos_q + rotate(query) * sin_q).astype(LOW)
-        key = (key * cos_k + rotate(key) * sin_k).astype(LOW)
-        raw = jnp.einsum("qkgd,pkd->kgqp", query, key, preferred_element_type=F32)
-        scores = jnp.where(allowed, raw * scale, -1e30)
-        top = jnp.max(scores, axis=-1, keepdims=True)
-        expo = jnp.exp(scores - top)
-        total = jnp.sum(expo, axis=-1, keepdims=True)
-        probs = expo / total
-        log_total = top + jnp.log(total)
-        attended = (
-            jnp.einsum("kgqp,pkd->qkgd", probs.astype(LOW), value, preferred_element_type=F32)
-            .reshape(length, q_width)
-            .astype(LOW)
-        )
-        middle = state + sum_pair(contract_last(attended, out_w))
-        gu_w, down_w = ffn_weights[layer]
-        factor_f = rms_factor(middle)
-        xf_all = spread_group((middle * factor_f * gain_ffn[layer]).astype(LOW))
-        if ahead:
-            xf_all, sections = tie(xf_all, sections)
-            sections = join_pair(sections, lax.ppermute(sections, bits[0], SWAP), bits[0], 1)
+        flat = jnp.concatenate([w_qkv[layer], w_out[layer]], axis=1)
+        start, more = (tokens, cotangent) if layer == 0 else (middle, in_slots(partial, 2 * LINE))
+        gains = (gain_attn[layer : layer + 1], gain_ffn[layer : layer + 1])
+        out = front(
+            start, more, gains, bias_all[layer : layer + 1], tables, flat, w_gateup, w_down,
+            layer, LINE, bits, block, qkv_width, 8 + layer,
+        )
+        if layer == 0:
+            gm_all = out[12].reshape(-1, cotangent.shape[1])
+        (state, middle, xa_all, query, key, value, log_total, attended) = out[:8]
+        xf_all, gu_w, down_w, both_w = (item.reshape(-1, item.shape[2]) for item in out[8:12])
+        xa_all = xa_all.reshape(length, -1)
+        attended = attended.reshape(length, -1)
+        query = query.reshape(length, kv_local, groups, HD)
+        key = key.reshape(length, kv_local, HD)
+        value = value.reshape(length, kv_local, HD)
+        log_total = log_total[None]
         gate_up = jnp.dot(xf_all, gu_w, preferred_element_type=F32)
         gate = gate_up[:, :block]
         up = gate_up[:, block:]
         act = jnp.where(valid, jax.nn.silu(gate) * up, 0.0).astype(LOW)
         partial = contract_last(act, down_w, LOW)
-        if ahead:
-            branch = sum_group(partial)
-            branch, sections, coming = tie(branch, sections, coming)
-            for number, bit in enumerate(bits[1:]):
-                sections = join_pair(sections, lax.ppermute(sections, bit, SWAP), bit, 2 + number)
-            sections = sections.reshape(-1, 3 * block)
-            ffn_weights.append((sections[:, : 2 * block], sections[:, 2 * block :]))
-            attn_weights.append(coming)
-            after = middle + branch
         saved.append(
-            (state, factor_a, xa_all, query, key, value, log_total, attended)
-            + (middle, factor_f, xf_all, gate, up, act)
-        )
-        if ahead:
-            state = after
+            (state, xa_all, query, key, value, log_total, attended)
+            + (middle, xf_all, gate, up, act, gu_w, down_w, both_w)
+        )
     grad = cotangent.astype(F32)
     grads_attn, grads_bias, grads_ga, grads_gf = ([] for _ in range(4))
     waiting, branches = None, [in_slots(partial, 2 * LINE)]
     grads_blocks = []
     for layer in reversed(range(layers)):
-        (state_in, factor_a, xa_all, query, key, value, log_total, attended) = saved[layer][:8]
-        (middle, factor_f, xf_all, gate, up, act) = saved[layer][8:]
-        gu_w, down_w = ffn_weights[layer]
-        both_w = attn_weights[layer]
+        (state_in, xa_all, query, key, value, log_total, attended) = saved[layer][:7]
+        (middle, xf_all, gate, up, act, gu_w, down_w, both_w) = saved[layer][7:]
+        factor_a, factor_f = rms_factor(state_in), rms_factor(middle)
         qkv_w, out_w = both_w[:, :qkv_width], both_w[:, qkv_width:]
         if waiting is not None:
             gm_all = spread_group(grad.astype(LOW))

time: 1010 us -> 948 us (0.939)
  waiting for transfers between devices: 51.8 us -> 17.2 us
  other arithmetic: 73.7 us -> 50.6 us
  Pallas kernels: 604 us -> 621 us
  matrix products: 138 us -> 127 us
    pallas_call x2, Pallas kernels: 182 us -> 333 us  [front(): pl.pallas_call(functools.partial(front_kernel, size, bits, block, half, l...]
    pallas_call x3 -> x1, Pallas kernels: 195 us -> 58.7 us  [gather(): pl.pallas_call(functools.partial(gather_kernel, size, bits), out_shape=ja...]
    select_n x6 -> x2, other arithmetic: 16.6 us -> 1.37 us  [join_pair(): jnp.where(index == 0, jnp.stack([own, other], axis=axis), jnp.stack([othe...]
    all_to_all x2, waiting for transfers between devices: 23.7 us -> 10.1 us  [local(): waiting = lax.all_to_all(folded, 'z', 0, 0, tiled=True)]
    ppermute x4 -> x2, waiting for transfers between devices: 11.4 us -> 0.66 us  [sum_pair(): other = lax.ppermute(take(halves, 1 - index, 0).astype(LOW), 't', SWAP)]
    convert_element_type x8 -> x0, other arithmetic: 10.5 us -> none  [the longest x2 3.74 us: local(): query = (query * cos_q + rotate(query) * sin_q).astype(LOW)]
    unnamed x238 -> x184, local copies, waits for them, and re-layouts: 29.4 us -> 24.4 us
    dot_general x8 -> x6, matrix products: 40.5 us -> 35.5 us  [contract_last(): lax.dot_general(left, right, (((1,), (1,)), ((), ())), preferred_element_...]
  transfers between devices with their start and end apart: 15 -> 7, of which waited for: 7 -> 3; matrix products, arithmetic and copies ran while one was open for 21% -> 17% of each run, Pallas kernels for 50% -> 19%
where the time goes in v3:
time: 948 us; the launch traced here: 938 us
  Pallas kernels  621 us (66%)
  matrix products  127 us (13%)
  local copies, waits for them, and re-layouts  86.6 us (9%)
  other arithmetic  50.6 us (5%)
  between operations  18.2 us (2%)
  starting transfers between devices  17.7 us (2%)
  waiting for transfers between devices  17.2 us (2%)
    pallas_call x2, Pallas kernels, front(): pl.pallas_call(functools.partial(front_kernel, size, bits, block, half, l...  333 us
    pallas_call x2, Pallas kernels, back(): pl.pallas_call(functools.partial(back_kernel, size, bits, branches), out_...  177 us
    pallas_call x1, Pallas kernels, gather(): pl.pallas_call(functools.partial(gather_kernel, size, bits), out_shape=ja...  58.7 us
    pallas_call x1, Pallas kernels, last(): pl.pallas_call(functools.partial(last_kernel, size, bits), out_shape=(jax...  52.4 us
    dot_general x8, matrix products, contract_first(): lax.dot_general(left, right, (((0,), (0,)), ((), ())), preferred_element_...  39 us
    dot_general x6, matrix products, contract_last(): lax.dot_general(left, right, (((1,), (1,)), ((), ())), preferred_element_...  35.5 us
    unnamed x184, local copies, waits for them, and re-layouts  24.4 us
    dot_general x2, matrix products, local(): gate_up = jnp.dot(xf_all, gu_w, preferred_element_type=F32)  23.1 us
  transfers between devices with their start and end apart: 7, of which 3 were waited for; matrix products, arithmetic and copies ran while one was open for 17% of the time, Pallas kernels for 19%

profile of v3, /device:TPU:26, one launch (start us, length us, event | category | flops | bytes accessed | tf_op | source)
XLA Modules:
  0.0 938.1 jit_solution(9792993684464428109)
XLA Ops:
  11.2 2.6 convert_add_fusion
  23.7 158.5 %shard_map.169 = (f32[128,1536]{1,0:T(8,128)}, f32[128,1536]{1,0:T(8,128)}, bf16[2,128,1536]{2,1,0:T(8,128)(2,1)}, bf16[256,768]{1,0:T(8,128)(2,1)}, bf16[256,12...) custom-call(bf16[128,1536]{1,0:T(8,128)(2,1)} %refs_0_.1, ...), custom_call_target="tpu_custom_call" | custom-call | bytes 525000000 | tf_op jit(solution)/shard_map/pallas_call | solution.py:962
  182.3 5.0 copy.52
  187.2 9.5 %fusion.94 = f32[1024,2304]{1,0:T(8,128)S(1)} fusion(bf16[1024,1536]{1,0:T(8,128)(2,1)S(1)} %bitcast.297, bf16[1536,2304]{1,0:T(8,128)(2,1)} %bitcast.322), kind=kOutput, calls=%fused_computation.217 | convolution fusion | flops 7247757312 | bytes 19660800 | tf_op jit(solution)/shard_map/dot_general | solution.py:1081
  198.4 2.8 copy-done.2
  201.4 5.6 fusion.95.refs_1_
  207.0 174.7 %shard_map.170 = (f32[128,1536]{1,0:T(8,128)}, f32[128,1536]{1,0:T(8,128)}, bf16[2,128,1536]{2,1,0:T(8,128)(2,1)}, bf16[256,768]{1,0:T(8,128)(2,1)}, bf16[256,12...) custom-call(f32[128,1536]{1,0:T(8,128)} %get-tuple-element.43.refs_0, ...), custom_call_target="tpu_custom_call" | custom-call | bytes 525000000 | tf_op jit(solution)/shard_map/pallas_call | solution.py:962
  381.8 4.7 copy.51
  387.2 13.6 %fusion.96 = f32[1024,2304]{1,0:T(8,128)} fusion(bf16[1024,1536]{1,0:T(8,128)(2,1)} %bitcast.303, bf16[1536,2304]{1,0:T(8,128)(2,1)} %bitcast.326), kind=kOutput, calls=%fused_computation.219 | convolution fusion | flops 7247757312 | bytes 19660800 | tf_op jit(solution)/shard_map/dot_general | solution.py:1081
  400.9 8.8 select_convert_fusion.4
  409.6 5.7 fusion.24.refs_3_
  415.3 5.6 fusion.97.refs_1_
  421.0 9.6 %fusion.4.refs_2_ = bf16[16,96,2304]{2,1,0:T(8,128)(2,1)} fusion(bf16[16,96,1024]{2,1,0:T(8,128)(2,1)S(1)} %bitcast.304, bf16[1024,1152]{1,0:T(8,128)(2,1)S(1)} %get-tuple-element.96, bf16[1024,1152]{1,0:T(8,128)(2,1)S(1)} %get-tuple-element.95), kind=kOutput, calls=%fused_computation.7 | convolution fusion | flops 7257194496 | bytes 14942208 | tf_op jit(solution)/shard_map/dot_general | solution.py:66
  430.6 9.3 fusion.refs_0_
  439.9 112.2 %shard_map.171 = (f32[128,1536]{1,0:T(8,128)}, f32[128,1536]{1,0:T(8,128)}, bf16[4,96,3456]{2,1,0:T(8,128)(2,1)}) custom-call(bf16[8,128,1536]{2,1,0:T(8,128)(2,1)} %fusion.refs_0_, bf16[8,128,1536]{2,1,0:T(8,128)(2,1)} %fusion.97.refs_1_, bf16[16,96,2304]{2,1,0:T(8,128)(2,1)} %fusion.4.refs_2_, bf16[16,96,1152]{2,1,0:T(8,128)(2,1)} %fusion.24.refs_3_), custom_call_target="tpu_custom_call" | custom-call | bytes 280000000 | tf_op jit(solution)/shard_map/pallas_call | solution.py:709
  553.4 2.7 fusion.80
  556.2 5.2 all-to-all-start
  566.8 4.9 copy.66
  572.8 2.0 reduce.3
  579.2 2.4 fusion.38
  592.6 3.0 fusion.16
  596.5 2.0 collective-permute-start.1
  600.4 2.9 pad_maximum_fusion.1
  603.3 1.9 fusion.53
  609.3 10.1 %all-to-all-done = bf16[4,96,3456]{2,1,0:T(8,128)(2,1)} async-done(((bf16[4,96,3456]{2,1,0:T(8,128)(2,1)}), bf16[4,96,3456]{2,1,0:T(8,128)(2,1)}, u32[]{:S(2)}, u32[]{:S(2)}) %all-to-all-start) | async-done | bytes 2654240 | tf_op jit(solution)/shard_map/all_to_all | solution.py:1116
  620.2 58.7 %shard_map.172 = bf16[8,128,1536]{2,1,0:T(8,128)(2,1)} custom-call(bf16[128,1536]{1,0:T(8,128)(2,1)} %convert_element_type.184.refs_0_), custom_call_target="tpu_custom_call" | custom-call | bytes 157286400 | tf_op jit(solution)/shard_map/pallas_call | solution.py:263
  679.0 5.0 copy.67
  684.0 8.8 fusion.22.refs_2_
  692.9 6.8 select_convert_fusion.1
  699.8 11.2 %fusion.11.refs_1_ = bf16[16,96,2304]{2,1,0:T(8,128)(2,1)} fusion(bf16[16,96,1024]{2,1,0:T(8,128)(2,1)S(1)} %bitcast.298, bf16[1024,1152]{1,0:T(8,128)(2,1)} %get-tuple-element.94, bf16[1024,1152]{1,0:T(8,128)(2,1)S(1)} %get-tuple-element.93), kind=kOutput, calls=%fused_computation.15 | convolution fusion | flops 7257194496 | bytes 14942208 | tf_op jit(solution)/shard_map/dot_general | solution.py:66
  710.9 8.9 fusion.7.refs_0_
  719.8 64.8 %shard_map.173 = (f32[128,1536]{1,0:T(8,128)}, bf16[4,96,3456]{2,1,0:T(8,128)(2,1)}) custom-call(bf16[8,128,1536]{2,1,0:T(8,128)(2,1)} %fusion.7.refs_0_, bf16[16,96,2304]{2,1,0:T(8,128)(2,1)} %fusion.11.refs_1_, bf16[16,96,1152]{2,1,0:T(8,128)(2,1)} %fusion.22.refs_2_), custom_call_target="tpu_custom_call" | custom-call | bytes 280000000 | tf_op jit(solution)/shard_map/pallas_call | solution.py:709
  784.6 6.6 all-to-all-start.1
  791.3 1.8 slice_dynamic-update-slice_fusion.11
  794.7 1.7 slice_dynamic-update-slice_fusion.9
  801.4 2.2 fusion.83
  805.0 2.1 collective-permute-start.2
  807.7 1.8 fusion.84
  809.5 6.4 collective-permute-done.2
  817.0 2.5 fusion.41
  825.8 3.1 fusion.14
  830.8 1.7 collective-permute-start.3
  835.6 2.8 pad_maximum_fusion
  838.4 8.1 copy.79
  850.7 52.4 %shard_map.174 = (f32[96,1792]{1,0:T(8,128)}, f32[80,128]{1,0:T(8,128)}) custom-call(bf16[16,96,1792]{2,1,0:T(8,128)(2,1)} %bitcast.275, f32[80,128]{1,0:T(8,128)} %pad_maximum_fusion.9.x_ref), custom_call_target="tpu_custom_call" | custom-call | bytes 210000000 | tf_op jit(solution)/shard_map/pallas_call | solution.py:635
  911.1 1.8 subtract_add_fusion
  921.2 1.9 maximum_convert_fusion.1
  923.1 4.9 maximum_convert_fusion
  (292 shorter events, 88.6 us)
Async XLA Ops:
  14.3 167.9 %copy-start.35 = (f32[256,64]{1,0:T(8,128)}, f32[256,64]{1,0:T(8,128)S(1)}, u32[]{:S(2)}) copy-start(f32[256,64]{1,0:T(8,128)S(1)} %get-tuple-element.133) | copy-start | bytes 196612
  22.1 378.8 %copy-start.68 = (pred[1152]{0:T(1024)(128)(4,1)}, pred[1152]{0:T(1024)(128)(4,1)S(1)}, u32[]{:S(2)}) copy-start(pred[1152]{0:T(1024)(128)(4,1)S(1)} %iota_compare_fusion.1) | copy-start | bytes 3460
  387.2 13.6 %copy-start.19 = (bf16[8,128,1536]{2,1,0:T(8,128)(2,1)S(1)}, bf16[8,128,1536]{2,1,0:T(8,128)(2,1)}, u32[]{:S(2)}) copy-start(bf16[8,128,1536]{2,1,0:T(8,128)(2,1)} %get-tuple-element.48) | copy-start | bytes 9437188
  387.2 13.6 %copy-start.77 = (bf16[16,96,1152]{2,1,0:T(8,128)(2,1)S(1)}, bf16[16,96,1152]{2,1,0:T(8,128)(2,1)}, u32[]{:S(2)}) copy-start(bf16[16,96,1152]{2,1,0:T(8,128)(2,1)} %get-tuple-element.49) | copy-start | bytes 10616836
  400.8 8.8 copy-start.20
  415.3 15.3 %slice-start.5 = ((s8[7077888]{0:T(1024)(128)(4,1)}), s8[4194304]{0:T(1024)(128)(4,1)S(1)}, s32[]{:S(2)}) async-start(s8[7077888]{0:T(1024)(128)(4,1)} %bitcast.327), calls=%async_computation.9 | async-start | bytes 8388608
  421.0 9.6 %slice-start.6 = ((s8[7077888]{0:T(1024)(128)(4,1)}), s8[2883584]{0:T(1024)(128)(4,1)S(1)}, s32[]{:S(2)}) async-start(s8[7077888]{0:T(1024)(128)(4,1)} %bitcast.327), calls=%async_computation.10 | async-start | bytes 5767168
  439.9 113.5 %copy-start.39 = (bf16[128,1536]{1,0:T(8,128)(2,1)S(1)}, bf16[128,1536]{1,0:T(8,128)(2,1)}, u32[]{:S(2)}) copy-start(bf16[128,1536]{1,0:T(8,128)(2,1)} %refs_1_.1) | copy-start | bytes 1179652
  556.1 20.9 %collective-permute-start = (bf16[128,1536]{1,0:T(8,128)(2,1)S(1)}, bf16[128,1536]{1,0:T(8,128)(2,1)}, u32[]{:S(2)}, u32[]{:S(2)}) collective-permute-start(bf16[128,1536]{1,0:T(8,128)(2,1)S(1)} %get-tuple-element.91), channel_id=1, source_target_pairs={{0,1},{1,0},{2,3},{3,2},{4,5},{5,4},{6,7},{7,6},{8,9},{9,8},{10,11... | collective-permute-start | bytes 1179656 | tf_op jit(solution)/shard_map/ppermute | solution.py:91
  556.2 7.4 copy-start.38
  556.2 8.1 copy-start.57
  556.2 63.2 %all-to-all-start = ((bf16[4,96,3456]{2,1,0:T(8,128)(2,1)}), bf16[4,96,3456]{2,1,0:T(8,128)(2,1)}, u32[]{:S(2)}, u32[]{:S(2)}) async-start(bf16[4,96,3456]{2,1,0:T(8,128)(2,1)} %get-tuple-element.60), calls=%async_computation | async-start | bytes 5308416 | tf_op jit(solution)/shard_map/all_to_all | solution.py:1116
  561.5 366.5 %reduce-scatter.2.cloned.1.call-start = ((), (), s32[]{:S(2)}) async-start(), calls=%async_computation.3 | async-start | bytes 5849088 | tf_op jit(solution)/shard_map/reduce_scatter | solution.py:1158
  566.8 8.1 copy-start.53
  566.8 9.5 %copy-start.4 = (f32[128,1536]{1,0:T(8,128)S(1)}, f32[128,1536]{1,0:T(8,128)}, u32[]{:S(2)}) copy-start(f32[128,1536]{1,0:T(8,128)} %get-tuple-element.63) | copy-start | bytes 2359300
  590.8 8.5 copy-start.46
  596.5 9.4 %collective-permute-start.1 = (bf16[128,1536]{1,0:T(8,128)(2,1)}, bf16[128,1536]{1,0:T(8,128)(2,1)}, u32[]{:S(2)}, u32[]{:S(2)}) collective-permute-start(bf16[128,1536]{1,0:T(8,128)(2,1)} %fusion.55), channel_id=1, source_target_pairs={{0,1},{1,0},{2,3},{3,2},{4,5},{5,4},{6,7},{7,6},{8,9},{9,8},{10,11... | collective-permute-start | bytes 1179656 | tf_op jit(solution)/shard_map/ppermute | solution.py:98
  609.3 69.6 %copy-start.7 = (f32[128,1536]{1,0:T(8,128)}, f32[128,1536]{1,0:T(8,128)S(1)}, u32[]{:S(2)}) copy-start(f32[128,1536]{1,0:T(8,128)S(1)} %subtract_add_fusion.2) | copy-start | bytes 2359300
  678.9 13.9 %slice-start = ((s8[9437184]{0:T(1024)(128)(4,1)}), s8[1048576]{0:T(1024)(128)(4,1)S(1)}, s32[]{:S(2)}) async-start(s8[9437184]{0:T(1024)(128)(4,1)} %bitcast.278), calls=%async_computation.4 | async-start | bytes 2097152
  684.0 8.9 copy-start
  684.0 8.9 slice-start.1
  684.0 8.9 slice-start.2
  684.0 8.9 copy-start.69
  684.0 8.9 copy-start.76
  692.9 18.0 %slice-start.3 = ((s8[7077888]{0:T(1024)(128)(4,1)}), s8[4194304]{0:T(1024)(128)(4,1)S(1)}, s32[]{:S(2)}) async-start(s8[7077888]{0:T(1024)(128)(4,1)} %bitcast.323), calls=%async_computation.7 | async-start | bytes 8388608
  699.7 11.2 %slice-start.4 = ((s8[7077888]{0:T(1024)(128)(4,1)}), s8[2883584]{0:T(1024)(128)(4,1)S(1)}, s32[]{:S(2)}) async-start(s8[7077888]{0:T(1024)(128)(4,1)} %bitcast.323), calls=%async_computation.8 | async-start | bytes 5767168
  699.8 11.2 %copy-start.78 = (bf16[1024,1152]{1,0:T(8,128)(2,1)S(1)}, bf16[1024,1152]{1,0:T(8,128)(2,1)}, u32[]{:S(2)}) copy-start(bf16[1024,1152]{1,0:T(8,128)(2,1)} %get-tuple-element.94) | copy-start | bytes 7077892
  784.6 128.3 %all-to-all-start.1 = ((bf16[4,96,3456]{2,1,0:T(8,128)(2,1)}), bf16[4,96,3456]{2,1,0:T(8,128)(2,1)}, u32[]{:S(2)}, u32[]{:S(2)}) async-start(bf16[4,96,3456]{2,1,0:T(8,128)(2,1)} %get-tuple-element.75), calls=%async_computation.2 | async-start | bytes 5308416 | tf_op jit(solution)/shard_map/all_to_all | solution.py:1116
  791.2 12.4 %copy-start.24 = (f32[128,1536]{1,0:T(8,128)S(1)}, f32[128,1536]{1,0:T(8,128)}, u32[]{:S(2)}) copy-start(f32[128,1536]{1,0:T(8,128)} %get-tuple-element.62) | copy-start | bytes 2359300
  791.2 12.4 %copy-start.60 = (f32[1536]{0:T(1024)S(1)}, f32[1536]{0:T(1024)}, u32[]{:S(2)}) copy-start(f32[1536]{0:T(1024)} %get-tuple-element.87) | copy-start | bytes 18436
  791.2 12.4 %copy-start.70 = (f32[128]{0:T(128)S(1)}, f32[128]{0:T(128)}, u32[]{:S(2)}) copy-start(f32[128]{0:T(128)} %get-tuple-element.140) | copy-start | bytes 1540
  791.3 12.6 %copy-start.8 = (f32[128,1536]{1,0:T(8,128)S(1)}, f32[128,1536]{1,0:T(8,128)}, u32[]{:S(2)}) copy-start(f32[128,1536]{1,0:T(8,128)} %copy-done.7) | copy-start | bytes 2359300
  791.3 12.6 %copy-start.72 = (f32[128]{0:T(128)S(1)}, f32[128]{0:T(128)}, u32[]{:S(2)}) copy-start(f32[128]{0:T(128)} %get-tuple-element.139) | copy-start | bytes 1540
  805.0 10.9 %collective-permute-start.2 = (bf16[128,1536]{1,0:T(8,128)(2,1)S(1)}, bf16[128,1536]{1,0:T(8,128)(2,1)S(1)}, u32[]{:S(2)}, u32[]{:S(2)}) collective-permute-start(bf16[128,1536]{1,0:T(8,128)(2,1)S(1)} %get-tuple-element.89), channel_id=1, source_target_pairs={{0,1},{1,0},{2,3},{3,2},{4,5},{5,4},{6,7},{7,6},{8,9},{9,8},{10,11... | collective-permute-start | bytes 1179656 | tf_op jit(solution)/shard_map/ppermute | solution.py:91
  825.7 7.0 copy-start.67
  825.7 7.1 copy-start.73
  825.8 7.8 copy-start.10
  825.8 7.7 copy-start.55
  830.8 15.8 %collective-permute-start.3 = (bf16[128,1536]{1,0:T(8,128)(2,1)}, bf16[128,1536]{1,0:T(8,128)(2,1)S(1)}, u32[]{:S(2)}, u32[]{:S(2)}) collective-permute-start(bf16[128,1536]{1,0:T(8,128)(2,1)} %fusion.56), channel_id=1, source_target_pairs={{0,1},{1,0},{2,3},{3,2},{4,5},{5,4},{6,7},{7,6},{8,9},{9,8},{10,11... | collective-permute-start | bytes 1179656 | tf_op jit(solution)/shard_map/ppermute | solution.py:98
  838.4 8.1 copy-start.27
  838.4 8.1 copy-start.71
  838.4 8.9 copy-start.65
  847.4 63.7 %copy-start.23 = (f32[128,1536]{1,0:T(8,128)S(1)}, f32[128,1536]{1,0:T(8,128)}, u32[]{:S(2)}) copy-start(f32[128,1536]{1,0:T(8,128)} %get-tuple-element.90) | copy-start | bytes 2359300
  848.0 63.1 %copy-start.74 = (f32[128]{0:T(128)S(1)}, f32[128]{0:T(128)}, u32[]{:S(2)}) copy-start(f32[128]{0:T(128)} %get-tuple-element.78) | copy-start | bytes 1540
  912.9 8.3 copy-start.48
  912.9 8.3 copy-start.49
  912.9 8.3 copy-start.50
  912.9 8.3 copy-start.51
  (45 other events, 155.9 us)
Sparse Core Ops, SparseCore 0:
  603.4 84.6 reduce-scatter.1

commit v4 on v3

--- a/solution.py
+++ b/solution.py
@@ -9,28 +9,12 @@
 from jax.sharding import Mesh
 from jax.sharding import PartitionSpec as P
 
-H = 12
-KV = 2
 HD = 128
 LINE = 4
 LANES = 128
 LOW = jnp.bfloat16
 F32 = jnp.float32
 MESH = pl.DeviceIdType.MESH
-
-
-def rms_factor(rows):
-    return lax.rsqrt(jnp.mean(rows * rows, axis=-1, keepdims=True) + 1e-06)
-
-
-def rotate(values):
-    half = values.shape[-1] // 2
-    return jnp.concatenate([-values[..., half:], values[..., :half]], axis=-1)
-
-
-def rotate_back(values):
-    half = values.shape[-1] // 2
-    return jnp.concatenate([values[..., half:], -values[..., :half]], axis=-1)
 
 
 def doc_layout(lens, count):
@@ -66,37 +50,8 @@
     return lax.dot_general(left, right, (((0,), (0,)), ((), ())), preferred_element_type=out)
 
 
-def norm_back(upstream, rows, factor, gain):
-    scaled = upstream * gain
-    gain_part = jnp.sum(upstream * rows * factor, axis=0)
-    result = factor * scaled - rows * factor**3 * jnp.mean(scaled * rows, axis=-1, keepdims=True)
-    return (result, gain_part)
-
-
-SWAP = [(0, 1), (1, 0)]
-
-
 def take(array, index, axis):
     return lax.dynamic_index_in_dim(array, index, axis, keepdims=False)
-
-
-def join_pair(own, other, axis_name, axis):
-    index = lax.axis_index(axis_name)
-    return jnp.where(
-        index == 0, jnp.stack([own, other], axis=axis), jnp.stack([other, own], axis=axis)
-    )
-
-
-def spread_pair(rows):
-    other = lax.ppermute(rows, "t", SWAP)
-    return join_pair(rows, other, "t", 0).reshape(2 * rows.shape[0], rows.shape[1])
-
-
-def sum_pair(partial):
-    index = lax.axis_index("t")
-    halves = partial.reshape(2, partial.shape[0] // 2, partial.shape[1])
-    other = lax.ppermute(take(halves, 1 - index, 0).astype(LOW), "t", SWAP)
-    return take(halves, index, 0) + other.astype(F32)
 
 
 def greet(axes_targets, conditions):
@@ -235,19 +190,6 @@
             guarded(condition, lambda make=make: make().wait_send())
 
 
-def gather_kernel(size, bits, *refs):
-    z = lax.axis_index("z")
-    mine = [lax.axis_index(bit) for bit in bits]
-    greet(
-        [("z", z + 1), ("z", z - 1)] + [(bit, 1 - m) for bit, m in zip(bits, mine)],
-        [z < size - 1, z > 0] + [None] * len(bits),
-    )
-    steps = Gather(size, bits, *refs)
-    steps.begin()
-    steps.middle()
-    steps.end()
-
-
 def gather_semaphores(size, bits):
     slots = size * 2 ** len(bits)
     return [
@@ -256,21 +198,6 @@
         pltpu.SemaphoreType.DMA((size, 2, 2 ** len(bits), len(bits))),
         pltpu.SemaphoreType.DMA((slots,)),
     ]
-
-
-def gather(x, size, bits, collective_id):
-    slots = size * 2 ** len(bits)
-    return pl.pallas_call(
-        functools.partial(gather_kernel, size, bits),
-        out_shape=jax.ShapeDtypeStruct((slots, *x.shape), x.dtype),
-        in_specs=[pl.BlockSpec(memory_space=pl.ANY)],
-        out_specs=pl.BlockSpec(memory_space=pl.ANY),
-        scratch_shapes=gather_semaphores(size, bits),
-        compiler_params=pltpu.CompilerParams(collective_id=collective_id, has_side_effects=True),
-        cost_estimate=pl.CostEstimate(
-            flops=0, transcendentals=0, bytes_accessed=slots * x.size * 100
-        ),
-    )(x)
 
 
 class Exchange:
@@ -499,8 +426,8 @@
         else:
             self.out_ref[...] = total
 
-    def begin(self):
-        self.fold.begin()
+    def begin(self, places=None):
+        self.fold.begin(places)
 
     def place(self, place):
         for stage in reversed(range(self.fold.count)):
@@ -602,7 +529,7 @@
 
 def comm_params(collective_id):
     return pltpu.CompilerParams(
-        collective_id=collective_id, has_side_effects=True, vmem_limit_bytes=56 * 2**20
+        collective_id=collective_id, has_side_effects=True, vmem_limit_bytes=60 * 2**20
     )
 
 
@@ -647,85 +574,6 @@
         compiler_params=comm_params(collective_id),
         cost_estimate=at_microseconds(60),
     )(partial, x)
-
-
-def back_kernel(size, bits, branches, *refs):
-    p_refs, (gu_ref, dn_ref), outs, (folded,), refs = in_groups(
-        refs, [branches, 2, branches, 1, len(refs)]
-    )
-    greet_all(size, ("t", *bits))
-    *scatters, gu_scratch, dn_scratch, (gu_done, dn_done, done_sems) = in_groups(
-        refs, [SCATTER_REFS] * branches + [7, 7, 3]
-    )
-    scatters = [
-        Scatter(size, ("t",), p, out, *scratch) for p, out, scratch in zip(p_refs, outs, scatters)
-    ]
-    order = list(range(size))
-    gu = Fold(size, bits, order, gu_ref, *gu_scratch)
-    dn = Fold(size, bits, order, dn_ref, *dn_scratch)
-    width, narrow = gu_ref.shape[2], dn_ref.shape[2]
-
-    def out_copy(number, place, line):
-        source = (gu_done, dn_done)[number].at[place]
-        low, count = ((0, width), (width, narrow))[number]
-        return pltpu.make_async_copy(
-            source, folded.at[line, :, pl.ds(low, count)], done_sems.at[number, place]
-        )
-
-    def done(number):
-        def keep(place, total):
-            (gu_done, dn_done)[number][place] = total.astype(LOW)
-            out_copy(number, place, gu.line(place)).start()
-
-        return keep
-
-    for steps in scatters:
-        steps.begin()
-    gu.begin()
-    dn.begin()
-    for place in range(size):
-        for stage in reversed(range(1, len(bits))):
-            gu.stage(place, stage)
-            dn.stage(place, stage)
-        for steps in scatters:
-            steps.place(place)
-    for steps in scatters:
-        steps.finish()
-    for place in range(size):
-        gu.stage(place, 0, done(0))
-        dn.stage(place, 0, done(1))
-    for place in range(size):
-        for number in range(2):
-            out_copy(number, place, gu.line(place)).wait()
-    for steps in (*scatters, gu, dn):
-        steps.end()
-
-
-def back(partials, gu, dn, size, bits, collective_id):
-    _, rows, columns = partials[0].shape
-    slots, few, width = gu.shape
-    narrow = dn.shape[2]
-    branches = len(partials)
-    out = pl.pallas_call(
-        functools.partial(back_kernel, size, bits, branches),
-        out_shape=(
-            *([jax.ShapeDtypeStruct((rows, columns), F32)] * branches),
-            jax.ShapeDtypeStruct((size, few, width + narrow), LOW),
-        ),
-        in_specs=[pl.BlockSpec(memory_space=pl.ANY)] * (branches + 2),
-        out_specs=[pl.BlockSpec(memory_space=pltpu.VMEM)] * branches + [pl.BlockSpec(memory_space=pl.ANY)],
-        scratch_shapes=[
-            *(scatter_scratch(size, ("t",), rows, columns) * branches),
-            *fold_scratch(size, bits, few, width),
-            *fold_scratch(size, bits, few, narrow),
-            pltpu.VMEM((size, few, width), LOW),
-            pltpu.VMEM((size, few, narrow), LOW),
-            pltpu.SemaphoreType.DMA((2, size)),
-        ],
-        compiler_params=comm_params(collective_id),
-        cost_estimate=at_microseconds(80),
-    )(*partials, gu, dn)
-    return out[:branches], out[branches]
 
 
 class Attend:
@@ -999,8 +847,322 @@
     )(x, more, *gains, bias, *tables, at, gu, dn)
 
 
-def spread_group(rows):
-    return gather(rows, LINE, ("t",), 1).reshape(-1, rows.shape[1])
+class AttendBack:
+    def __init__(self, ins, outs, scratch, width, epsilon=1e-06):
+        (self.g_ref, self.state_ref, self.middle_ref, self.ga_gain, self.gf_gain, self.cos_ref, self.sin_ref) = ins[:7]
+        (self.mask_ref, self.q_ref, self.k_ref, self.v_ref, self.lse_ref, self.far_w) = ins[7:]
+        (self.grad_ref, self.ga_ref, self.lin_ref, self.bias_ref, self.pa_ref, self.pf_ref) = outs
+        (self.w_ref, self.w_sem, self.dk, self.dv, self.sum_buf, self.send_buf, self.land_buf) = scratch[:7]
+        (self.send_sems, self.recv_sems) = scratch[7:]
+        self.t = lax.axis_index("t")
+        self.slots, self.few = self.w_ref.shape[:2]
+        self.model = self.slots * self.few
+        self.count = self.state_ref.shape[0]
+        self.q_width = self.q_ref.shape[1]
+        self.width, self.epsilon = width, epsilon
+
+    def pair_copy(self, number, source, landing):
+        return pltpu.make_async_remote_copy(
+            src_ref=source,
+            dst_ref=landing,
+            send_sem=self.send_sems.at[number],
+            recv_sem=self.recv_sems.at[number],
+            device_id={"t": 1 - self.t},
+            device_id_type=MESH,
+        )
+
+    def ga_copy(self, side):
+        return self.pair_copy(0, self.ga_ref.at[side], self.ga_ref.at[side])
+
+    def half_copy(self):
+        return self.pair_copy(1, self.send_buf, self.land_buf)
+
+    def weight_copy(self):
+        return pltpu.make_async_copy(self.far_w, self.w_ref, self.w_sem)
+
+    def norm_back(self, upstream, rows, gain):
+        factor = lax.rsqrt(jnp.mean(rows * rows, axis=-1, keepdims=True) + self.epsilon)
+        scaled = upstream * gain
+        part = jnp.sum(upstream * rows * factor, axis=0, keepdims=True)
+        inner = jnp.mean(scaled * rows, axis=-1, keepdims=True)
+        return factor * scaled - rows * factor**3 * inner, part
+
+    def prepare(self):
+        self.weight_copy().start()
+
+    def begin(self, d_xf):
+        d_mid, part = self.norm_back(d_xf, self.middle_ref[...], self.gf_gain[...])
+        self.pf_ref[...] = part
+        grad = self.g_ref[...].astype(F32) + d_mid
+        self.grad_ref[...] = grad
+        self.ga_ref[self.t] = grad.astype(LOW)
+        self.ga_copy(self.t).start()
+        self.dk[...] = jnp.zeros_like(self.dk)
+        self.dv[...] = jnp.zeros_like(self.dv)
+
+    def arrive(self):
+        self.weight_copy().wait()
+        self.ga_copy(1 - self.t).wait_recv()
+
+    def unrope(self, values):
+        return values * self.cos_ref[...] - pltpu.roll(values, HD // 2, 1) * self.sin_ref[...]
+
+    def keep(self, low, values):
+        count = values.shape[1]
+        self.bias_ref[:, low : low + count] = jnp.sum(values, axis=0, keepdims=True)
+        values = values.astype(LOW)
+        self.lin_ref[0, :, low : low + count] = values[: self.count]
+        self.lin_ref[1, :, low : low + count] = values[self.count :]
+
+    def heads(self, first):
+        low, count = self.width + first * HD, 2 * HD
+        weight = self.w_ref[:, :, low : low + count].reshape(self.model, count)
+        above = self.ga_ref[...].reshape(2 * self.count, self.model)
+        d_out = jnp.dot(above, weight, preferred_element_type=F32).astype(LOW)
+        key, value = self.k_ref[...], self.v_ref[...]
+        last = (((1,), (1,)), ((), ()))
+        early = (((0,), (0,)), ((), ()))
+        scale = 1.0 / math.sqrt(HD)
+        for number in range(2):
+            head = first + number
+            query = self.q_ref[:, head * HD : (head + 1) * HD]
+            d_head = d_out[:, number * HD : (number + 1) * HD]
+            raw = lax.dot_general(query, key, last, preferred_element_type=F32)
+            scores = jnp.where(self.mask_ref[...] > 0, raw * scale, -1e30)
+            probs = jnp.exp(scores - self.lse_ref[head])
+            d_probs = lax.dot_general(d_head, value, last, preferred_element_type=F32)
+            centre = jnp.sum(probs * d_probs, axis=-1, keepdims=True)
+            d_raw = (probs * (d_probs - centre) * scale).astype(LOW)
+            d_query = jnp.dot(d_raw, key, preferred_element_type=F32)
+            self.dk[...] += lax.dot_general(d_raw, query, early, preferred_element_type=F32)
+            self.dv[...] += lax.dot_general(
+                probs.astype(LOW), d_head, early, preferred_element_type=F32
+            )
+            self.keep(head * HD, self.unrope(d_query))
+
+    def keys(self):
+        self.keep(self.q_width, self.unrope(self.dk[...]))
+        self.keep(self.q_width + HD, self.dv[...])
+
+    def projected(self, half):
+        left, step = self.lin_ref[half], self.slots // 4
+        for low in range(0, self.slots, step):
+            weight = self.w_ref[low : low + step, :, : self.width].reshape(step * self.few, self.width)
+            yield slice(low * self.few, (low + step) * self.few), lax.dot_general(
+                left, weight, (((1,), (1,)), ((), ())), preferred_element_type=F32
+            )
+
+    def other_half(self):
+        for where, part in self.projected(1 - self.t):
+            self.send_buf[:, where] = part.astype(LOW)
+        self.half_copy().start()
+
+    def own_half(self):
+        for where, part in self.projected(self.t):
+            self.sum_buf[:, where] = part
+
+    def finish(self):
+        self.half_copy().wait_recv()
+        d_xa = self.sum_buf[...] + self.land_buf[...].astype(F32)
+        d_in, part = self.norm_back(d_xa, self.state_ref[...], self.ga_gain[...])
+        self.pa_ref[...] = part
+        grad = self.grad_ref[...] + d_in
+        self.grad_ref[...] = grad
+        return grad
+
+    def end(self):
+        self.ga_copy(self.t).wait_send()
+        self.half_copy().wait_send()
+
+
+class Blocks:
+    def __init__(self, size, bits, gu_ref, dn_ref, out_ref, gu_fold, dn_fold, done, sems):
+        self.size, self.out_ref = size, out_ref
+        order = list(range(1, size)) + [0]
+        self.folds = [Fold(size, bits, order, gu_ref, *gu_fold), Fold(size, bits, order, dn_ref, *dn_fold)]
+        self.done = done
+        self.own_sems, self.send_sems, self.recv_sems = sems
+        self.width, self.narrow = gu_ref.shape[2], dn_ref.shape[2]
+        self.z = lax.axis_index("z")
+
+    def landing(self, number, slot):
+        low, count = ((0, self.width), (self.width, self.narrow))[number]
+        return self.out_ref.at[slot, :, pl.ds(low, count)]
+
+    def line_copy(self, number, place, slot):
+        return pltpu.make_async_remote_copy(
+            src_ref=self.done[number].at[place],
+            dst_ref=self.landing(number, slot),
+            send_sem=self.send_sems.at[number, place],
+            recv_sem=self.recv_sems.at[number, slot],
+            device_id={"z": self.folds[0].line(place)},
+            device_id_type=MESH,
+        )
+
+    def own_copy(self, number):
+        return pltpu.make_async_copy(
+            self.done[number].at[self.size - 1], self.landing(number, self.z), self.own_sems.at[number]
+        )
+
+    def begin(self):
+        for fold in self.folds:
+            fold.begin()
+
+    def inner(self, place):
+        for stage in reversed(range(1, self.folds[0].count)):
+            for fold in self.folds:
+                fold.stage(place, stage)
+
+    def send(self, place):
+        for number, fold in enumerate(self.folds):
+
+            def keep(place, total, number=number):
+                self.done[number][place] = total.astype(LOW)
+                if place < self.size - 1:
+                    self.line_copy(number, place, self.z).start()
+                else:
+                    self.own_copy(number).start()
+
+            fold.stage(place, 0, keep)
+
+    def end(self):
+        for number, fold in enumerate(self.folds):
+            for offset in range(1, self.size):
+                slot = lax.rem(self.z - offset + self.size, self.size)
+                self.line_copy(number, 0, slot).wait_recv()
+            for place in range(self.size - 1):
+                self.line_copy(number, place, self.z).wait_send()
+            self.own_copy(number).wait()
+            fold.end()
+
+
+def back_kernel(size, bits, width, final, *refs):
+    top, bottom = final
+    counts = [1, 1 if top else 0, 2, 13, 6, 1, 1 if top else 0, 0 if bottom else 1]
+    p_ref, branch_ref, wide, ins, outs, (blocks_ref,), branch_out, gm_out, refs = in_groups(
+        refs, counts + [len(refs)]
+    )
+    (dxf_ref,), dxf_scratch, gu_fold, dn_fold, done, sems, work_scratch, refs = in_groups(
+        refs, [1, SCATTER_REFS, 7, 7, 2, 3, 9, len(refs)]
+    )
+    greet_all(size, ("t", *bits))
+    rows = Scatter(size, ("t",), p_ref[0], dxf_ref, *dxf_scratch)
+    blocks = Blocks(size, bits, *wide, blocks_ref, gu_fold, dn_fold, done, sems)
+    work = AttendBack(ins, outs, work_scratch, width)
+    branch = onward = None
+    if top:
+        branch_scratch, refs = in_groups(refs, [SCATTER_REFS, len(refs)])
+        branch = Scatter(size, ("t",), branch_ref[0], branch_out[0], *branch_scratch)
+    if not bottom:
+        gm_ref, *gm_sems = refs
+        onward = Gather(size, ("t",), gm_ref, gm_out[0], *gm_sems)
+    rows.begin()
+    blocks.begin()
+    work.prepare()
+    blocks.inner(0)
+    rows.place(0)
+    blocks.inner(1)
+    blocks.inner(2)
+    rows.place(1)
+    blocks.inner(3)
+    blocks.send(0)
+    rows.place(2)
+    rows.place(3)
+    if top:
+        branch.begin([0])
+    rows.finish()
+    blocks.send(1)
+    work.begin(dxf_ref[...])
+    if top:
+        branch.begin([1])
+    work.arrive()
+    work.heads(0)
+    if top:
+        branch.place(0)
+    work.heads(2)
+    blocks.send(2)
+    work.heads(4)
+    work.keys()
+    work.other_half()
+    if top:
+        branch.place(1)
+        branch.begin([2])
+    work.own_half()
+    blocks.send(3)
+    grad = work.finish()
+    if not bottom:
+        gm_ref[...] = grad.astype(LOW)
+        onward.begin()
+    if top:
+        branch.begin([3])
+        branch.place(2)
+    if not bottom:
+        onward.step(1)
+        onward.on_bits(0)
+    if top:
+        branch.place(3)
+    if not bottom:
+        onward.step(2)
+        onward.on_bits(1)
+        onward.step(3)
+        onward.on_bits(2)
+        onward.on_bits(3)
+    if top:
+        branch.finish()
+    for steps in (rows, blocks, work, branch, onward):
+        if steps is not None:
+            steps.end()
+
+
+def back(partial, branch, gu, dn, ins, size, bits, width, bottom, collective_id):
+    count, model = ins[1].shape
+    length, q_width = ins[8].shape
+    slots, few, wide = gu.shape
+    narrow = dn.shape[2]
+    top = branch is not None
+    held, far = pl.BlockSpec(memory_space=pltpu.VMEM), pl.BlockSpec(memory_space=pl.ANY)
+    shape = jax.ShapeDtypeStruct
+    rows_scratch = scatter_scratch(size, ("t",), count, model)
+    return pl.pallas_call(
+        functools.partial(back_kernel, size, bits, width, (top, bottom)),
+        out_shape=(
+            shape((count, model), F32),
+            shape((2, count, model), LOW),
+            shape((2, count, width), LOW),
+            shape((1, width), F32),
+            shape((1, model), F32),
+            shape((1, model), F32),
+            shape((size, few, wide + narrow), LOW),
+            *([shape((count, model), F32)] if top else []),
+            *([] if bottom else [shape((2 * size, count, model), LOW)]),
+        ),
+        in_specs=[far] * (4 if top else 3) + [held] * 12 + [far],
+        out_specs=[held] * 6 + [far] + [held] * top + [far] * (not bottom),
+        scratch_shapes=[
+            pltpu.VMEM((count, model), F32),
+            *rows_scratch,
+            *fold_scratch(size, bits, few, wide),
+            *fold_scratch(size, bits, few, narrow),
+            pltpu.VMEM((size, few, wide), LOW),
+            pltpu.VMEM((size, few, narrow), LOW),
+            pltpu.SemaphoreType.DMA((2,)),
+            pltpu.SemaphoreType.DMA((2, size)),
+            pltpu.SemaphoreType.DMA((2, size)),
+            pltpu.VMEM(ins[12].shape, LOW),
+            pltpu.SemaphoreType.DMA,
+            pltpu.VMEM((length, HD), F32),
+            pltpu.VMEM((length, HD), F32),
+            pltpu.VMEM((count, model), F32),
+            pltpu.VMEM((count, model), LOW),
+            pltpu.VMEM((count, model), LOW),
+            pltpu.SemaphoreType.DMA((2,)),
+            pltpu.SemaphoreType.DMA((2,)),
+            *(rows_scratch if top else []),
+            *([] if bottom else [pltpu.VMEM((count, model), LOW), *gather_semaphores(size, ("t",))]),
+        ],
+        compiler_params=comm_params(collective_id),
+        cost_estimate=at_microseconds(120),
+    )(partial, *([branch] if top else []), gu, dn, *ins)
 
 
 def in_slots(partial, slots):
@@ -1013,10 +1175,6 @@
 
 def block_start(line, block, half):
     return min(line * block, half - block)
-
-
-def tie(value, *others):
-    return lax.optimization_barrier((value, *others))
 
 
 def from_blocks(blocks, parts, half):
@@ -1037,23 +1195,14 @@
     count = tokens.shape[0]
     length = count * tensor_size
     layers = w_qkv.shape[0]
-    kv_local = KV // tensor_size
-    groups = H // KV
-    q_width = kv_local * groups * HD
-    kv_width = kv_local * HD
     qkv_width = w_qkv.shape[2]
     rows = w_qkv.shape[1]
     half = w_down.shape[2]
     block = block_width(half)
-    scale = 1.0 / math.sqrt(HD)
     positions, allowed = doc_layout(doc_lengths[0], length)
     cosine, sine = rope_tables(positions, HD)
     turned = jnp.where(jnp.arange(HD) < HD // 2, -sine, sine)
     tables = (cosine, turned, allowed.astype(F32))
-    cos_q = cosine[:, None, None, :]
-    sin_q = sine[:, None, None, :]
-    cos_k = cosine[:, None, :]
-    sin_k = sine[:, None, :]
     gain_attn = norm_attn.astype(F32)
     gain_ffn = norm_ffn.astype(F32)
     bias_all = b_qkv.astype(F32)
@@ -1071,13 +1220,10 @@
         if layer == 0:
             gm_all = out[12].reshape(-1, cotangent.shape[1])
         (state, middle, xa_all, query, key, value, log_total, attended) = out[:8]
-        xf_all, gu_w, down_w, both_w = (item.reshape(-1, item.shape[2]) for item in out[8:12])
+        xf_all, gu_w, down_w = (item.reshape(-1, item.shape[2]) for item in out[8:11])
+        both_w = out[11]
         xa_all = xa_all.reshape(length, -1)
         attended = attended.reshape(length, -1)
-        query = query.reshape(length, kv_local, groups, HD)
-        key = key.reshape(length, kv_local, HD)
-        value = value.reshape(length, kv_local, HD)
-        log_total = log_total[None]
         gate_up = jnp.dot(xf_all, gu_w, preferred_element_type=F32)
         gate = gate_up[:, :block]
         up = gate_up[:, block:]
@@ -1087,17 +1233,11 @@
             (state, xa_all, query, key, value, log_total, attended)
             + (middle, xf_all, gate, up, act, gu_w, down_w, both_w)
         )
-    grad = cotangent.astype(F32)
-    grads_attn, grads_bias, grads_ga, grads_gf = ([] for _ in range(4))
-    waiting, branches = None, [in_slots(partial, 2 * LINE)]
-    grads_blocks = []
+    grad, branch = cotangent, in_slots(partial, 2 * LINE)
+    grads_attn, grads_bias, grads_ga, grads_gf, grads_blocks = ([] for _ in range(5))
     for layer in reversed(range(layers)):
         (state_in, xa_all, query, key, value, log_total, attended) = saved[layer][:7]
         (middle, xf_all, gate, up, act, gu_w, down_w, both_w) = saved[layer][7:]
-        factor_a, factor_f = rms_factor(state_in), rms_factor(middle)
-        qkv_w, out_w = both_w[:, :qkv_width], both_w[:, qkv_width:]
-        if waiting is not None:
-            gm_all = spread_group(grad.astype(LOW))
         d_down = contract_first(gm_all, act, LOW)
         d_act = jnp.dot(gm_all, down_w, preferred_element_type=F32)
         sig = jax.nn.sigmoid(gate)
@@ -1107,49 +1247,22 @@
             [jnp.where(valid, d_gate, 0.0), jnp.where(valid, d_up, 0.0)], axis=1
         ).astype(LOW)
         d_gateup = contract_first(xf_all, d_gu, LOW)
-        branches.insert(0, in_slots(contract_last(d_gu, gu_w, LOW), 2 * LINE))
-        slots = in_slots(d_gateup, d_gateup.shape[0] // rows), in_slots(d_down, d_down.shape[0] // rows)
-        (d_xf, *others), folded = back(branches, *slots, LINE, bits, 6 + layer)
-        branches = []
-        if others:
-            output = (middle + others[0]).astype(LOW)
-        waiting = lax.all_to_all(folded, "z", 0, 0, tiled=True)
-        d_mid, part_f = norm_back(d_xf, middle, factor_f, gain_ffn[layer])
-        grad = grad + d_mid
-        ga_all = spread_pair(grad.astype(LOW))
-        d_att = jnp.dot(ga_all, out_w, preferred_element_type=F32).astype(LOW)
-        raw = jnp.einsum("qkgd,pkd->kgqp", query, key, preferred_element_type=F32)
-        scores = jnp.where(allowed, raw * scale, -1e30)
-        probs = jnp.exp(scores - log_total)
-        d_att4 = d_att.reshape(length, kv_local, groups, HD)
-        d_probs = jnp.einsum("qkgd,pkd->kgqp", d_att4, value, preferred_element_type=F32)
-        centre = jnp.sum(probs * d_probs, axis=-1, keepdims=True)
-        d_raw = (probs * (d_probs - centre) * scale).astype(LOW)
-        d_query = jnp.einsum("kgqp,pkd->qkgd", d_raw, key, preferred_element_type=F32)
-        d_key = jnp.einsum("kgqp,qkgd->pkd", d_raw, query, preferred_element_type=F32)
-        d_value = jnp.einsum(
-            "kgqp,qkgd->pkd", probs.astype(LOW), d_att4, preferred_element_type=F32
-        )
-        d_query = d_query * cos_q + rotate_back(d_query * sin_q)
-        d_key = d_key * cos_k + rotate_back(d_key * sin_k)
-        d_lin = jnp.concatenate(
-            [
-                d_query.reshape(length, q_width),
-                d_key.reshape(length, kv_width),
-                d_value.reshape(length, kv_width),
-            ],
-            axis=1,
-        )
-        grads_bias.append(jnp.sum(d_lin, axis=0))
-        d_lin_low = d_lin.astype(LOW)
-        d_xa = sum_pair(contract_last(d_lin_low, qkv_w))
-        d_in, part_a = norm_back(d_xa, state_in, factor_a, gain_attn[layer])
-        grad = grad + d_in
-        if layer > 0:
-            grad, waiting = tie(grad, waiting)
-        grads_blocks.append(waiting)
+        partial = in_slots(contract_last(d_gu, gu_w, LOW), 2 * LINE)
+        wide = (in_slots(d_gateup, d_gateup.shape[0] // rows), in_slots(d_down, d_down.shape[0] // rows))
+        gains = (gain_attn[layer : layer + 1], gain_ffn[layer : layer + 1])
+        ins = (grad, state_in, middle, *gains, *tables, query, key, value, log_total, both_w)
+        out = back(partial, branch, *wide, ins, LINE, bits, qkv_width, layer == 0, 16 + layer)
+        (grad, ga_all, d_lin, d_bias, part_a, part_f, blocks), rest = out[:7], list(out[7:])
+        if branch is not None:
+            output = (middle + rest.pop(0)).astype(LOW)
+            branch = None
+        if rest:
+            gm_all = rest[0].reshape(-1, rest[0].shape[2])
+        grads_bias.append(d_bias[0])
+        grads_blocks.append(blocks)
+        d_lin, ga_all = d_lin.reshape(length, -1), ga_all.reshape(length, -1)
         d_both = jnp.concatenate(
-            [contract_first(xa_all, d_lin_low, LOW), contract_first(ga_all, attended, LOW)], axis=1
+            [contract_first(xa_all, d_lin, LOW), contract_first(ga_all, attended, LOW)], axis=1
         )
         if layer == 0:
             d_both = in_slots(d_both, d_both.shape[0] // rows)
@@ -1157,8 +1270,8 @@
             grads_attn.append(
                 lax.psum_scatter(d_both, dp, scatter_dimension=0, tiled=True).astype(F32)
             )
-        grads_ga.append(part_a)
-        grads_gf.append(part_f)
+        grads_ga.append(part_a[0])
+        grads_gf.append(part_f[0])
 
     def ordered(items):
         return jnp.stack(items[::-1], axis=0)

time: 948 us -> 915 us (0.965)
  Pallas kernels: 621 us -> 696 us
  local copies, waits for them, and re-layouts: 86.6 us -> 50.2 us
  other arithmetic: 50.6 us -> 27 us
  starting transfers between devices: 17.7 us -> 0.04 us
  waiting for transfers between devices: 17.2 us -> 0.02 us
  matrix products: 127 us -> 114 us
    pallas_call x3 -> x2, Pallas kernels: 236 us -> 309 us  [back(): pl.pallas_call(functools.partial(back_kernel, size, bits, width, (top, bo...]
    dot_general x12 -> x0, matrix products: 13.4 us -> none  [the longest x2 4.91 us: local(): d_att = jnp.dot(ga_all, out_w, preferred_element_type=F32).astype(LOW)]
    all_to_all x2 -> x0, starting transfers between devices: 11.8 us -> none  [local(): waiting = lax.all_to_all(folded, 'z', 0, 0, tiled=True)]
    unnamed x184 -> x67, local copies, waits for them, and re-layouts: 24.4 us -> 13.4 us
    all_to_all x2 -> x0, waiting for transfers between devices: 10.1 us -> none  [local(): waiting = lax.all_to_all(folded, 'z', 0, 0, tiled=True)]
    dot_general x6 -> x4, matrix products: 35.5 us -> 29.3 us  [contract_last(): lax.dot_general(left, right, (((1,), (1,)), ((), ())), preferred_element_...]
  transfers between devices with their start and end apart: 7 -> 1, of which waited for: 3 -> 0; matrix products, arithmetic and copies ran while one was open for 17% -> 10% of each run, Pallas kernels for 19% -> 19%
where the time goes in v4:
time: 915 us; the launch traced here: 904 us
  Pallas kernels  696 us (76%)
  matrix products  114 us (12%)
  local copies, waits for them, and re-layouts  50.2 us (5%)
  other arithmetic  27 us (3%)
  between operations  17.3 us (2%)
    pallas_call x2, Pallas kernels, front(): pl.pallas_call(functools.partial(front_kernel, size, bits, block, half, l...  333 us
    pallas_call x2, Pallas kernels, back(): pl.pallas_call(functools.partial(back_kernel, size, bits, width, (top, bo...  309 us
    pallas_call x1, Pallas kernels, last(): pl.pallas_call(functools.partial(last_kernel, size, bits), out_shape=(jax...  53.6 us
    dot_general x8, matrix products, contract_first(): lax.dot_general(left, right, (((0,), (0,)), ((), ())), preferred_element_...  40.4 us
    dot_general x4, matrix products, contract_last(): lax.dot_general(left, right, (((1,), (1,)), ((), ())), preferred_element_...  29.3 us
    dot_general x2, matrix products, local(): gate_up = jnp.dot(xf_all, gu_w, preferred_element_type=F32)  23.4 us
    dot_general x2, matrix products, local(): d_act = jnp.dot(gm_all, down_w, preferred_element_type=F32)  20.8 us
  transfers between devices with their start and end apart: 1, of which 0 were waited for; matrix products, arithmetic and copies ran while one was open for 10% of the time, Pallas kernels for 19%

profile of v4, /device:TPU:26, one launch (start us, length us, event | category | flops | bytes accessed | tf_op | source)
XLA Modules:
  0.0 904.5 jit_solution(6704751990937602910)
XLA Ops:
  7.3 1.4 fusion.33
  11.2 2.6 convert_add_fusion
  16.0 1.0 slice_bitcast_fusion
  17.0 1.0 slice_bitcast_fusion.2
  18.0 1.4 fusion.32
  20.1 1.4 fusion.30
  21.5 0.9 pad_maximum_fusion.3
  22.4 158.5 %shard_map.169 = (f32[128,1536]{1,0:T(8,128)}, f32[128,1536]{1,0:T(8,128)}, bf16[2,128,1536]{2,1,0:T(8,128)(2,1)}, bf16[256,768]{1,0:T(8,128)(2,1)}, bf16[256,12...) custom-call(bf16[128,1536]{1,0:T(8,128)(2,1)} %refs_0_.1, ...), custom_call_target="tpu_custom_call" | custom-call | bytes 525000000 | tf_op jit(solution)/shard_map/pallas_call | solution.py:810
  181.0 5.0 copy.20
  186.0 9.5 %fusion.34 = f32[1024,2304]{1,0:T(8,128)S(1)} fusion(bf16[1024,1536]{1,0:T(8,128)(2,1)S(1)} %bitcast.100, bf16[1536,2304]{1,0:T(8,128)(2,1)} %bitcast.115), kind=kOutput, calls=%fused_computation.100 | convolution fusion | flops 7247757312 | bytes 19660800 | tf_op jit(solution)/shard_map/dot_general | solution.py:1227
  195.5 1.6 select_convert_fusion.5
  197.1 2.8 copy-done
  200.1 5.6 fusion.35.refs_1_
  205.8 174.5 %shard_map.170 = (f32[128,1536]{1,0:T(8,128)}, f32[128,1536]{1,0:T(8,128)}, bf16[2,128,1536]{2,1,0:T(8,128)(2,1)}, bf16[256,768]{1,0:T(8,128)(2,1)}, bf16[256,12...) custom-call(f32[128,1536]{1,0:T(8,128)} %get-tuple-element.52.refs_0, ...), custom_call_target="tpu_custom_call" | custom-call | bytes 525000000 | tf_op jit(solution)/shard_map/pallas_call | solution.py:810
  380.3 4.6 copy.19
  384.9 13.9 %fusion.36 = f32[1024,2304]{1,0:T(8,128)} fusion(bf16[1024,1536]{1,0:T(8,128)(2,1)} %bitcast.108, bf16[1536,2304]{1,0:T(8,128)(2,1)} %bitcast.119), kind=kOutput, calls=%fused_computation.102 | convolution fusion | flops 7247757312 | bytes 19660800 | tf_op jit(solution)/shard_map/dot_general | solution.py:1227
  398.8 8.8 select_convert_fusion.4
  407.6 5.7 fusion.16.refs_3_
  413.3 5.6 fusion.37.refs_1_
  418.9 9.6 %fusion.4.refs_2_ = bf16[16,96,2304]{2,1,0:T(8,128)(2,1)} fusion(bf16[16,96,1024]{2,1,0:T(8,128)(2,1)S(1)} %bitcast.109, bf16[1024,1152]{1,0:T(8,128)(2,1)S(1)} %get-tuple-element.98, bf16[1024,1152]{1,0:T(8,128)(2,1)S(1)} %get-tuple-element.97), kind=kOutput, calls=%fused_computation.7 | convolution fusion | flops 7257194496 | bytes 14942208 | tf_op jit(solution)/shard_map/dot_general | solution.py:50
  428.6 9.0 fusion.refs_0_
  437.6 191.8 %shard_map.171 = (f32[128,1536]{1,0:T(8,128)}, bf16[2,128,1536]{2,1,0:T(8,128)(2,1)}, bf16[2,128,1024]{2,1,0:T(8,128)(2,1)}, f32[1,1024]{1,0:T(1,128)}, f32[1,15...) custom-call(bf16[8,128,1536]{2,1,0:T(8,128)(2,1)} %fusion.refs_0_, ...), custom_call_target="tpu_custom_call" | custom-call | bytes 420000000 | tf_op jit(solution)/shard_map/pallas_call | solution.py:1126
  629.4 2.4 convolution_bitcast_fusion
  631.8 1.3 convolution_bitcast_fusion.2
  633.1 2.9 pad_maximum_fusion.1
  636.0 4.6 copy.22
  640.6 8.9 fusion.14.refs_2_
  649.5 2.8 copy.21
  652.4 12.1 %select_convert_fusion.1 = (bf16[1024,1152]{1,0:T(8,128)(2,1)S(1)}, bf16[1024,1152]{1,0:T(8,128)(2,1)S(1)}) fusion(f32[1024,2304]{1,0:T(8,128)} %copy-done, pred[1152]{0:T(1024)(128)(4,1)S(1)} %iota_compare_fusion.1, bf16[1024,1536]{1,0:T(8,128)(2,1)} %bitcast.103, bf16[1536,1152]{1,0:T(8,128)(2,1)} %bitcast.123), kind=kOutput, calls=%fused_computation.19 | convolution fusion | flops 3641573376 | bytes 20841600 | tf_op jit(solution)/shard_map/dot_general | solution.py:1242
  664.5 9.6 %fusion.11.refs_1_ = bf16[16,96,2304]{2,1,0:T(8,128)(2,1)} fusion(bf16[16,96,1024]{2,1,0:T(8,128)(2,1)S(1)} %bitcast.110, bf16[1024,1152]{1,0:T(8,128)(2,1)S(1)} %get-tuple-element.96, bf16[1024,1152]{1,0:T(8,128)(2,1)S(1)} %get-tuple-element.95), kind=kOutput, calls=%fused_computation.15 | convolution fusion | flops 7257194496 | bytes 14942208 | tf_op jit(solution)/shard_map/dot_general | solution.py:50
  674.1 9.0 fusion.7.refs_0_
  683.2 117.6 %shard_map.172 = (f32[128,1536]{1,0:T(8,128)}, bf16[2,128,1536]{2,1,0:T(8,128)(2,1)}, bf16[2,128,1024]{2,1,0:T(8,128)(2,1)}, f32[1,1024]{1,0:T(1,128)}, f32[1,15...) custom-call(bf16[8,128,1536]{2,1,0:T(8,128)(2,1)} %fusion.7.refs_0_, ...), custom_call_target="tpu_custom_call" | custom-call | bytes 420000000 | tf_op jit(solution)/shard_map/pallas_call | solution.py:1126
  800.8 1.7 slice_dynamic-update-slice_fusion.11
  802.6 1.6 slice_dynamic-update-slice_fusion.10
  806.5 2.1 convolution_bitcast_fusion.1
  809.4 2.8 pad_maximum_fusion
  812.2 8.5 copy.25
  821.4 53.6 %shard_map.173 = (f32[96,1792]{1,0:T(8,128)}, f32[80,128]{1,0:T(8,128)}) custom-call(bf16[16,96,1792]{2,1,0:T(8,128)(2,1)} %bitcast.99, f32[80,128]{1,0:T(8,128)} %pad_maximum_fusion.6.x_ref), custom_call_target="tpu_custom_call" | custom-call | bytes 210000000 | tf_op jit(solution)/shard_map/pallas_call | solution.py:562
  878.3 1.9 slice_dynamic-update-slice_fusion.9
  880.1 1.6 slice_dynamic-update-slice_fusion.15
  881.9 1.7 slice_dynamic-update-slice_fusion.8
  886.0 0.9 add_convert_fusion
  886.8 1.9 maximum_convert_fusion.1
  888.7 4.9 maximum_convert_fusion
  893.6 1.1 bitcast_convert_fusion
  894.7 0.9 pad_maximum_fusion.2
  895.5 1.0 fusion.18
  896.5 0.9 copy.53
  (92 shorter events, 12.7 us)
Async XLA Ops:
  7.2 886.4 %reduce-scatter.2.cloned.1.call-start = ((), (), s32[]{:S(2)}) async-start(), calls=%async_computation.1 | async-start | bytes 5849088 | tf_op jit(solution)/shard_map/reduce_scatter | solution.py:1271
  181.0 5.0 copy-start.2
  195.5 4.4 copy-start
  195.5 4.7 copy-start.21
  199.9 5.9 copy-start.11
  384.9 13.9 %copy-start.3 = (bf16[8,128,1536]{2,1,0:T(8,128)(2,1)S(1)}, bf16[8,128,1536]{2,1,0:T(8,128)(2,1)}, u32[]{:S(2)}) copy-start(bf16[8,128,1536]{2,1,0:T(8,128)(2,1)} %get-tuple-element.57) | copy-start | bytes 9437188
  384.9 13.9 %copy-start.22 = (bf16[16,96,1152]{2,1,0:T(8,128)(2,1)S(1)}, bf16[16,96,1152]{2,1,0:T(8,128)(2,1)}, u32[]{:S(2)}) copy-start(bf16[16,96,1152]{2,1,0:T(8,128)(2,1)} %get-tuple-element.58) | copy-start | bytes 10616836
  398.8 8.8 copy-start.4
  413.3 5.6 copy-start.5
  413.3 15.3 %slice-start.2 = ((s8[7077888]{0:T(1024)(128)(4,1)}), s8[4194304]{0:T(1024)(128)(4,1)S(1)}, s32[]{:S(2)}) async-start(s8[7077888]{0:T(1024)(128)(4,1)} %bitcast.120), calls=%async_computation.4 | async-start | bytes 8388608
  418.9 9.6 %slice-start.3 = ((s8[7077888]{0:T(1024)(128)(4,1)}), s8[2883584]{0:T(1024)(128)(4,1)S(1)}, s32[]{:S(2)}) async-start(s8[7077888]{0:T(1024)(128)(4,1)} %bitcast.120), calls=%async_computation.5 | async-start | bytes 5767168
  629.4 2.4 copy-start.13
  629.4 2.4 copy-start.17
  652.4 12.1 %copy-start.6 = (bf16[1536,1024]{1,0:T(8,128)(2,1)S(1)}, bf16[1536,1024]{1,0:T(8,128)(2,1)}, u32[]{:S(2)}) copy-start(bf16[1536,1024]{1,0:T(8,128)(2,1)} %copy.21) | copy-start | bytes 9437188
  652.4 21.7 %slice-start = ((s8[7077888]{0:T(1024)(128)(4,1)}), s8[4194304]{0:T(1024)(128)(4,1)S(1)}, s32[]{:S(2)}) async-start(s8[7077888]{0:T(1024)(128)(4,1)} %bitcast.116), calls=%async_computation.2 | async-start | bytes 8388608
  664.5 9.7 %slice-start.1 = ((s8[7077888]{0:T(1024)(128)(4,1)}), s8[2883584]{0:T(1024)(128)(4,1)S(1)}, s32[]{:S(2)}) async-start(s8[7077888]{0:T(1024)(128)(4,1)} %bitcast.116), calls=%async_computation.3 | async-start | bytes 5767168
  683.1 121.1 %copy-start.19 = (f32[1,1536]{1,0:T(1,128)S(1)}, f32[1,1536]{1,0:T(1,128)}, u32[]{:S(2)}) copy-start(f32[1,1536]{1,0:T(1,128)} %get-tuple-element.82) | copy-start | bytes 18436
  683.2 121.8 %copy-start.18 = (f32[1,1536]{1,0:T(1,128)S(1)}, f32[1,1536]{1,0:T(1,128)}, u32[]{:S(2)}) copy-start(f32[1,1536]{1,0:T(1,128)} %get-tuple-element.84) | copy-start | bytes 18436
  683.2 122.5 %copy-start.20 = (f32[1,1024]{1,0:T(1,128)S(1)}, f32[1,1024]{1,0:T(1,128)}, u32[]{:S(2)}) copy-start(f32[1,1024]{1,0:T(1,128)} %get-tuple-element.86) | copy-start | bytes 12292
  683.2 123.3 %copy-start.12 = (bf16[2,128,1536]{2,1,0:T(8,128)(2,1)S(1)}, bf16[2,128,1536]{2,1,0:T(8,128)(2,1)}, u32[]{:S(2)}) copy-start(bf16[2,128,1536]{2,1,0:T(8,128)(2,1)} %get-tuple-element.77) | copy-start | bytes 2359300
  800.8 7.8 copy-start.8
  800.8 7.8 copy-start.16
  821.4 60.4 %copy-start.9 = (bf16[4,96,3456]{2,1,0:T(8,128)(2,1)S(1)}, bf16[4,96,3456]{2,1,0:T(8,128)(2,1)}, u32[]{:S(2)}) copy-start(bf16[4,96,3456]{2,1,0:T(8,128)(2,1)} %get-tuple-element.94) | copy-start | bytes 7962628
  877.7 5.9 copy-start.10
  883.5 2.4 copy-start.1
  883.5 2.4 copy-start.15
  888.7 6.0 copy-start.7
  893.6 2.9 copy-start.14
Sparse Core Ops, SparseCore 0:
  636.1 107.3 reduce-scatter.1

commit v5 on v4

--- a/solution.py
+++ b/solution.py
@@ -535,45 +535,6 @@
 
 def at_microseconds(time):
     return pl.CostEstimate(flops=0, transcendentals=0, bytes_accessed=time * 3500000)
-
-
-def last_kernel(size, bits, p_ref, x_ref, out_ref, sum_ref, *refs):
-    greet_all(size, ("t", *bits))
-    given, rest = in_groups(refs, [SCATTER_REFS, 4])
-    small = Total(size, ("t", *bits), x_ref, sum_ref, *rest)
-    steps = Scatter(size, bits, p_ref, out_ref, *given)
-    small.begin()
-    steps.begin()
-    for place in range(size):
-        steps.place(place)
-        if place <= len(bits):
-            small.pair(place)
-    for number in range(size, len(bits) + 1):
-        small.pair(number)
-    steps.finish()
-    small.finish()
-    steps.end()
-    small.end()
-
-
-def last(partial, x, size, bits, collective_id):
-    slots, rows, columns = partial.shape
-    number = len(bits) + 1
-    return pl.pallas_call(
-        functools.partial(last_kernel, size, bits),
-        out_shape=(jax.ShapeDtypeStruct((rows, columns), F32), jax.ShapeDtypeStruct(x.shape, F32)),
-        in_specs=[pl.BlockSpec(memory_space=pl.ANY), pl.BlockSpec(memory_space=pltpu.VMEM)],
-        out_specs=[pl.BlockSpec(memory_space=pltpu.VMEM)] * 2,
-        scratch_shapes=[
-            *scatter_scratch(size, bits, rows, columns),
-            pltpu.VMEM((number + 1, *x.shape), F32),
-            pltpu.VMEM((number + size - 1, *x.shape), F32),
-            pltpu.SemaphoreType.DMA((number + size - 1,)),
-            pltpu.SemaphoreType.DMA((number + size - 1,)),
-        ],
-        compiler_params=comm_params(collective_id),
-        cost_estimate=at_microseconds(60),
-    )(partial, x)
 
 
 class Attend:
@@ -850,7 +811,7 @@
 class AttendBack:
     def __init__(self, ins, outs, scratch, width, epsilon=1e-06):
         (self.g_ref, self.state_ref, self.middle_ref, self.ga_gain, self.gf_gain, self.cos_ref, self.sin_ref) = ins[:7]
-        (self.mask_ref, self.q_ref, self.k_ref, self.v_ref, self.lse_ref, self.far_w) = ins[7:]
+        (self.mask_ref, self.q_ref, self.k_ref, self.v_ref, self.lse_ref, self.xa_ref, self.o_ref, self.far_w) = ins[7:]
         (self.grad_ref, self.ga_ref, self.lin_ref, self.bias_ref, self.pa_ref, self.pf_ref) = outs
         (self.w_ref, self.w_sem, self.dk, self.dv, self.sum_buf, self.send_buf, self.land_buf) = scratch[:7]
         (self.send_sems, self.recv_sems) = scratch[7:]
@@ -961,6 +922,20 @@
         for where, part in self.projected(self.t):
             self.sum_buf[:, where] = part
 
+    def gradients(self):
+        step = self.slots // 4
+        early = (((0,), (0,)), ((), ()))
+        pairs = ((self.xa_ref, self.lin_ref, 0, self.width), (self.ga_ref, self.o_ref, self.width, self.q_width))
+        for left_ref, right_ref, low, count in pairs:
+            right = right_ref[...].reshape(2 * self.count, count)
+            for slot in range(0, self.slots, step):
+                where = slice(slot * self.few, (slot + step) * self.few)
+                left = left_ref[:, :, where].reshape(2 * self.count, step * self.few)
+                part = lax.dot_general(left, right, early, preferred_element_type=F32)
+                self.w_ref[slot : slot + step, :, low : low + count] = part.astype(LOW).reshape(
+                    step, self.few, count
+                )
+
     def finish(self):
         self.half_copy().wait_recv()
         d_xa = self.sum_buf[...] + self.land_buf[...].astype(F32)
@@ -1038,9 +1013,9 @@
 
 def back_kernel(size, bits, width, final, *refs):
     top, bottom = final
-    counts = [1, 1 if top else 0, 2, 13, 6, 1, 1 if top else 0, 0 if bottom else 1]
-    p_ref, branch_ref, wide, ins, outs, (blocks_ref,), branch_out, gm_out, refs = in_groups(
-        refs, counts + [len(refs)]
+    counts = [1, 1 if top else 0, 2, 15, 3 if bottom else 0, 6, 2, 1 if top else 0, 1]
+    p_ref, branch_ref, wide, ins, above, outs, (blocks_ref, attn_ref), branch_out, more_out, refs = (
+        in_groups(refs, counts + [len(refs)])
     )
     (dxf_ref,), dxf_scratch, gu_fold, dn_fold, done, sems, work_scratch, refs = in_groups(
         refs, [1, SCATTER_REFS, 7, 7, 2, 3, 9, len(refs)]
@@ -1049,13 +1024,18 @@
     rows = Scatter(size, ("t",), p_ref[0], dxf_ref, *dxf_scratch)
     blocks = Blocks(size, bits, *wide, blocks_ref, gu_fold, dn_fold, done, sems)
     work = AttendBack(ins, outs, work_scratch, width)
-    branch = onward = None
+    branch = None
     if top:
         branch_scratch, refs = in_groups(refs, [SCATTER_REFS, len(refs)])
         branch = Scatter(size, ("t",), branch_ref[0], branch_out[0], *branch_scratch)
     if not bottom:
-        gm_ref, *gm_sems = refs
-        onward = Gather(size, ("t",), gm_ref, gm_out[0], *gm_sems)
+        gm_ref, kept_sem, *gm_sems = refs
+        onward = Gather(size, ("t",), gm_ref, more_out[0], *gm_sems)
+        kept = pltpu.make_async_copy(work.w_ref, attn_ref, kept_sem)
+    else:
+        attn_scratch, (x_ref, *small_scratch) = in_groups(refs, [SCATTER_REFS, len(refs)])
+        final = Scatter(size, bits, work.w_ref, attn_ref, *attn_scratch)
+        small = Total(size, ("t", *bits), x_ref, more_out[0], *small_scratch)
     rows.begin()
     blocks.begin()
     work.prepare()
@@ -1089,7 +1069,32 @@
         branch.begin([2])
     work.own_half()
     blocks.send(3)
+    work.gradients()
+    if bottom:
+        final.begin()
+    else:
+        kept.start()
     grad = work.finish()
+    if bottom:
+        pa_above, pf_above, bias_above = above
+        x_ref[...] = jnp.zeros_like(x_ref)
+        x_ref[0:1, :] = work.pa_ref[...]
+        x_ref[1:2, :] = pa_above[...]
+        x_ref[2:3, :] = work.pf_ref[...]
+        x_ref[3:4, :] = pf_above[...]
+        for side in range(2):
+            mine = (work.t == side).astype(F32)
+            x_ref[4 + 2 * side : 5 + 2 * side, : work.width] = work.bias_ref[...] * mine
+            x_ref[5 + 2 * side : 6 + 2 * side, : work.width] = bias_above[...] * mine
+        small.begin()
+        for place in range(size):
+            final.place(place)
+            if place <= len(bits):
+                small.pair(place)
+        for number in range(size, len(bits) + 1):
+            small.pair(number)
+        final.finish()
+        small.finish()
     if not bottom:
         gm_ref[...] = grad.astype(LOW)
         onward.begin()
@@ -1109,17 +1114,21 @@
         onward.on_bits(3)
     if top:
         branch.finish()
-    for steps in (rows, blocks, work, branch, onward):
+    for steps in (rows, blocks, work, *((final, small) if bottom else (onward,)), branch):
         if steps is not None:
             steps.end()
-
-
-def back(partial, branch, gu, dn, ins, size, bits, width, bottom, collective_id):
+    if not bottom:
+        kept.wait()
+
+
+def back(partial, branch, gu, dn, ins, above, size, bits, width, collective_id):
     count, model = ins[1].shape
     length, q_width = ins[8].shape
     slots, few, wide = gu.shape
     narrow = dn.shape[2]
-    top = branch is not None
+    top, bottom = branch is not None, bool(above)
+    number = len(bits) + 1
+    weight = ins[14].shape
     held, far = pl.BlockSpec(memory_space=pltpu.VMEM), pl.BlockSpec(memory_space=pl.ANY)
     shape = jax.ShapeDtypeStruct
     rows_scratch = scatter_scratch(size, ("t",), count, model)
@@ -1133,11 +1142,12 @@
             shape((1, model), F32),
             shape((1, model), F32),
             shape((size, few, wide + narrow), LOW),
+            shape(weight[1:], F32) if bottom else shape(weight, LOW),
             *([shape((count, model), F32)] if top else []),
-            *([] if bottom else [shape((2 * size, count, model), LOW)]),
+            shape((8, model), F32) if bottom else shape((2 * size, count, model), LOW),
         ),
-        in_specs=[far] * (4 if top else 3) + [held] * 12 + [far],
-        out_specs=[held] * 6 + [far] + [held] * top + [far] * (not bottom),
+        in_specs=[far] * (4 if top else 3) + [held] * 14 + [far] + [held] * len(above),
+        out_specs=[held] * 6 + [far, held if bottom else far] + [held] * top + [held if bottom else far],
         scratch_shapes=[
             pltpu.VMEM((count, model), F32),
             *rows_scratch,
@@ -1148,7 +1158,7 @@
             pltpu.SemaphoreType.DMA((2,)),
             pltpu.SemaphoreType.DMA((2, size)),
             pltpu.SemaphoreType.DMA((2, size)),
-            pltpu.VMEM(ins[12].shape, LOW),
+            pltpu.VMEM(weight, LOW),
             pltpu.SemaphoreType.DMA,
             pltpu.VMEM((length, HD), F32),
             pltpu.VMEM((length, HD), F32),
@@ -1158,11 +1168,57 @@
             pltpu.SemaphoreType.DMA((2,)),
             pltpu.SemaphoreType.DMA((2,)),
             *(rows_scratch if top else []),
-            *([] if bottom else [pltpu.VMEM((count, model), LOW), *gather_semaphores(size, ("t",))]),
+            *(
+                [
+                    *scatter_scratch(size, bits, *weight[1:]),
+                    pltpu.VMEM((8, model), F32),
+                    pltpu.VMEM((number + 1, 8, model), F32),
+                    pltpu.VMEM((number + size - 1, 8, model), F32),
+                    pltpu.SemaphoreType.DMA((number + size - 1,)),
+                    pltpu.SemaphoreType.DMA((number + size - 1,)),
+                ]
+                if bottom
+                else [
+                    pltpu.VMEM((count, model), LOW),
+                    pltpu.SemaphoreType.DMA,
+                    *gather_semaphores(size, ("t",)),
+                ]
+            ),
         ],
         compiler_params=comm_params(collective_id),
         cost_estimate=at_microseconds(120),
-    )(partial, *([branch] if top else []), gu, dn, *ins)
+    )(partial, *([branch] if top else []), gu, dn, *ins, *above)
+
+
+def settle_kernel(half, width, *refs):
+    *blocks, attn_low, attn_high, gu_ref, dn_ref, qkv_ref, out_ref = refs
+    block = blocks[0].shape[2] // 3
+    for layer, ref in enumerate(blocks):
+        for line in range(LINE):
+            low = block_start(line, block, half)
+            skip = line * block - low
+            for part in range(2):
+                piece = ref[line, :, part * block + skip : (part + 1) * block].astype(F32)
+                gu_ref[layer, :, part * half + low + skip : part * half + low + block] = piece
+            dn_ref[layer, :, low + skip : low + block] = ref[line, :, 2 * block + skip :].astype(F32)
+    for layer, ref in enumerate((attn_low, attn_high)):
+        qkv_ref[layer] = ref[:, :width].astype(F32)
+        out_ref[layer] = ref[:, width:].astype(F32)
+
+
+def settle(blocks, attn, half, width):
+    few = attn[0].shape[0]
+    shape = jax.ShapeDtypeStruct
+    return pl.pallas_call(
+        functools.partial(settle_kernel, half, width),
+        out_shape=(
+            shape((2, few, 2 * half), F32),
+            shape((2, few, half), F32),
+            shape((2, few, width), F32),
+            shape((2, few, attn[0].shape[1] - width), F32),
+        ),
+        compiler_params=pltpu.CompilerParams(vmem_limit_bytes=56 * 2**20),
+    )(*blocks, *attn)
 
 
 def in_slots(partial, slots):
@@ -1175,16 +1231,6 @@
 
 def block_start(line, block, half):
     return min(line * block, half - block)
-
-
-def from_blocks(blocks, parts, half):
-    block = blocks.shape[2] // 3
-    pieces = []
-    for part in parts:
-        for line in range(LINE):
-            skip = line * block - block_start(line, block, half)
-            pieces.append(blocks[line, :, part * block + skip : (part + 1) * block])
-    return jnp.concatenate(pieces, axis=1).astype(F32)
 
 
 def local(
@@ -1222,8 +1268,6 @@
         (state, middle, xa_all, query, key, value, log_total, attended) = out[:8]
         xf_all, gu_w, down_w = (item.reshape(-1, item.shape[2]) for item in out[8:11])
         both_w = out[11]
-        xa_all = xa_all.reshape(length, -1)
-        attended = attended.reshape(length, -1)
         gate_up = jnp.dot(xf_all, gu_w, preferred_element_type=F32)
         gate = gate_up[:, :block]
         up = gate_up[:, block:]
@@ -1233,8 +1277,8 @@
             (state, xa_all, query, key, value, log_total, attended)
             + (middle, xf_all, gate, up, act, gu_w, down_w, both_w)
         )
-    grad, branch = cotangent, in_slots(partial, 2 * LINE)
-    grads_attn, grads_bias, grads_ga, grads_gf, grads_blocks = ([] for _ in range(5))
+    grad, branch, above = cotangent, in_slots(partial, 2 * LINE), []
+    grads_attn, grads_blocks = [], []
     for layer in reversed(range(layers)):
         (state_in, xa_all, query, key, value, log_total, attended) = saved[layer][:7]
         (middle, xf_all, gate, up, act, gu_w, down_w, both_w) = saved[layer][7:]
@@ -1250,58 +1294,35 @@
         partial = in_slots(contract_last(d_gu, gu_w, LOW), 2 * LINE)
         wide = (in_slots(d_gateup, d_gateup.shape[0] // rows), in_slots(d_down, d_down.shape[0] // rows))
         gains = (gain_attn[layer : layer + 1], gain_ffn[layer : layer + 1])
-        ins = (grad, state_in, middle, *gains, *tables, query, key, value, log_total, both_w)
-        out = back(partial, branch, *wide, ins, LINE, bits, qkv_width, layer == 0, 16 + layer)
-        (grad, ga_all, d_lin, d_bias, part_a, part_f, blocks), rest = out[:7], list(out[7:])
+        ins = (grad, state_in, middle, *gains, *tables, query, key, value, log_total, xa_all, attended, both_w)
+        out = back(
+            partial, branch, *wide, ins, above if layer == 0 else [], LINE, bits, qkv_width, 16 + layer
+        )
+        (grad, _, _, d_bias, part_a, part_f, blocks, d_attn), rest = out[:8], out[8:]
+        grads_blocks.append(blocks)
         if branch is not None:
-            output = (middle + rest.pop(0)).astype(LOW)
+            output = (middle + rest[0]).astype(LOW)
             branch = None
-        if rest:
-            gm_all = rest[0].reshape(-1, rest[0].shape[2])
-        grads_bias.append(d_bias[0])
-        grads_blocks.append(blocks)
-        d_lin, ga_all = d_lin.reshape(length, -1), ga_all.reshape(length, -1)
-        d_both = jnp.concatenate(
-            [contract_first(xa_all, d_lin, LOW), contract_first(ga_all, attended, LOW)], axis=1
-        )
-        if layer == 0:
-            d_both = in_slots(d_both, d_both.shape[0] // rows)
-        else:
-            grads_attn.append(
-                lax.psum_scatter(d_both, dp, scatter_dimension=0, tiled=True).astype(F32)
+        if layer > 0:
+            gm_all = rest[-1].reshape(-1, rest[-1].shape[2])
+            above = [part_a, part_f, d_bias]
+            d_attn = lax.psum_scatter(
+                d_attn.reshape(-1, d_attn.shape[2]), dp, scatter_dimension=0, tiled=True
             )
-        grads_ga.append(part_a[0])
-        grads_gf.append(part_f[0])
-
-    def ordered(items):
-        return jnp.stack(items[::-1], axis=0)
-
+        grads_attn.append(d_attn)
+    sums = rest[-1]
     side = lax.axis_index("t")
-    bias = ordered(grads_bias)
-    spread = jnp.where(
-        (jnp.arange(tensor_size) == side)[:, None, None], bias[None], jnp.zeros_like(bias)[None]
-    )
-    small = (ordered(grads_ga), ordered(grads_gf), spread)
-    flat = jnp.concatenate([item.reshape(-1, LANES) for item in small], axis=0)
-    last_attn, flat = last(d_both, flat, LINE, bits, 4)
-    grads_attn.append(last_attn)
-    full_ga, full_gf, full_bias = (
-        part.reshape(item.shape)
-        for part, item in zip(
-            jnp.split(flat, [small[0].size // LANES, 2 * small[0].size // LANES], axis=0), small
-        )
-    )
-    both = ordered(grads_attn)
+    d_gu_all, d_dn_all, d_qkv_all, d_out_all = settle(grads_blocks[::-1], grads_attn[::-1], half, qkv_width)
     return (
         output,
         grad,
-        full_ga,
-        full_gf,
-        both[:, :, :qkv_width],
-        take(full_bias, side, 0),
-        both[:, :, qkv_width:],
-        ordered([from_blocks(blocks, (0, 1), half) for blocks in grads_blocks]),
-        ordered([from_blocks(blocks, (2,), half) for blocks in grads_blocks]),
+        sums[0:2],
+        sums[2:4],
+        d_qkv_all,
+        lax.dynamic_slice_in_dim(sums, 4 + 2 * side, 2, 0)[:, :qkv_width],
+        d_out_all,
+        d_gu_all,
+        d_dn_all,
     )
 
 

time: 915 us -> 860 us (0.940)
  other arithmetic: 27 us -> 8.81 us
  local copies, waits for them, and re-layouts: 50.2 us -> 32.7 us
  matrix products: 114 us -> 103 us
    pallas_call x1, Pallas kernels: 53.6 us -> 7.43 us  [settle(): pl.pallas_call(functools.partial(settle_kernel, half, width), out_shape=(...]
    pallas_call x2, Pallas kernels: 309 us -> 349 us  [back(): pl.pallas_call(functools.partial(back_kernel, size, bits, width, (top, bo...]
    another operation x8 -> x0, other arithmetic: 11.8 us -> none  [ordered(): return jnp.stack(items[::-1], axis=0)]
    dot_general x8 -> x4, matrix products: 40.4 us -> 35.2 us  [contract_first(): lax.dot_general(left, right, (((0,), (0,)), ((), ())), preferred_element_...]
  transfers between devices with their start and end apart: 1 -> 1, of which waited for: 0 -> 0; matrix products, arithmetic and copies ran while one was open for 10% -> 6% of each run, Pallas kernels for 19% -> 18%
where the time goes in v5:
time: 860 us; the launch traced here: 852 us
  Pallas kernels  690 us (80%)
  matrix products  103 us (12%)
  local copies, waits for them, and re-layouts  32.7 us (4%)
  between operations  17.4 us (2%)
  other arithmetic  8.81 us (1%)
    pallas_call x2, Pallas kernels, back(): pl.pallas_call(functools.partial(back_kernel, size, bits, width, (top, bo...  349 us
    pallas_call x2, Pallas kernels, front(): pl.pallas_call(functools.partial(front_kernel, size, bits, block, half, l...  333 us
    dot_general x4, matrix products, contract_first(): lax.dot_general(left, right, (((0,), (0,)), ((), ())), preferred_element_...  35.2 us
    dot_general x4, matrix products, contract_last(): lax.dot_general(left, right, (((1,), (1,)), ((), ())), preferred_element_...  29.5 us
    dot_general x2, matrix products, local(): gate_up = jnp.dot(xf_all, gu_w, preferred_element_type=F32)  22.8 us
    dot_general x4, local copies, waits for them, and re-layouts, contract_first(): lax.dot_general(left, right, (((0,), (0,)), ((), ())), preferred_element_...  17.7 us
  transfers between devices with their start and end apart: 1, of which 0 were waited for; matrix products, arithmetic and copies ran while one was open for 6% of the time, Pallas kernels for 18%

profile of v5, /device:TPU:26, one launch (start us, length us, event | category | flops | bytes accessed | tf_op | source)
XLA Modules:
  0.0 851.6 jit_solution(13692228012303251432)
XLA Ops:
  7.2 0.0 reduce-scatter.2.cloned.1.call-start
  7.3 1.4 fusion.28
  11.2 2.6 convert_add_fusion
  13.8 0.5 multiply_sine_fusion
  14.4 0.8 pad_maximum_fusion.2.refs_5_.refs_9_.refs_8_
  15.1 0.8 fusion.19.refs_7_.refs_11_.refs_10_
  16.0 1.0 slice_bitcast_fusion
  17.0 1.0 slice_bitcast_fusion.2
  18.0 1.4 fusion.27
  19.4 0.8 negate_select_fusion.refs_6_.refs_10_.refs_9_
  20.1 1.4 fusion.25
  21.5 0.9 pad_maximum_fusion
  22.4 158.5 %shard_map.169 = (f32[128,1536]{1,0:T(8,128)}, f32[128,1536]{1,0:T(8,128)}, bf16[2,128,1536]{2,1,0:T(8,128)(2,1)}, bf16[256,768]{1,0:T(8,128)(2,1)}, bf16[256,12...) custom-call(bf16[128,1536]{1,0:T(8,128)(2,1)} %refs_0_.1, ...), custom_call_target="tpu_custom_call" | custom-call | bytes 525000000 | tf_op jit(solution)/shard_map/pallas_call | solution.py:771
  180.9 5.0 copy.20
  185.9 9.5 %fusion.29 = f32[1024,2304]{1,0:T(8,128)S(1)} fusion(bf16[1024,1536]{1,0:T(8,128)(2,1)S(1)} %bitcast.81, bf16[1536,2304]{1,0:T(8,128)(2,1)} %bitcast.93), kind=kOutput, calls=%fused_computation.61 | convolution fusion | flops 7247757312 | bytes 19660800 | tf_op jit(solution)/shard_map/dot_general | solution.py:1271
  195.5 1.6 select_convert_fusion.5
  197.1 2.8 copy-done
  199.9 0.2 copy-done.14
  200.1 5.6 fusion.30.refs_1_
  205.7 174.4 %shard_map.170 = (f32[128,1536]{1,0:T(8,128)}, f32[128,1536]{1,0:T(8,128)}, bf16[2,128,1536]{2,1,0:T(8,128)(2,1)}, bf16[256,768]{1,0:T(8,128)(2,1)}, bf16[256,12...) custom-call(f32[128,1536]{1,0:T(8,128)} %get-tuple-element.50.refs_0, ...), custom_call_target="tpu_custom_call" | custom-call | bytes 525000000 | tf_op jit(solution)/shard_map/pallas_call | solution.py:771
  380.2 0.0 copy-start.7
  380.2 4.8 copy.19
  385.0 13.2 %fusion.31 = f32[1024,2304]{1,0:T(8,128)} fusion(bf16[1024,1536]{1,0:T(8,128)(2,1)S(1)} %bitcast.88, bf16[1536,2304]{1,0:T(8,128)(2,1)} %bitcast.97), kind=kOutput, calls=%fused_computation.63 | convolution fusion | flops 7247757312 | bytes 19660800 | tf_op jit(solution)/shard_map/dot_general | solution.py:1271
  398.2 8.8 %select_convert_fusion.4 = (bf16[1024,1152]{1,0:T(8,128)(2,1)S(1)}, bf16[1024,1152]{1,0:T(8,128)(2,1)S(1)}, bf16[1024,1152]{1,0:T(8,128)(2,1)S(1)}) fusion(f32[1024,2304]{1,0:T(8,128)} %fusion.31, pred[1152]{0:T(1024)(128)(4,1)S(1)} %iota_compare_fusion.1, bf16[1024,1536]{1,0:T(8,128)(2,1)S(1)} %bitcast.83, bf16[1536,1152]{1,0:T(8,128)(2,1)S(1)} %bitcast.103), kind=kOutput, calls=%fused_computation.20 | convolution fusion | flops 3646291968 | bytes 23200896 | tf_op jit(solution)/shard_map/dot_general | solution.py:1286
  407.0 0.0 copy-done.6
  407.0 5.7 fusion.16.refs_3_
  412.7 5.8 fusion.32.refs_1_
  418.5 9.6 %fusion.4.refs_2_ = bf16[16,96,2304]{2,1,0:T(8,128)(2,1)} fusion(bf16[16,96,1024]{2,1,0:T(8,128)(2,1)S(1)} %bitcast.89, bf16[1024,1152]{1,0:T(8,128)(2,1)S(1)} %get-tuple-element.94, bf16[1024,1152]{1,0:T(8,128)(2,1)S(1)} %get-tuple-element.93), kind=kOutput, calls=%fused_computation.5 | convolution fusion | flops 7257194496 | bytes 14942208 | tf_op jit(solution)/shard_map/dot_general | solution.py:50
  428.1 0.0 slice-done.5
  428.1 9.0 %fusion.refs_0_ = bf16[8,128,1536]{2,1,0:T(8,128)(2,1)} fusion(bf16[1536,2304,1]{1,0,2:T(8,128)(2,1)S(1)} %bitcast.100, bf16[8,128,1152]{2,1,0:T(8,128)(2,1)S(1)} %bitcast.106, bf16[8,128,1152]{2,1,0:T(8,128)(2,1)S(1)} %bitcast.105), kind=kOutput, calls=%fused_computation | convolution fusion | flops 7257194496 | bytes 14942208 | tf_op jit(solution)/shard_map/dot_general | solution.py:46
  437.1 192.3 %shard_map.171 = (f32[128,1536]{1,0:T(8,128)}, bf16[2,128,1536]{2,1,0:T(8,128)(2,1)}, bf16[2,128,1024]{2,1,0:T(8,128)(2,1)}, f32[1,1024]{1,0:T(1,128)}, f32[1,15...) custom-call(bf16[8,128,1536]{2,1,0:T(8,128)(2,1)} %fusion.refs_0_, ...), custom_call_target="tpu_custom_call" | custom-call | bytes 420000000 | tf_op jit(solution)/shard_map/pallas_call | solution.py:1135
  629.4 0.0 reduce-scatter.2.cloned.1.call-update
  629.5 1.9 copy-done.4
  631.3 2.9 copy.22
  634.3 5.0 copy.21
  639.3 0.0 copy-start.5
  639.3 8.7 %fusion.14.refs_2_ = bf16[16,96,1152]{2,1,0:T(8,128)(2,1)} fusion(bf16[16,96,1024]{2,1,0:T(8,128)(2,1)} %bitcast.91, bf16[1024,1152]{1,0:T(8,128)(2,1)S(1)} %copy-done.11), kind=kOutput, calls=%fused_computation.24 | convolution fusion | flops 3623878656 | bytes 9043968 | tf_op jit(solution)/shard_map/dot_general | solution.py:50
  648.1 0.0 copy-start.9
  648.1 0.0 slice-start.3
  648.1 6.9 select_convert_fusion.1
  654.9 11.2 %fusion.11.refs_1_ = bf16[16,96,2304]{2,1,0:T(8,128)(2,1)} fusion(bf16[16,96,1024]{2,1,0:T(8,128)(2,1)S(1)} %bitcast.90, bf16[1024,1152]{1,0:T(8,128)(2,1)} %get-tuple-element.92, bf16[1024,1152]{1,0:T(8,128)(2,1)S(1)} %get-tuple-element.91), kind=kOutput, calls=%fused_computation.13 | convolution fusion | flops 7257194496 | bytes 14942208 | tf_op jit(solution)/shard_map/dot_general | solution.py:50
  666.1 9.1 %fusion.7.refs_0_ = bf16[8,128,1536]{2,1,0:T(8,128)(2,1)} fusion(bf16[1536,2304,1]{1,0,2:T(8,128)(2,1)S(1)} %bitcast.96, bf16[8,128,1152]{2,1,0:T(8,128)(2,1)S(1)} %bitcast.108, bf16[8,128,1152]{2,1,0:T(8,128)(2,1)S(1)} %bitcast.107), kind=kOutput, calls=%fused_computation.8 | convolution fusion | flops 7257194496 | bytes 14942208 | tf_op jit(solution)/shard_map/dot_general | solution.py:46
  675.3 156.9 %shard_map.172 = (f32[128,1536]{1,0:T(8,128)}, bf16[2,128,1536]{2,1,0:T(8,128)(2,1)}, bf16[2,128,1024]{2,1,0:T(8,128)(2,1)}, f32[1,1024]{1,0:T(1,128)}, f32[1,15...) custom-call(bf16[8,128,1536]{2,1,0:T(8,128)(2,1)} %fusion.7.refs_0_,, ...), custom_call_target="tpu_custom_call" | custom-call | bytes 420000000 | tf_op jit(solution)/shard_map/pallas_call | solution.py:1135
  832.2 1.4 constant_dynamic-slice_fusion
  833.6 1.5 fusion.24
  835.1 0.8 add_convert_fusion
  835.9 7.4 shard_map.173
  843.4 0.9 copy.24
  (48 shorter events, 0.1 us)
Async XLA Ops:
  7.2 828.7 %reduce-scatter.2.cloned.1.call-start = ((), (), s32[]{:S(2)}) async-start(), calls=%async_computation.1 | async-start | bytes 5849088 | tf_op jit(solution)/shard_map/reduce_scatter | solution.py:1309
  180.9 5.0 copy-start.2
  195.5 4.4 copy-start
  195.5 4.7 copy-start.14
  199.9 5.9 copy-start.10
  380.2 4.8 copy-start.7
  385.0 13.3 %copy-start.3 = (bf16[8,128,1536]{2,1,0:T(8,128)(2,1)S(1)}, bf16[8,128,1536]{2,1,0:T(8,128)(2,1)}, u32[]{:S(2)}) copy-start(bf16[8,128,1536]{2,1,0:T(8,128)(2,1)} %get-tuple-element.55) | copy-start | bytes 9437188
  385.0 13.3 %copy-start.16 = (bf16[16,96,1152]{2,1,0:T(8,128)(2,1)S(1)}, bf16[16,96,1152]{2,1,0:T(8,128)(2,1)}, u32[]{:S(2)}) copy-start(bf16[16,96,1152]{2,1,0:T(8,128)(2,1)} %get-tuple-element.56) | copy-start | bytes 10616836
  398.2 8.8 %copy-start.6 = (bf16[1536,1024]{1,0:T(8,128)(2,1)S(1)}, bf16[1536,1024]{1,0:T(8,128)(2,1)}, u32[]{:S(2)}) copy-start(bf16[1536,1024]{1,0:T(8,128)(2,1)} %copy.20) | copy-start | bytes 9437188
  412.7 5.8 copy-start.8
  412.7 15.4 %slice-start.5 = ((s8[7077888]{0:T(1024)(128)(4,1)}), s8[4194304]{0:T(1024)(128)(4,1)S(1)}, s32[]{:S(2)}) async-start(s8[7077888]{0:T(1024)(128)(4,1)} %bitcast.98), calls=%async_computation.7 | async-start | bytes 8388608
  418.5 9.6 %slice-start.6 = ((s8[7077888]{0:T(1024)(128)(4,1)}), s8[2883584]{0:T(1024)(128)(4,1)S(1)}, s32[]{:S(2)}) async-start(s8[7077888]{0:T(1024)(128)(4,1)} %bitcast.98), calls=%async_computation.8 | async-start | bytes 5767168
  629.4 1.9 copy-start.4
  634.3 5.0 copy-start.11
  634.3 13.8 %slice-start = ((s8[9437184]{0:T(1024)(128)(4,1)}), s8[1048576]{0:T(1024)(128)(4,1)S(1)}, s32[]{:S(2)}) async-start(s8[9437184]{0:T(1024)(128)(4,1)} %bitcast.77), calls=%async_computation.2 | async-start | bytes 2097152
  639.3 8.8 %slice-start.1 = ((s8[9437184]{0:T(1024)(128)(4,1)}), s8[4194304]{0:T(1024)(128)(4,1)S(1)}, s32[]{:S(2)}) async-start(s8[9437184]{0:T(1024)(128)(4,1)} %bitcast.77), calls=%async_computation.3 | async-start | bytes 8388608
  639.3 8.8 %slice-start.2 = ((s8[9437184]{0:T(1024)(128)(4,1)}), s8[4194304]{0:T(1024)(128)(4,1)S(1)}, s32[]{:S(2)}) async-start(s8[9437184]{0:T(1024)(128)(4,1)} %bitcast.77), calls=%async_computation.4 | async-start | bytes 8388608
  639.3 8.8 %copy-start.5 = (bf16[8,128,1536]{2,1,0:T(8,128)(2,1)S(1)}, bf16[8,128,1536]{2,1,0:T(8,128)(2,1)}, u32[]{:S(2)}) copy-start(bf16[8,128,1536]{2,1,0:T(8,128)(2,1)} %get-tuple-element.68) | copy-start | bytes 9437188
  639.3 8.8 %copy-start.15 = (bf16[16,96,1152]{2,1,0:T(8,128)(2,1)S(1)}, bf16[16,96,1152]{2,1,0:T(8,128)(2,1)}, u32[]{:S(2)}) copy-start(bf16[16,96,1152]{2,1,0:T(8,128)(2,1)} %get-tuple-element.53) | copy-start | bytes 10616836
  648.1 6.9 copy-start.9
  648.1 18.1 %slice-start.3 = ((s8[7077888]{0:T(1024)(128)(4,1)}), s8[2883584]{0:T(1024)(128)(4,1)S(1)}, s32[]{:S(2)}) async-start(s8[7077888]{0:T(1024)(128)(4,1)} %bitcast.94), calls=%async_computation.5 | async-start | bytes 5767168
  654.9 11.2 %slice-start.4 = ((s8[7077888]{0:T(1024)(128)(4,1)}), s8[4194304]{0:T(1024)(128)(4,1)S(1)}, s32[]{:S(2)}) async-start(s8[7077888]{0:T(1024)(128)(4,1)} %bitcast.94), calls=%async_computation.6 | async-start | bytes 8388608
  654.9 11.2 %copy-start.17 = (bf16[1024,1152]{1,0:T(8,128)(2,1)S(1)}, bf16[1024,1152]{1,0:T(8,128)(2,1)}, u32[]{:S(2)}) copy-start(bf16[1024,1152]{1,0:T(8,128)(2,1)} %get-tuple-element.92) | copy-start | bytes 7077892
  675.3 159.8 %copy-start.1 = (f32[128,1536]{1,0:T(8,128)S(1)}, f32[128,1536]{1,0:T(8,128)}, u32[]{:S(2)}) copy-start(f32[128,1536]{1,0:T(8,128)} %get-tuple-element.54.refs_6_) | copy-start | bytes 2359300
  675.3 159.8 %copy-start.13 = (f32[128,1536]{1,0:T(8,128)S(1)}, f32[128,1536]{1,0:T(8,128)}, u32[]{:S(2)}) copy-start(f32[128,1536]{1,0:T(8,128)} %get-tuple-element.67) | copy-start | bytes 2359300
  832.2 11.2 %copy-start.12 = (f32[128,1536]{1,0:T(8,128)S(1)}, f32[128,1536]{1,0:T(8,128)}, u32[]{:S(2)}) copy-start(f32[128,1536]{1,0:T(8,128)} %get-tuple-element.130) | copy-start | bytes 2359300
Sparse Core Ops, SparseCore 0:
  629.6 106.7 reduce-scatter.1

commit v6 on v5

--- a/solution.py
+++ b/solution.py
@@ -325,6 +325,8 @@
         self.mine = [lax.axis_index(bit) for bit in bits]
 
     def line(self, place):
+        if self.order is None:
+            return relay_line(self.z, place, self.size)
         return lax.rem(self.z + self.order[place], self.size)
 
     def index(self, place, stage, variant):
@@ -402,6 +404,14 @@
     ]
 
 
+def relay_line(z, place, size):
+    order = []
+    for line in range(size):
+        others = sorted((other for other in range(size) if other != line), key=lambda other: -abs(other - line))
+        order.append([*others, line])
+    return sum(jnp.where(z == line, order[line][place], 0) for line in range(size))
+
+
 class Scatter:
     def __init__(self, size, bits, p_ref, out_ref, line_out, line_in, line_send, line_recv, *fold):
         order = list(range(1, size)) + [0]
@@ -444,12 +454,78 @@
             self.line_copy(place).wait_send()
 
 
-def scatter_scratch(size, bits, rows, columns):
+class Relay:
+    def __init__(self, size, bits, p_ref, out_ref, line_out, line_in, line_send, line_recv, *fold):
+        self.fold = Fold(size, bits, None, p_ref, *fold)
+        self.size, self.out_ref, self.z = size, out_ref, lax.axis_index("z")
+        self.line_out, self.line_in, self.line_send, self.line_recv = line_out, line_in, line_send, line_recv
+
+    def line_copy(self, place, line):
+        right = (line > self.z).astype(jnp.int32)
+        slot = (1 - right) * (self.size - 1) + jnp.abs(line - self.z) - 1
+        return pltpu.make_async_remote_copy(
+            src_ref=self.line_out.at[place],
+            dst_ref=self.line_in.at[slot],
+            send_sem=self.line_send.at[place],
+            recv_sem=self.line_recv.at[slot],
+            device_id={"z": self.z + 2 * right - 1},
+            device_id_type=MESH,
+        )
+
+    def landed(self, slot):
+        pltpu.make_async_remote_copy(
+            src_ref=self.line_in.at[slot],
+            dst_ref=self.line_in.at[slot],
+            send_sem=self.line_send.at[0],
+            recv_sem=self.line_recv.at[slot],
+            device_id={"z": lax.rem(self.z + 1, self.size)},
+            device_id_type=MESH,
+        ).wait_recv()
+
+    def done(self, place, total):
+        if place == self.size - 1:
+            self.out_ref[...] = total
+            return
+        line = self.fold.line(place)
+        right = line > self.z
+        self.line_out[place] = total.astype(LOW)
+        slot = (1 - right.astype(jnp.int32)) * (self.size - 1) + jnp.abs(line - self.z)
+
+        @pl.when(jnp.where(right, self.z > 0, self.z < self.size - 1))
+        def _():
+            self.landed(slot)
+            self.line_out[place] = (total + self.line_in[slot].astype(F32)).astype(LOW)
+
+        self.line_copy(place, line).start()
+
+    def begin(self, places=None):
+        self.fold.begin(places)
+
+    def place(self, place):
+        for stage in reversed(range(self.fold.count)):
+            self.fold.stage(place, stage, self.done)
+
+    def finish(self):
+        for slot, there in ((0, self.z > 0), (self.size - 1, self.z < self.size - 1)):
+
+            @pl.when(there)
+            def _(slot=slot):
+                self.landed(slot)
+                self.out_ref[...] += self.line_in[slot].astype(F32)
+
+    def end(self):
+        self.fold.end()
+        for place in range(self.size - 1):
+            self.line_copy(place, self.fold.line(place)).wait_send()
+
+
+def scatter_scratch(size, bits, rows, columns, relay=False):
+    lands = (size - 1) * (2 if relay else 1)
     return [
         pltpu.VMEM((size - 1, rows, columns), LOW),
-        pltpu.VMEM((size - 1, rows, columns), LOW),
+        pltpu.VMEM((lands, rows, columns), LOW),
         pltpu.SemaphoreType.DMA((size - 1,)),
-        pltpu.SemaphoreType.DMA((size - 1,)),
+        pltpu.SemaphoreType.DMA((lands,)),
         *fold_scratch(size, bits, rows, columns),
     ]
 
@@ -656,102 +732,98 @@
 
 def front_kernel(size, bits, block, half, layer, width, *refs):
     first = layer == 0
-    inputs, outs, refs = in_groups(refs, [11, 13 if first else 12, len(refs)])
+    inputs, outs, refs = in_groups(refs, [11, 13 if first else 11, len(refs)])
     (x_ref, more_ref, ga_ref, gf_ref, bias_ref, cos_ref, sin_ref, mask_ref, at_ref, gu_ref, dn_ref) = inputs
-    xf_out, gu_out, dn_out, at_out = outs[8:12]
-    (w_ref, xf_ref, at_sem), pair, at_sems, feed_sems, rows_sems, rest = in_groups(
-        refs, [3, 4, 4, 4, 4, len(refs)]
-    )
+    xf_out, gu_out, dn_out = outs[8:11]
+    (w_ref, xf_ref, at_sem), pair, feed_sems, rows_sems, rest = in_groups(refs, [3, 4, 4, 4, len(refs)])
     greet_all(size, ("t", *bits))
     work = Attend(
         x_ref, ga_ref, bias_ref, cos_ref, sin_ref, mask_ref, w_ref, outs[:8], pair, width
     )
-    attention = Gather(size, bits, at_ref, w_ref, *at_sems)
     feed = Exchange(
         size, bits, block, half, gu_ref.at[layer], dn_ref.at[layer], gu_out, dn_out, feed_sems
     )
     rows = Gather(size, ("t",), xf_ref, xf_out, *rows_sems)
-    kept = pltpu.make_async_copy(w_ref, at_out, at_sem)
     if first:
-        side = Gather(size, ("t",), more_ref, outs[12], *rest)
+        at_sems, next_sems = in_groups(rest, [4, 4])
+        attention = Gather(size, bits, at_ref, w_ref, *at_sems)
+        ahead = Gather(size, bits, more_ref, outs[12], *next_sems)
+        moved = pltpu.make_async_copy(w_ref, outs[11], at_sem)
         attention.begin()
-        side.begin()
         feed.begin()
         work.begin(x_ref[...].astype(F32))
         attention.step(1)
-        side.step(1)
         attention.step(2)
         attention.on_bits(0)
-        side.on_bits(0)
-        side.step(2)
+        attention.step(3)
         feed.send(1)
-        attention.step(3)
         attention.on_bits(1)
-        side.on_bits(1)
-        side.step(3)
-        feed.on_bits(0)
-        attention.on_bits(2)
-        feed.sent(1)
-        feed.send(3)
-        feed.step(1)
-        attention.on_bits(3)
-        attention.settle()
-        work.keys()
-        work.heads(0)
-        side.on_bits(2)
-        side.on_bits(3)
-    else:
-        total_ref, *rest = rest
-        side = Scatter(size, ("t",), more_ref, total_ref, *rest)
-        attention.begin()
-        side.begin()
-        feed.begin()
-        side.place(0)
-        attention.step(1)
-        side.place(1)
-        attention.step(2)
-        attention.on_bits(0)
-        side.place(2)
-        attention.step(3)
-        attention.on_bits(1)
-        side.place(3)
-        feed.send(1)
         attention.on_bits(2)
         attention.on_bits(3)
         attention.settle()
-        side.finish()
-        work.begin(x_ref[...] + total_ref[...])
+        moved.start()
         feed.on_bits(0)
         feed.sent(1)
         feed.send(3)
         feed.step(1)
-        work.keys()
-        work.heads(0)
-    kept.start()
+        steps = (attention, ahead)
+    else:
+        total_ref, *rest = rest
+        side = Scatter(size, ("t",), more_ref, total_ref, *rest)
+        moved = pltpu.make_async_copy(at_ref, w_ref, at_sem)
+        moved.start()
+        side.begin()
+        feed.begin()
+        for place in range(size):
+            side.place(place)
+        feed.send(1)
+        side.finish()
+        work.begin(x_ref[...] + total_ref[...])
+        moved.wait()
+        feed.on_bits(0)
+        feed.sent(1)
+        feed.send(3)
+        feed.step(1)
+        steps = (side,)
+    work.keys()
+    work.heads(0)
+    work.heads(2)
+    work.heads(4)
+    work.other_half()
+    work.own_half()
     feed.sent(3)
     feed.send(2)
     feed.step(3)
     feed.on_bits(1)
-    work.heads(2)
-    work.heads(4)
-    work.other_half()
-    work.own_half()
     work.finish(gf_ref, xf_ref)
     rows.begin()
+    if first:
+        ahead.begin()
     rows.step(1)
     rows.on_bits(0)
+    if first:
+        ahead.step(1)
     rows.step(2)
     feed.sent(2)
     feed.step(2)
     rows.on_bits(1)
+    if first:
+        ahead.on_bits(0)
     feed.on_bits(3)
     rows.step(3)
+    if first:
+        ahead.step(2)
     rows.on_bits(2)
     feed.on_bits(2)
     rows.on_bits(3)
-    kept.wait()
-    for steps in (attention, side, feed, work, rows):
-        steps.end()
+    if first:
+        ahead.on_bits(1)
+        ahead.step(3)
+        ahead.on_bits(2)
+        ahead.on_bits(3)
+        moved.wait()
+    for item in (*steps, feed, work, rows):
+        item.end()
 
 
 def front(x, more, gains, bias, tables, at, gu, dn, layer, size, bits, block, width, collective_id):
@@ -759,12 +831,13 @@
     count, model = x.shape
     few, half = dn.shape[1:]
     length = 2 * count
-    q_width = at.shape[1] - width
+    q_width = at.shape[-1] - width
     first = layer == 0
     held, far = pl.BlockSpec(memory_space=pltpu.VMEM), pl.BlockSpec(memory_space=pl.ANY)
     shape = jax.ShapeDtypeStruct
+    weight = (slots, few, at.shape[-1])
     more_scratch = (
-        gather_semaphores(size, ("t",))
+        gather_semaphores(size, bits) * 2
         if first
         else [pltpu.VMEM((count, model), F32), *scatter_scratch(size, ("t",), count, model)]
     )
@@ -782,20 +855,18 @@
             shape((2 * size, count, model), LOW),
             shape((slots, few, 2 * block), LOW),
             shape((slots, few, block), LOW),
-            shape((slots, few, at.shape[1]), LOW),
-            *([shape((2 * size, count, model), LOW)] if first else []),
+            *([shape(weight, LOW)] * 2 if first else []),
         ),
         in_specs=[held, far] + [held] * 6 + [far] * 3,
-        out_specs=[held] * 8 + [far] * (5 if first else 4),
+        out_specs=[held] * 8 + [far] * (5 if first else 3),
         scratch_shapes=[
-            pltpu.VMEM((slots, few, at.shape[1]), LOW),
+            pltpu.VMEM(weight, LOW),
             pltpu.VMEM((count, model), LOW),
             pltpu.SemaphoreType.DMA,
             pltpu.VMEM((count, model), LOW),
             pltpu.VMEM((count, model), LOW),
             pltpu.SemaphoreType.DMA((2,)),
             pltpu.SemaphoreType.DMA((2,)),
-            *gather_semaphores(size, bits),
             pltpu.SemaphoreType.DMA((3,)),
             pltpu.SemaphoreType.DMA((size - 1, 3)),
             pltpu.SemaphoreType.DMA((size, 2 ** len(bits), len(bits), 3)),
@@ -951,8 +1022,8 @@
 
 
 class Blocks:
-    def __init__(self, size, bits, gu_ref, dn_ref, out_ref, gu_fold, dn_fold, done, sems):
-        self.size, self.out_ref = size, out_ref
+    def __init__(self, size, bits, gu_ref, dn_ref, outs, gu_fold, dn_fold, done, sems):
+        self.size, self.outs, self.sending = size, outs, len(outs) == 1
         order = list(range(1, size)) + [0]
         self.folds = [Fold(size, bits, order, gu_ref, *gu_fold), Fold(size, bits, order, dn_ref, *dn_fold)]
         self.done = done
@@ -960,9 +1031,11 @@
         self.width, self.narrow = gu_ref.shape[2], dn_ref.shape[2]
         self.z = lax.axis_index("z")
 
+    def columns(self, number):
+        return pl.ds(*((0, self.width), (self.width, self.narrow))[number])
+
     def landing(self, number, slot):
-        low, count = ((0, self.width), (self.width, self.narrow))[number]
-        return self.out_ref.at[slot, :, pl.ds(low, count)]
+        return self.outs[0].at[slot, :, self.columns(number)]
 
     def line_copy(self, number, place, slot):
         return pltpu.make_async_remote_copy(
@@ -974,9 +1047,14 @@
             device_id_type=MESH,
         )
 
-    def own_copy(self, number):
+    def own_copy(self, number, place):
+        landing = (
+            self.landing(number, self.z)
+            if self.sending
+            else self.outs[place].at[:, self.columns(number)]
+        )
         return pltpu.make_async_copy(
-            self.done[number].at[self.size - 1], self.landing(number, self.z), self.own_sems.at[number]
+            self.done[number].at[place], landing, self.own_sems.at[number, place]
         )
 
     def begin(self):
@@ -993,28 +1071,29 @@
 
             def keep(place, total, number=number):
                 self.done[number][place] = total.astype(LOW)
-                if place < self.size - 1:
+                if self.sending and place < self.size - 1:
                     self.line_copy(number, place, self.z).start()
                 else:
-                    self.own_copy(number).start()
+                    self.own_copy(number, place).start()
 
             fold.stage(place, 0, keep)
 
     def end(self):
         for number, fold in enumerate(self.folds):
-            for offset in range(1, self.size):
-                slot = lax.rem(self.z - offset + self.size, self.size)
+            for place in range(self.size):
+                if not self.sending or place == self.size - 1:
+                    self.own_copy(number, place).wait()
+                    continue
+                slot = lax.rem(self.z - place - 1 + self.size, self.size)
                 self.line_copy(number, 0, slot).wait_recv()
-            for place in range(self.size - 1):
                 self.line_copy(number, place, self.z).wait_send()
-            self.own_copy(number).wait()
             fold.end()
 
 
 def back_kernel(size, bits, width, final, *refs):
     top, bottom = final
-    counts = [1, 1 if top else 0, 2, 15, 3 if bottom else 0, 6, 2, 1 if top else 0, 1]
-    p_ref, branch_ref, wide, ins, above, outs, (blocks_ref, attn_ref), branch_out, more_out, refs = (
+    counts = [1, 1 if top else 0, 2, 15, 3 if bottom else 0, 6, 1 if bottom else size, 1, 1 if top else 0, 1]
+    p_ref, branch_ref, wide, ins, above, outs, folded, (attn_ref,), branch_out, more_out, refs = (
         in_groups(refs, counts + [len(refs)])
     )
     (dxf_ref,), dxf_scratch, gu_fold, dn_fold, done, sems, work_scratch, refs = in_groups(
@@ -1022,12 +1101,12 @@
     )
     greet_all(size, ("t", *bits))
     rows = Scatter(size, ("t",), p_ref[0], dxf_ref, *dxf_scratch)
-    blocks = Blocks(size, bits, *wide, blocks_ref, gu_fold, dn_fold, done, sems)
+    blocks = Blocks(size, bits, *wide, folded, gu_fold, dn_fold, done, sems)
     work = AttendBack(ins, outs, work_scratch, width)
     branch = None
     if top:
         branch_scratch, refs = in_groups(refs, [SCATTER_REFS, len(refs)])
-        branch = Scatter(size, ("t",), branch_ref[0], branch_out[0], *branch_scratch)
+        branch = Relay(size, ("t",), branch_ref[0], branch_out[0], *branch_scratch)
     if not bottom:
         gm_ref, kept_sem, *gm_sems = refs
         onward = Gather(size, ("t",), gm_ref, more_out[0], *gm_sems)
@@ -1132,6 +1211,7 @@
     held, far = pl.BlockSpec(memory_space=pltpu.VMEM), pl.BlockSpec(memory_space=pl.ANY)
     shape = jax.ShapeDtypeStruct
     rows_scratch = scatter_scratch(size, ("t",), count, model)
+    branch_scratch = scatter_scratch(size, ("t",), count, model, relay=True)
     return pl.pallas_call(
         functools.partial(back_kernel, size, bits, width, (top, bottom)),
         out_shape=(
@@ -1141,13 +1221,19 @@
             shape((1, width), F32),
             shape((1, model), F32),
             shape((1, model), F32),
-            shape((size, few, wide + narrow), LOW),
+            *(
+                [shape((size, few, wide + narrow), LOW)]
+                if bottom
+                else [shape((few, wide + narrow), LOW)] * size
+            ),
             shape(weight[1:], F32) if bottom else shape(weight, LOW),
             *([shape((count, model), F32)] if top else []),
             shape((8, model), F32) if bottom else shape((2 * size, count, model), LOW),
         ),
         in_specs=[far] * (4 if top else 3) + [held] * 14 + [far] + [held] * len(above),
-        out_specs=[held] * 6 + [far, held if bottom else far] + [held] * top + [held if bottom else far],
+        out_specs=[held] * 6
+        + ([far, held] if bottom else [far] * (size + 1))
+        + [held] * top + [held if bottom else far],
         scratch_shapes=[
             pltpu.VMEM((count, model), F32),
             *rows_scratch,
@@ -1155,9 +1241,7 @@
             *fold_scratch(size, bits, few, narrow),
             pltpu.VMEM((size, few, wide), LOW),
             pltpu.VMEM((size, few, narrow), LOW),
-            pltpu.SemaphoreType.DMA((2,)),
-            pltpu.SemaphoreType.DMA((2, size)),
-            pltpu.SemaphoreType.DMA((2, size)),
+            *([pltpu.SemaphoreType.DMA((2, size))] * 3),
             pltpu.VMEM(weight, LOW),
             pltpu.SemaphoreType.DMA,
             pltpu.VMEM((length, HD), F32),
@@ -1167,7 +1251,7 @@
             pltpu.VMEM((count, model), LOW),
             pltpu.SemaphoreType.DMA((2,)),
             pltpu.SemaphoreType.DMA((2,)),
-            *(rows_scratch if top else []),
+            *(branch_scratch if top else []),
             *(
                 [
                     *scatter_scratch(size, bits, *weight[1:]),
@@ -1186,27 +1270,39 @@
             ),
         ],
         compiler_params=comm_params(collective_id),
-        cost_estimate=at_microseconds(120),
+        cost_estimate=at_microseconds(5 if bottom else 150),
     )(partial, *([branch] if top else []), gu, dn, *ins, *above)
 
 
 def settle_kernel(half, width, *refs):
-    *blocks, attn_low, attn_high, gu_ref, dn_ref, qkv_ref, out_ref = refs
-    block = blocks[0].shape[2] // 3
-    for layer, ref in enumerate(blocks):
+    low_ref, *high_refs = refs[: LINE + 1]
+    attn_low, attn_high, gu_ref, dn_ref, qkv_ref, out_ref = refs[LINE + 1 :]
+    block = low_ref.shape[2] // 3
+    z = lax.axis_index("z")
+    for layer in range(2):
         for line in range(LINE):
             low = block_start(line, block, half)
             skip = line * block - low
-            for part in range(2):
-                piece = ref[line, :, part * block + skip : (part + 1) * block].astype(F32)
-                gu_ref[layer, :, part * half + low + skip : part * half + low + block] = piece
-            dn_ref[layer, :, low + skip : low + block] = ref[line, :, 2 * block + skip :].astype(F32)
+            for part in range(3):
+                where = slice(part * block + skip, (part + 1) * block)
+                if layer == 0:
+                    piece = low_ref[line, :, where]
+                else:
+                    offset = lax.rem(z - line + LINE, LINE)
+                    piece = high_refs[LINE - 1][:, where]
+                    for o in range(1, LINE):
+                        piece = jnp.where(offset == o, high_refs[o - 1][:, where], piece)
+                piece = piece.astype(F32)
+                if part < 2:
+                    gu_ref[layer, :, part * half + low + skip : part * half + low + block] = piece
+                else:
+                    dn_ref[layer, :, low + skip : low + block] = piece
     for layer, ref in enumerate((attn_low, attn_high)):
         qkv_ref[layer] = ref[:, :width].astype(F32)
         out_ref[layer] = ref[:, width:].astype(F32)
 
 
-def settle(blocks, attn, half, width):
+def settle(blocks, arrived, attn, half, width):
     few = attn[0].shape[0]
     shape = jax.ShapeDtypeStruct
     return pl.pallas_call(
@@ -1218,7 +1314,7 @@
             shape((2, few, attn[0].shape[1] - width), F32),
         ),
         compiler_params=pltpu.CompilerParams(vmem_limit_bytes=56 * 2**20),
-    )(*blocks, *attn)
+    )(blocks, *arrived, *attn)
 
 
 def in_slots(partial, slots):
@@ -1254,20 +1350,25 @@
     bias_all = b_qkv.astype(F32)
     line = lax.axis_index("z")
     valid = jnp.arange(block) >= line * block - jnp.minimum(line * block, half - block)
+    flats = [jnp.concatenate([w_qkv[layer], w_out[layer]], axis=1) for layer in range(layers)]
     saved = []
     for layer in range(layers):
-        flat = jnp.concatenate([w_qkv[layer], w_out[layer]], axis=1)
-        start, more = (tokens, cotangent) if layer == 0 else (middle, in_slots(partial, 2 * LINE))
         gains = (gain_attn[layer : layer + 1], gain_ffn[layer : layer + 1])
+        if layer == 0:
+            start, more, weight = tokens, flats[1], flats[0]
+        else:
+            start, more, weight = middle, in_slots(partial, 2 * LINE), attn_weights[layer]
         out = front(
-            start, more, gains, bias_all[layer : layer + 1], tables, flat, w_gateup, w_down,
+            start, more, gains, bias_all[layer : layer + 1], tables, weight, w_gateup, w_down,
             layer, LINE, bits, block, qkv_width, 8 + layer,
         )
-        if layer == 0:
-            gm_all = out[12].reshape(-1, cotangent.shape[1])
         (state, middle, xa_all, query, key, value, log_total, attended) = out[:8]
         xf_all, gu_w, down_w = (item.reshape(-1, item.shape[2]) for item in out[8:11])
-        both_w = out[11]
+        if layer == 0:
+            attn_weights = out[11:]
+            xf_all, late = lax.optimization_barrier((xf_all, cotangent))
+            gm_all = lax.all_gather(late, ("z", "t"), axis=0, tiled=True)
+        both_w = attn_weights[layer]
         gate_up = jnp.dot(xf_all, gu_w, preferred_element_type=F32)
         gate = gate_up[:, :block]
         up = gate_up[:, block:]
@@ -1278,7 +1379,7 @@
             + (middle, xf_all, gate, up, act, gu_w, down_w, both_w)
         )
     grad, branch, above = cotangent, in_slots(partial, 2 * LINE), []
-    grads_attn, grads_blocks = [], []
+    grads_attn = []
     for layer in reversed(range(layers)):
         (state_in, xa_all, query, key, value, log_total, attended) = saved[layer][:7]
         (middle, xf_all, gate, up, act, gu_w, down_w, both_w) = saved[layer][7:]
@@ -1298,8 +1399,16 @@
         out = back(
             partial, branch, *wide, ins, above if layer == 0 else [], LINE, bits, qkv_width, 16 + layer
         )
-        (grad, _, _, d_bias, part_a, part_f, blocks, d_attn), rest = out[:8], out[8:]
-        grads_blocks.append(blocks)
+        (grad, _, _, d_bias, part_a, part_f), rest = out[:6], out[6:]
+        if layer > 0:
+            (*folded, d_attn), rest = rest[: LINE + 1], rest[LINE + 1 :]
+            arrived = [
+                lax.ppermute(folded[o - 1], "z", [(i, (i + o) % LINE) for i in range(LINE)])
+                for o in range(1, LINE)
+            ]
+            arrived.append(folded[LINE - 1])
+        else:
+            (blocks, d_attn), rest = rest[:2], rest[2:]
         if branch is not None:
             output = (middle + rest[0]).astype(LOW)
             branch = None
@@ -1312,7 +1421,7 @@
         grads_attn.append(d_attn)
     sums = rest[-1]
     side = lax.axis_index("t")
-    d_gu_all, d_dn_all, d_qkv_all, d_out_all = settle(grads_blocks[::-1], grads_attn[::-1], half, qkv_width)
+    d_gu_all, d_dn_all, d_qkv_all, d_out_all = settle(blocks, arrived, grads_attn[::-1], half, qkv_width)
     return (
         output,
         grad,

time: 860 us -> 817 us (0.950)
  Pallas kernels: 690 us -> 646 us
  local copies, waits for them, and re-layouts: 32.7 us -> 22.6 us
  starting transfers between devices: 0.04 us -> 9.91 us
    pallas_call x2, Pallas kernels: 349 us -> 306 us  [back(): pl.pallas_call(functools.partial(back_kernel, size, bits, width, (top, bo...]
    ppermute x0 -> x3, starting transfers between devices: none -> 9.53 us  [local(): lax.ppermute(folded[o - 1], 'z', [(i, (i + o) % LINE) for i in range(LINE)])]
    dot_general x4 -> x2, local copies, waits for them, and re-layouts: 17.7 us -> 9.54 us  [contract_first(): lax.dot_general(left, right, (((0,), (0,)), ((), ())), preferred_element_...]
  transfers between devices with their start and end apart: 1 -> 5, of which waited for: 0 -> 0; matrix products, arithmetic and copies ran while one was open for 6% -> 10% of each run, Pallas kernels for 18% -> 43%
where the time goes in v6:
time: 817 us; the launch traced here: 811 us
  Pallas kernels  646 us (79%)
  matrix products  107 us (13%)
  local copies, waits for them, and re-layouts  22.6 us (3%)
  between operations  17.1 us (2%)
  starting transfers between devices  9.91 us (1%)
  other arithmetic  8.8 us (1%)
    pallas_call x2, Pallas kernels, front(): pl.pallas_call(functools.partial(front_kernel, size, bits, block, half, l...  333 us
    pallas_call x2, Pallas kernels, back(): pl.pallas_call(functools.partial(back_kernel, size, bits, width, (top, bo...  306 us
    dot_general x4, matrix products, contract_first(): lax.dot_general(left, right, (((0,), (0,)), ((), ())), preferred_element_...  36.3 us
    dot_general x4, matrix products, contract_last(): lax.dot_general(left, right, (((1,), (1,)), ((), ())), preferred_element_...  29.4 us
    dot_general x2, matrix products, local(): gate_up = jnp.dot(xf_all, gu_w, preferred_element_type=F32)  23.6 us
    dot_general x2, matrix products, local(): d_act = jnp.dot(gm_all, down_w, preferred_element_type=F32)  17.6 us
  transfers between devices with their start and end apart: 5, of which 0 were waited for; matrix products, arithmetic and copies ran while one was open for 10% of the time, Pallas kernels for 43%

profile of v6, /device:TPU:26, one launch (start us, length us, event | category | flops | bytes accessed | tf_op | source)
XLA Modules:
  0.0 811.4 jit_solution(11509347695621088995)
XLA Ops:
  7.2 0.0 all-gather.2.cloned.1.call-start
  7.2 1.4 fusion.27
  11.2 2.6 convert_add_fusion
  13.8 1.4 fusion.26
  15.2 0.8 fusion.18.refs_7_.refs_11_.refs_10_
  16.0 0.5 multiply_sine_fusion
  16.6 0.8 pad_maximum_fusion.2.refs_5_.refs_9_.refs_8_
  17.3 1.0 slice_bitcast_fusion.2
  18.3 1.1 slice_bitcast_fusion
  19.4 1.4 fusion.24
  20.8 0.8 negate_select_fusion.refs_6_.refs_10_.refs_9_
  21.5 0.9 pad_maximum_fusion
  22.4 159.2 %shard_map.169 = (f32[128,1536]{1,0:T(8,128)}, f32[128,1536]{1,0:T(8,128)}, bf16[2,128,1536]{2,1,0:T(8,128)(2,1)}, bf16[256,768]{1,0:T(8,128)(2,1)}, bf16[256,12...) custom-call(bf16[128,1536]{1,0:T(8,128)(2,1)} %refs_0_.1, ...), custom_call_target="tpu_custom_call" | custom-call | bytes 525000000 | tf_op jit(solution)/shard_map/pallas_call | solution.py:844
  181.6 0.0 all-gather.2.cloned.1.call-update
  181.6 0.3 reduce-scatter.2.cloned.1.call-start
  182.0 10.5 %fusion.28 = f32[1024,2304]{1,0:T(8,128)S(1)} fusion(bf16[1024,1536]{1,0:T(8,128)(2,1)} %bitcast.91, bf16[1536,2304]{1,0:T(8,128)(2,1)} %bitcast.79), kind=kOutput, calls=%fused_computation.59 | convolution fusion | flops 7247757312 | bytes 19660800 | tf_op jit(solution)/shard_map/dot_general | solution.py:1372
  192.5 1.6 select_convert_fusion.5
  194.1 2.8 copy-done
  196.9 0.2 copy-done.9
  197.1 5.6 fusion.29.refs_1_
  202.7 173.7 %shard_map.170 = (f32[128,1536]{1,0:T(8,128)}, f32[128,1536]{1,0:T(8,128)}, bf16[2,128,1536]{2,1,0:T(8,128)(2,1)}, bf16[256,768]{1,0:T(8,128)(2,1)}, bf16[256,12...) custom-call(f32[128,1536]{1,0:T(8,128)} %get-tuple-element.54.refs_0, ...), custom_call_target="tpu_custom_call" | custom-call | bytes 525000000 | tf_op jit(solution)/shard_map/pallas_call | solution.py:844
  376.4 4.8 copy.19
  381.2 13.1 %fusion.30 = f32[1024,2304]{1,0:T(8,128)} fusion(bf16[1024,1536]{1,0:T(8,128)(2,1)S(1)} %bitcast.75, bf16[1536,2304]{1,0:T(8,128)(2,1)} %bitcast.83), kind=kOutput, calls=%fused_computation.61 | convolution fusion | flops 7247757312 | bytes 19660800 | tf_op jit(solution)/shard_map/dot_general | solution.py:1372
  394.3 10.8 %select_convert_fusion.4 = (bf16[1024,1152]{1,0:T(8,128)(2,1)S(1)}, bf16[1024,1152]{1,0:T(8,128)(2,1)S(1)}, bf16[1024,1152]{1,0:T(8,128)(2,1)S(1)}) fusion(f32[1024,2304]{1,0:T(8,128)} %fusion.30, pred[1152]{0:T(1024)(128)(4,1)S(1)} %iota_compare_fusion.1, bf16[1024,1536]{1,0:T(8,128)(2,1)} %all-gather.2.cloned.1.call-done, bf16[1536,1152]{1,0:T(8,128)(2,1)} %bitcast.89), kind=kOutput, calls=%fused_computation.20 | convolution fusion | flops 3646291968 | bytes 23200896 | tf_op jit(solution)/shard_map/dot_general | solution.py:1387
  405.2 0.0 copy-start.4
  405.2 0.0 slice-start.5
  405.2 5.7 fusion.31.refs_1_
  410.9 9.7 %fusion.4.refs_2_ = bf16[16,96,2304]{2,1,0:T(8,128)(2,1)} fusion(bf16[16,96,1024]{2,1,0:T(8,128)(2,1)S(1)} %bitcast.76, bf16[1024,1152]{1,0:T(8,128)(2,1)S(1)} %get-tuple-element.102, bf16[1024,1152]{1,0:T(8,128)(2,1)S(1)} %get-tuple-element.101), kind=kOutput, calls=%fused_computation.5 | convolution fusion | flops 7257194496 | bytes 14942208 | tf_op jit(solution)/shard_map/dot_general | solution.py:50
  420.6 8.9 %fusion.refs_0_ = bf16[8,128,1536]{2,1,0:T(8,128)(2,1)} fusion(bf16[1536,2304,1]{1,0,2:T(8,128)(2,1)S(1)} %bitcast.86, bf16[8,128,1152]{2,1,0:T(8,128)(2,1)S(1)} %bitcast.95, bf16[8,128,1152]{2,1,0:T(8,128)(2,1)S(1)} %bitcast.94), kind=kOutput, calls=%fused_computation | convolution fusion | flops 7257194496 | bytes 14942208 | tf_op jit(solution)/shard_map/dot_general | solution.py:46
  429.5 5.9 fusion.32
  435.4 131.4 %shard_map.171 = (f32[128,1536]{1,0:T(8,128)}, bf16[2,128,1536]{2,1,0:T(8,128)(2,1)}, bf16[2,128,1024]{2,1,0:T(8,128)(2,1)}, f32[1,1024]{1,0:T(1,128)}, f32[1,15...) custom-call(bf16[8,128,1536]{2,1,0:T(8,128)(2,1)} %fusion.refs_0_, ...), custom_call_target="tpu_custom_call" | custom-call | bytes 525000000 | tf_op jit(solution)/shard_map/pallas_call | solution.py:1215
  566.8 0.0 reduce-scatter.2.cloned.1.call-update
  566.9 0.2 collective-permute-start
  567.1 9.3 %collective-permute-start.1 = (bf16[96,3456]{1,0:T(8,128)(2,1)}, bf16[96,3456]{1,0:T(8,128)(2,1)}, u32[]{:S(2)}, u32[]{:S(2)}) collective-permute-start(bf16[96,3456]{1,0:T(8,128)(2,1)} %get-tuple-element.90), channel_id=1, source_target_pairs={{0,16},{8,24},{16,0},{24,8},{1,17},{9,25},{17,1},{25,9},{2,18},{10... | collective-permute-start | bytes 1990664 | tf_op jit(solution)/shard_map/ppermute | solution.py:1406
  576.4 4.8 copy.20
  581.2 0.0 slice-start.3
  581.2 8.7 %fusion.15.refs_2_ = bf16[16,96,1152]{2,1,0:T(8,128)(2,1)} fusion(bf16[16,96,1024]{2,1,0:T(8,128)(2,1)} %bitcast.77, bf16[1024,1152]{1,0:T(8,128)(2,1)S(1)} %copy-done.6), kind=kOutput, calls=%fused_computation.24 | convolution fusion | flops 3623878656 | bytes 9043968 | tf_op jit(solution)/shard_map/dot_general | solution.py:50
  589.9 0.0 slice-start.4
  589.9 6.8 select_convert_fusion.1
  596.7 11.9 %fusion.11 = bf16[1536,2304]{1,0:T(8,128)(2,1)} fusion(bf16[1024,1536]{1,0:T(8,128)(2,1)} %bitcast.92, bf16[1024,1152]{1,0:T(8,128)(2,1)} %get-tuple-element.100, bf16[1024,1152]{1,0:T(8,128)(2,1)S(1)} %get-tuple-element.99), kind=kOutput, calls=%fused_computation.12 | convolution fusion | flops 7257194496 | bytes 14942208 | tf_op jit(solution)/shard_map/dot_general | solution.py:50
  608.7 9.3 %fusion.7.refs_0_ = bf16[8,128,1536]{2,1,0:T(8,128)(2,1)} fusion(bf16[1536,2304,1]{1,0,2:T(8,128)(2,1)S(1)} %bitcast.82, bf16[8,128,1152]{2,1,0:T(8,128)(2,1)S(1)} %bitcast.97, bf16[8,128,1152]{2,1,0:T(8,128)(2,1)S(1)} %bitcast.96), kind=kOutput, calls=%fused_computation.8 | convolution fusion | flops 7257194496 | bytes 14942208 | tf_op jit(solution)/shard_map/dot_general | solution.py:46
  618.0 174.2 %shard_map.172 = (f32[128,1536]{1,0:T(8,128)}, bf16[2,128,1536]{2,1,0:T(8,128)(2,1)}, bf16[2,128,1024]{2,1,0:T(8,128)(2,1)}, f32[1,1024]{1,0:T(1,128)}, f32[1,15...) custom-call(bf16[8,128,1536]{2,1,0:T(8,128)(2,1)} %fusion.7.refs_0_,, ...), custom_call_target="tpu_custom_call" | custom-call | bytes 17500000 | tf_op jit(solution)/shard_map/pallas_call | solution.py:1215
  792.2 1.5 fusion.23
  793.7 1.4 constant_dynamic-slice_fusion
  795.1 0.8 add_convert_fusion
  795.9 0.0 reduce-scatter.2.cloned.1.call-done.refs_6_
  796.0 7.5 shard_map.173
  803.5 0.9 copy.22
  (47 shorter events, 0.1 us)
Async XLA Ops:
  7.2 387.2 %all-gather.2.cloned.1.call-start = ((), (), s32[]{:S(2)}) async-start(), calls=%async_computation.1 | async-start | bytes 3538944 | tf_op jit(solution)/shard_map/all_gather | solution.py:1370
  181.6 614.3 %reduce-scatter.2.cloned.1.call-start = ((), (), s32[]{:S(2)}) async-start(), calls=%async_computation.2 | async-start | bytes 5849088 | tf_op jit(solution)/shard_map/reduce_scatter | solution.py:1418
  192.4 4.4 copy-start
  192.5 4.7 copy-start.9
  196.9 5.8 copy-start.5
  376.4 4.8 copy-start.3
  394.3 10.8 %copy-start.11 = (bf16[16,96,1152]{2,1,0:T(8,128)(2,1)S(1)}, bf16[16,96,1152]{2,1,0:T(8,128)(2,1)}, u32[]{:S(2)}) copy-start(bf16[16,96,1152]{2,1,0:T(8,128)(2,1)} %get-tuple-element.62) | copy-start | bytes 10616836
  405.2 5.7 copy-start.4
  405.2 15.4 %slice-start.5 = ((s8[7077888]{0:T(1024)(128)(4,1)}), s8[4194304]{0:T(1024)(128)(4,1)S(1)}, s32[]{:S(2)}) async-start(s8[7077888]{0:T(1024)(128)(4,1)} %bitcast.84), calls=%async_computation.8 | async-start | bytes 8388608
  410.9 9.7 %slice-start.6 = ((s8[7077888]{0:T(1024)(128)(4,1)}), s8[2883584]{0:T(1024)(128)(4,1)S(1)}, s32[]{:S(2)}) async-start(s8[7077888]{0:T(1024)(128)(4,1)} %bitcast.84), calls=%async_computation.9 | async-start | bytes 5767168
  420.6 8.9 %copy-start.12 = (bf16[1024,1536]{1,0:T(8,128)(2,1)S(1)}, bf16[1024,1536]{1,0:T(8,128)(2,1)}, u32[]{:S(2)}) copy-start(bf16[1024,1536]{1,0:T(8,128)(2,1)} %all-gather.2.cloned.1.call-done) | copy-start | bytes 9437188
  566.8 14.3 %copy-start.6 = (bf16[1024,1152]{1,0:T(8,128)(2,1)S(1)}, bf16[1024,1152]{1,0:T(8,128)(2,1)}, u32[]{:S(2)}) copy-start(bf16[1024,1152]{1,0:T(8,128)(2,1)} %copy-done.5) | copy-start | bytes 7077892
  566.9 229.1 %collective-permute-start = (bf16[96,3456]{1,0:T(8,128)(2,1)}, bf16[96,3456]{1,0:T(8,128)(2,1)}, u32[]{:S(2)}, u32[]{:S(2)}) collective-permute-start(bf16[96,3456]{1,0:T(8,128)(2,1)} %get-tuple-element.89), channel_id=1, source_target_pairs={{0,8},{8,16},{16,24},{24,0},{1,9},{9,17},{17,25},{25,1},{2,10},{10... | collective-permute-start | bytes 1990664 | tf_op jit(solution)/shard_map/ppermute | solution.py:1406
  567.1 228.8 %collective-permute-start.1 = (bf16[96,3456]{1,0:T(8,128)(2,1)}, bf16[96,3456]{1,0:T(8,128)(2,1)}, u32[]{:S(2)}, u32[]{:S(2)}) collective-permute-start(bf16[96,3456]{1,0:T(8,128)(2,1)} %get-tuple-element.90), channel_id=1, source_target_pairs={{0,16},{8,24},{16,0},{24,8},{1,17},{9,25},{17,1},{25,9},{2,18},{10... | collective-permute-start | bytes 1990664 | tf_op jit(solution)/shard_map/ppermute | solution.py:1406
  576.4 219.5 %collective-permute-start.2 = (bf16[96,3456]{1,0:T(8,128)(2,1)}, bf16[96,3456]{1,0:T(8,128)(2,1)}, u32[]{:S(2)}, u32[]{:S(2)}) collective-permute-start(bf16[96,3456]{1,0:T(8,128)(2,1)} %get-tuple-element.91), channel_id=1, source_target_pairs={{0,24},{8,0},{16,8},{24,16},{1,25},{9,1},{17,9},{25,17},{2,26},{10... | collective-permute-start | bytes 1990664 | tf_op jit(solution)/shard_map/ppermute | solution.py:1406
  576.4 13.5 %slice-start = ((s8[9437184]{0:T(1024)(128)(4,1)}), s8[1048576]{0:T(1024)(128)(4,1)S(1)}, s32[]{:S(2)}) async-start(s8[9437184]{0:T(1024)(128)(4,1)} %bitcast.67), calls=%async_computation.3 | async-start | bytes 2097152
  581.1 8.7 %slice-start.1 = ((s8[9437184]{0:T(1024)(128)(4,1)}), s8[4194304]{0:T(1024)(128)(4,1)S(1)}, s32[]{:S(2)}) async-start(s8[9437184]{0:T(1024)(128)(4,1)} %bitcast.67), calls=%async_computation.4 | async-start | bytes 8388608
  581.2 8.8 %slice-start.2 = ((s8[9437184]{0:T(1024)(128)(4,1)}), s8[4194304]{0:T(1024)(128)(4,1)S(1)}, s32[]{:S(2)}) async-start(s8[9437184]{0:T(1024)(128)(4,1)} %bitcast.67), calls=%async_computation.5 | async-start | bytes 8388608
  581.2 8.8 %copy-start.2 = (bf16[8,128,1536]{2,1,0:T(8,128)(2,1)S(1)}, bf16[8,128,1536]{2,1,0:T(8,128)(2,1)}, u32[]{:S(2)}) copy-start(bf16[8,128,1536]{2,1,0:T(8,128)(2,1)} %get-tuple-element.73) | copy-start | bytes 9437188
  581.2 8.8 %copy-start.10 = (bf16[16,96,1152]{2,1,0:T(8,128)(2,1)S(1)}, bf16[16,96,1152]{2,1,0:T(8,128)(2,1)}, u32[]{:S(2)}) copy-start(bf16[16,96,1152]{2,1,0:T(8,128)(2,1)} %get-tuple-element.58) | copy-start | bytes 10616836
  581.2 27.5 %slice-start.3 = ((s8[7077888]{0:T(1024)(128)(4,1)}), s8[4194304]{0:T(1024)(128)(4,1)S(1)}, s32[]{:S(2)}) async-start(s8[7077888]{0:T(1024)(128)(4,1)} %bitcast.80), calls=%async_computation.6 | async-start | bytes 8388608
  589.9 18.8 %slice-start.4 = ((s8[7077888]{0:T(1024)(128)(4,1)}), s8[2883584]{0:T(1024)(128)(4,1)S(1)}, s32[]{:S(2)}) async-start(s8[7077888]{0:T(1024)(128)(4,1)} %bitcast.80), calls=%async_computation.7 | async-start | bytes 5767168
  596.7 12.0 %copy-start.13 = (bf16[1024,1152]{1,0:T(8,128)(2,1)S(1)}, bf16[1024,1152]{1,0:T(8,128)(2,1)}, u32[]{:S(2)}) copy-start(bf16[1024,1152]{1,0:T(8,128)(2,1)} %get-tuple-element.100) | copy-start | bytes 7077892
  618.0 177.1 %copy-start.1 = (f32[128,1536]{1,0:T(8,128)S(1)}, f32[128,1536]{1,0:T(8,128)}, u32[]{:S(2)}) copy-start(f32[128,1536]{1,0:T(8,128)} %get-tuple-element.60.refs_6_) | copy-start | bytes 2359300
  618.0 177.1 %copy-start.8 = (f32[128,1536]{1,0:T(8,128)S(1)}, f32[128,1536]{1,0:T(8,128)}, u32[]{:S(2)}) copy-start(f32[128,1536]{1,0:T(8,128)} %get-tuple-element.72) | copy-start | bytes 2359300
  792.2 11.3 %copy-start.7 = (f32[128,1536]{1,0:T(8,128)S(1)}, f32[128,1536]{1,0:T(8,128)}, u32[]{:S(2)}) copy-start(f32[128,1536]{1,0:T(8,128)} %get-tuple-element.138) | copy-start | bytes 2359300
Sparse Core Ops, SparseCore 0:
  181.7 90.4 all-gather.1
  567.0 127.7 reduce-scatter.1

commit v7 on v6

--- a/solution.py
+++ b/solution.py
@@ -369,7 +369,7 @@
                 self.own_copy(place, variant).wait()
                 held = self.own_buf[place * 2**self.last + variant].astype(F32)
             else:
-                held = self.sums[place * (2**self.last - 1) + 2**stage - 1 + variant]
+                held = self.sums[place * (2**self.last - 1) + 2**stage - 1 + variant].astype(F32)
             self.copy(place, stage, variant).wait_recv()
             total = held + self.stage_in[self.index(place, stage, variant)].astype(F32)
             if stage == 0:
@@ -381,7 +381,7 @@
                 self.stage_out[number] = total.astype(LOW)
                 self.copy(place, stage - 1, lower).start()
             else:
-                self.sums[number] = total
+                self.sums[number] = total.astype(LOW)
 
     def end(self):
         for place in range(self.size):
@@ -395,7 +395,7 @@
     inner, lower = size * (2**count - 1), size * (2 ** (count - 1) - 1)
     return [
         pltpu.VMEM((size * 2 ** (count - 1), rows, columns), LOW),
-        pltpu.VMEM((max(lower, 1), rows, columns) if lower else (1, 8, LANES), F32),
+        pltpu.VMEM((max(lower, 1), rows, columns) if lower else (1, 16, LANES), LOW),
         pltpu.VMEM((inner, rows, columns), LOW),
         pltpu.VMEM((max(lower, 1), rows, columns) if lower else (1, 16, LANES), LOW),
         pltpu.SemaphoreType.DMA((size * 2 ** (count - 1),)),
@@ -410,48 +410,6 @@
         others = sorted((other for other in range(size) if other != line), key=lambda other: -abs(other - line))
         order.append([*others, line])
     return sum(jnp.where(z == line, order[line][place], 0) for line in range(size))
-
-
-class Scatter:
-    def __init__(self, size, bits, p_ref, out_ref, line_out, line_in, line_send, line_recv, *fold):
-        order = list(range(1, size)) + [0]
-        self.fold = Fold(size, bits, order, p_ref, *fold)
-        self.size, self.out_ref = size, out_ref
-        self.line_out, self.line_in, self.line_send, self.line_recv = line_out, line_in, line_send, line_recv
-
-    def line_copy(self, place):
-        return pltpu.make_async_remote_copy(
-            src_ref=self.line_out.at[place],
-            dst_ref=self.line_in.at[place],
-            send_sem=self.line_send.at[place],
-            recv_sem=self.line_recv.at[place],
-            device_id={"z": self.fold.line(place)},
-            device_id_type=MESH,
-        )
-
-    def done(self, place, total):
-        if place < self.size - 1:
-            self.line_out[place] = total.astype(LOW)
-            self.line_copy(place).start()
-        else:
-            self.out_ref[...] = total
-
-    def begin(self, places=None):
-        self.fold.begin(places)
-
-    def place(self, place):
-        for stage in reversed(range(self.fold.count)):
-            self.fold.stage(place, stage, self.done)
-
-    def finish(self):
-        for place in range(self.size - 1):
-            self.line_copy(place).wait_recv()
-            self.out_ref[...] += self.line_in[place].astype(F32)
-
-    def end(self):
-        self.fold.end()
-        for place in range(self.size - 1):
-            self.line_copy(place).wait_send()
 
 
 class Relay:
@@ -519,8 +477,8 @@
             self.line_copy(place, self.fold.line(place)).wait_send()
 
 
-def scatter_scratch(size, bits, rows, columns, relay=False):
-    lands = (size - 1) * (2 if relay else 1)
+def scatter_scratch(size, bits, rows, columns):
+    lands = 2 * (size - 1)
     return [
         pltpu.VMEM((size - 1, rows, columns), LOW),
         pltpu.VMEM((lands, rows, columns), LOW),
@@ -605,7 +563,7 @@
 
 def comm_params(collective_id):
     return pltpu.CompilerParams(
-        collective_id=collective_id, has_side_effects=True, vmem_limit_bytes=60 * 2**20
+        collective_id=collective_id, has_side_effects=True, vmem_limit_bytes=61 * 2**20
     )
 
 
@@ -769,7 +727,7 @@
         steps = (attention, ahead)
     else:
         total_ref, *rest = rest
-        side = Scatter(size, ("t",), more_ref, total_ref, *rest)
+        side = Relay(size, ("t",), more_ref, total_ref, *rest)
         moved = pltpu.make_async_copy(at_ref, w_ref, at_sem)
         moved.start()
         side.begin()
@@ -1100,7 +1058,7 @@
         refs, [1, SCATTER_REFS, 7, 7, 2, 3, 9, len(refs)]
     )
     greet_all(size, ("t", *bits))
-    rows = Scatter(size, ("t",), p_ref[0], dxf_ref, *dxf_scratch)
+    rows = Relay(size, ("t",), p_ref[0], dxf_ref, *dxf_scratch)
     blocks = Blocks(size, bits, *wide, folded, gu_fold, dn_fold, done, sems)
     work = AttendBack(ins, outs, work_scratch, width)
     branch = None
@@ -1113,7 +1071,7 @@
         kept = pltpu.make_async_copy(work.w_ref, attn_ref, kept_sem)
     else:
         attn_scratch, (x_ref, *small_scratch) = in_groups(refs, [SCATTER_REFS, len(refs)])
-        final = Scatter(size, bits, work.w_ref, attn_ref, *attn_scratch)
+        final = Relay(size, bits, work.w_ref, attn_ref, *attn_scratch)
         small = Total(size, ("t", *bits), x_ref, more_out[0], *small_scratch)
     rows.begin()
     blocks.begin()
@@ -1124,14 +1082,14 @@
     blocks.inner(2)
     rows.place(1)
     blocks.inner(3)
-    blocks.send(0)
     rows.place(2)
     rows.place(3)
     if top:
         branch.begin([0])
     rows.finish()
+    work.begin(dxf_ref[...])
+    blocks.send(0)
     blocks.send(1)
-    work.begin(dxf_ref[...])
     if top:
         branch.begin([1])
     work.arrive()
@@ -1211,7 +1169,6 @@
     held, far = pl.BlockSpec(memory_space=pltpu.VMEM), pl.BlockSpec(memory_space=pl.ANY)
     shape = jax.ShapeDtypeStruct
     rows_scratch = scatter_scratch(size, ("t",), count, model)
-    branch_scratch = scatter_scratch(size, ("t",), count, model, relay=True)
     return pl.pallas_call(
         functools.partial(back_kernel, size, bits, width, (top, bottom)),
         out_shape=(
@@ -1251,7 +1208,7 @@
             pltpu.VMEM((count, model), LOW),
             pltpu.SemaphoreType.DMA((2,)),
             pltpu.SemaphoreType.DMA((2,)),
-            *(branch_scratch if top else []),
+            *(rows_scratch if top else []),
             *(
                 [
                     *scatter_scratch(size, bits, *weight[1:]),

time: 817 us -> 789 us (0.966)
  Pallas kernels: 646 us -> 606 us
  matrix products: 107 us -> 116 us
    pallas_call x2, Pallas kernels: 306 us -> 277 us  [back(): pl.pallas_call(functools.partial(back_kernel, size, bits, width, (top, bo...]
    pallas_call x2, Pallas kernels: 333 us -> 321 us  [front(): pl.pallas_call(functools.partial(front_kernel, size, bits, block, half, l...]
    dot_general x4, matrix products: 36.3 us -> 46.5 us  [contract_first(): lax.dot_general(left, right, (((0,), (0,)), ((), ())), preferred_element_...]
  transfers between devices with their start and end apart: 5 -> 5, of which waited for: 0 -> 0; matrix products, arithmetic and copies ran while one was open for 10% -> 10% of each run, Pallas kernels for 43% -> 40%
where the time goes in v7:
time: 789 us; the launch traced here: 778 us
  Pallas kernels  606 us (77%)
  matrix products  116 us (15%)
  local copies, waits for them, and re-layouts  22.6 us (3%)
  between operations  17.1 us (2%)
  other arithmetic  8.8 us (1%)
    pallas_call x2, Pallas kernels, front(): pl.pallas_call(functools.partial(front_kernel, size, bits, block, half, l...  321 us
    pallas_call x2, Pallas kernels, back(): pl.pallas_call(functools.partial(back_kernel, size, bits, width, (top, bo...  277 us
    dot_general x4, matrix products, contract_first(): lax.dot_general(left, right, (((0,), (0,)), ((), ())), preferred_element_...  46.5 us
    dot_general x4, matrix products, contract_last(): lax.dot_general(left, right, (((1,), (1,)), ((), ())), preferred_element_...  29.1 us
    dot_general x2, matrix products, local(): gate_up = jnp.dot(xf_all, gu_w, preferred_element_type=F32)  23.1 us
    dot_general x2, matrix products, local(): d_act = jnp.dot(gm_all, down_w, preferred_element_type=F32)  17.6 us
  transfers between devices with their start and end apart: 5, of which 0 were waited for; matrix products, arithmetic and copies ran while one was open for 10% of the time, Pallas kernels for 40%

profile of v7, /device:TPU:26, one launch (start us, length us, event | category | flops | bytes accessed | tf_op | source)
XLA Modules:
  0.0 778.0 jit_solution(15485449924909906758)
XLA Ops:
  7.2 0.0 all-gather.2.cloned.1.call-start
  7.2 1.4 fusion.27
  11.2 2.6 convert_add_fusion
  13.8 1.4 fusion.26
  15.2 0.8 fusion.18.refs_7_.refs_11_.refs_10_
  16.0 0.5 multiply_sine_fusion
  16.6 0.8 pad_maximum_fusion.2.refs_5_.refs_9_.refs_8_
  17.3 1.0 slice_bitcast_fusion.2
  18.3 1.1 slice_bitcast_fusion
  19.4 1.4 fusion.24
  20.8 0.8 negate_select_fusion.refs_6_.refs_10_.refs_9_
  21.5 0.9 pad_maximum_fusion
  22.4 159.2 %shard_map.169 = (f32[128,1536]{1,0:T(8,128)}, f32[128,1536]{1,0:T(8,128)}, bf16[2,128,1536]{2,1,0:T(8,128)(2,1)}, bf16[256,768]{1,0:T(8,128)(2,1)}, bf16[256,12...) custom-call(bf16[128,1536]{1,0:T(8,128)(2,1)} %refs_0_.1, ...), custom_call_target="tpu_custom_call" | custom-call | bytes 525000000 | tf_op jit(solution)/shard_map/pallas_call | solution.py:802
  181.6 0.0 all-gather.2.cloned.1.call-update
  181.6 0.0 reduce-scatter.2.cloned.1.call-start
  181.7 10.5 %fusion.28 = f32[1024,2304]{1,0:T(8,128)S(1)} fusion(bf16[1024,1536]{1,0:T(8,128)(2,1)} %bitcast.91, bf16[1536,2304]{1,0:T(8,128)(2,1)} %bitcast.79), kind=kOutput, calls=%fused_computation.59 | convolution fusion | flops 7247757312 | bytes 19660800 | tf_op jit(solution)/shard_map/dot_general | solution.py:1329
  192.2 1.6 select_convert_fusion.5
  193.8 2.8 copy-done
  196.6 0.2 copy-done.9
  196.8 5.6 fusion.29.refs_1_
  202.4 161.9 %shard_map.170 = (f32[128,1536]{1,0:T(8,128)}, f32[128,1536]{1,0:T(8,128)}, bf16[2,128,1536]{2,1,0:T(8,128)(2,1)}, bf16[256,768]{1,0:T(8,128)(2,1)}, bf16[256,12...) custom-call(f32[128,1536]{1,0:T(8,128)} %get-tuple-element.54.refs_0, ...), custom_call_target="tpu_custom_call" | custom-call | bytes 525000000 | tf_op jit(solution)/shard_map/pallas_call | solution.py:802
  364.4 4.8 copy.19
  369.2 12.6 %fusion.30 = f32[1024,2304]{1,0:T(8,128)} fusion(bf16[1024,1536]{1,0:T(8,128)(2,1)S(1)} %bitcast.75, bf16[1536,2304]{1,0:T(8,128)(2,1)} %bitcast.83), kind=kOutput, calls=%fused_computation.61 | convolution fusion | flops 7247757312 | bytes 19660800 | tf_op jit(solution)/shard_map/dot_general | solution.py:1329
  381.7 10.8 %select_convert_fusion.4 = (bf16[1024,1152]{1,0:T(8,128)(2,1)S(1)}, bf16[1024,1152]{1,0:T(8,128)(2,1)S(1)}, bf16[1024,1152]{1,0:T(8,128)(2,1)S(1)}) fusion(f32[1024,2304]{1,0:T(8,128)} %fusion.30, pred[1152]{0:T(1024)(128)(4,1)S(1)} %iota_compare_fusion.1, bf16[1024,1536]{1,0:T(8,128)(2,1)} %all-gather.2.cloned.1.call-done, bf16[1536,1152]{1,0:T(8,128)(2,1)} %bitcast.89), kind=kOutput, calls=%fused_computation.20 | convolution fusion | flops 3646291968 | bytes 23200896 | tf_op jit(solution)/shard_map/dot_general | solution.py:1344
  392.6 0.0 copy-start.4
  392.6 0.0 slice-start.5
  392.6 5.7 fusion.31.refs_1_
  398.3 9.7 %fusion.4.refs_2_ = bf16[16,96,2304]{2,1,0:T(8,128)(2,1)} fusion(bf16[16,96,1024]{2,1,0:T(8,128)(2,1)S(1)} %bitcast.76, bf16[1024,1152]{1,0:T(8,128)(2,1)S(1)} %get-tuple-element.102, bf16[1024,1152]{1,0:T(8,128)(2,1)S(1)} %get-tuple-element.101), kind=kOutput, calls=%fused_computation.5 | convolution fusion | flops 7257194496 | bytes 14942208 | tf_op jit(solution)/shard_map/dot_general | solution.py:50
  408.0 8.9 %fusion.refs_0_ = bf16[8,128,1536]{2,1,0:T(8,128)(2,1)} fusion(bf16[1536,2304,1]{1,0,2:T(8,128)(2,1)S(1)} %bitcast.86, bf16[8,128,1152]{2,1,0:T(8,128)(2,1)S(1)} %bitcast.95, bf16[8,128,1152]{2,1,0:T(8,128)(2,1)S(1)} %bitcast.94), kind=kOutput, calls=%fused_computation | convolution fusion | flops 7257194496 | bytes 14942208 | tf_op jit(solution)/shard_map/dot_general | solution.py:46
  416.9 16.1 %fusion.32 = bf16[1536,1152]{1,0:T(8,128)(2,1)} fusion(bf16[1024,1536]{1,0:T(8,128)(2,1)S(1)} %copy-done.12, bf16[1024,1152]{1,0:T(8,128)(2,1)S(1)} %get-tuple-element.103), kind=kOutput, calls=%fused_computation.63 | convolution fusion | flops 3623878656 | bytes 9043968 | tf_op jit(solution)/shard_map/dot_general | solution.py:50
  432.9 129.9 %shard_map.171 = (f32[128,1536]{1,0:T(8,128)}, bf16[2,128,1536]{2,1,0:T(8,128)(2,1)}, bf16[2,128,1024]{2,1,0:T(8,128)(2,1)}, f32[1,1024]{1,0:T(1,128)}, f32[1,15...) custom-call(bf16[8,128,1536]{2,1,0:T(8,128)(2,1)} %fusion.refs_0_, ...), custom_call_target="tpu_custom_call" | custom-call | bytes 525000000 | tf_op jit(solution)/shard_map/pallas_call | solution.py:1172
  562.8 0.0 reduce-scatter.2.cloned.1.call-update
  562.9 1.4 collective-permute-start
  564.2 5.3 collective-permute-start.1
  569.5 0.9 collective-permute-start.2
  570.4 4.7 copy.20
  575.1 0.0 slice-start.3
  575.1 8.8 %fusion.15.refs_2_ = bf16[16,96,1152]{2,1,0:T(8,128)(2,1)} fusion(bf16[16,96,1024]{2,1,0:T(8,128)(2,1)} %bitcast.77, bf16[1024,1152]{1,0:T(8,128)(2,1)S(1)} %copy-done.6), kind=kOutput, calls=%fused_computation.24 | convolution fusion | flops 3623878656 | bytes 9043968 | tf_op jit(solution)/shard_map/dot_general | solution.py:50
  584.0 6.8 select_convert_fusion.1
  590.8 11.9 %fusion.11 = bf16[1536,2304]{1,0:T(8,128)(2,1)} fusion(bf16[1024,1536]{1,0:T(8,128)(2,1)} %bitcast.92, bf16[1024,1152]{1,0:T(8,128)(2,1)} %get-tuple-element.100, bf16[1024,1152]{1,0:T(8,128)(2,1)S(1)} %get-tuple-element.99), kind=kOutput, calls=%fused_computation.12 | convolution fusion | flops 7257194496 | bytes 14942208 | tf_op jit(solution)/shard_map/dot_general | solution.py:50
  602.7 8.9 %fusion.7.refs_0_ = bf16[8,128,1536]{2,1,0:T(8,128)(2,1)} fusion(bf16[1536,2304,1]{1,0,2:T(8,128)(2,1)S(1)} %bitcast.82, bf16[8,128,1152]{2,1,0:T(8,128)(2,1)S(1)} %bitcast.97, bf16[8,128,1152]{2,1,0:T(8,128)(2,1)S(1)} %bitcast.96), kind=kOutput, calls=%fused_computation.8 | convolution fusion | flops 7257194496 | bytes 14942208 | tf_op jit(solution)/shard_map/dot_general | solution.py:46
  611.6 147.2 %shard_map.172 = (f32[128,1536]{1,0:T(8,128)}, bf16[2,128,1536]{2,1,0:T(8,128)(2,1)}, bf16[2,128,1024]{2,1,0:T(8,128)(2,1)}, f32[1,1024]{1,0:T(1,128)}, f32[1,15...) custom-call(bf16[8,128,1536]{2,1,0:T(8,128)(2,1)} %fusion.7.refs_0_,, ...), custom_call_target="tpu_custom_call" | custom-call | bytes 17500000 | tf_op jit(solution)/shard_map/pallas_call | solution.py:1172
  758.8 1.5 fusion.23
  760.3 1.4 constant_dynamic-slice_fusion
  761.7 0.8 add_convert_fusion
  762.5 0.0 reduce-scatter.2.cloned.1.call-done.refs_6_
  762.6 7.5 shard_map.173
  770.1 0.9 copy.22
  (47 shorter events, 0.1 us)
Async XLA Ops:
  7.2 374.6 %all-gather.2.cloned.1.call-start = ((), (), s32[]{:S(2)}) async-start(), calls=%async_computation.1 | async-start | bytes 3538944 | tf_op jit(solution)/shard_map/all_gather | solution.py:1327
  181.6 581.0 %reduce-scatter.2.cloned.1.call-start = ((), (), s32[]{:S(2)}) async-start(), calls=%async_computation.2 | async-start | bytes 5849088 | tf_op jit(solution)/shard_map/reduce_scatter | solution.py:1375
  192.2 4.4 copy-start
  192.2 4.7 copy-start.9
  196.6 5.8 copy-start.5
  364.4 4.8 copy-start.3
  381.7 10.8 %copy-start.11 = (bf16[16,96,1152]{2,1,0:T(8,128)(2,1)S(1)}, bf16[16,96,1152]{2,1,0:T(8,128)(2,1)}, u32[]{:S(2)}) copy-start(bf16[16,96,1152]{2,1,0:T(8,128)(2,1)} %get-tuple-element.62) | copy-start | bytes 10616836
  392.6 5.7 copy-start.4
  392.6 15.4 %slice-start.5 = ((s8[7077888]{0:T(1024)(128)(4,1)}), s8[4194304]{0:T(1024)(128)(4,1)S(1)}, s32[]{:S(2)}) async-start(s8[7077888]{0:T(1024)(128)(4,1)} %bitcast.84), calls=%async_computation.8 | async-start | bytes 8388608
  398.3 9.7 %slice-start.6 = ((s8[7077888]{0:T(1024)(128)(4,1)}), s8[2883584]{0:T(1024)(128)(4,1)S(1)}, s32[]{:S(2)}) async-start(s8[7077888]{0:T(1024)(128)(4,1)} %bitcast.84), calls=%async_computation.9 | async-start | bytes 5767168
  408.0 8.9 %copy-start.12 = (bf16[1024,1536]{1,0:T(8,128)(2,1)S(1)}, bf16[1024,1536]{1,0:T(8,128)(2,1)}, u32[]{:S(2)}) copy-start(bf16[1024,1536]{1,0:T(8,128)(2,1)} %all-gather.2.cloned.1.call-done) | copy-start | bytes 9437188
  562.8 12.3 %copy-start.6 = (bf16[1024,1152]{1,0:T(8,128)(2,1)S(1)}, bf16[1024,1152]{1,0:T(8,128)(2,1)}, u32[]{:S(2)}) copy-start(bf16[1024,1152]{1,0:T(8,128)(2,1)} %copy-done.5) | copy-start | bytes 7077892
  562.9 199.7 %collective-permute-start = (bf16[96,3456]{1,0:T(8,128)(2,1)}, bf16[96,3456]{1,0:T(8,128)(2,1)}, u32[]{:S(2)}, u32[]{:S(2)}) collective-permute-start(bf16[96,3456]{1,0:T(8,128)(2,1)} %get-tuple-element.89), channel_id=1, source_target_pairs={{0,8},{8,16},{16,24},{24,0},{1,9},{9,17},{17,25},{25,1},{2,10},{10... | collective-permute-start | bytes 1990664 | tf_op jit(solution)/shard_map/ppermute | solution.py:1363
  564.2 198.3 %collective-permute-start.1 = (bf16[96,3456]{1,0:T(8,128)(2,1)}, bf16[96,3456]{1,0:T(8,128)(2,1)}, u32[]{:S(2)}, u32[]{:S(2)}) collective-permute-start(bf16[96,3456]{1,0:T(8,128)(2,1)} %get-tuple-element.90), channel_id=1, source_target_pairs={{0,16},{8,24},{16,0},{24,8},{1,17},{9,25},{17,1},{25,9},{2,18},{10... | collective-permute-start | bytes 1990664 | tf_op jit(solution)/shard_map/ppermute | solution.py:1363
  569.5 193.0 %collective-permute-start.2 = (bf16[96,3456]{1,0:T(8,128)(2,1)}, bf16[96,3456]{1,0:T(8,128)(2,1)}, u32[]{:S(2)}, u32[]{:S(2)}) collective-permute-start(bf16[96,3456]{1,0:T(8,128)(2,1)} %get-tuple-element.91), channel_id=1, source_target_pairs={{0,24},{8,0},{16,8},{24,16},{1,25},{9,1},{17,9},{25,17},{2,26},{10... | collective-permute-start | bytes 1990664 | tf_op jit(solution)/shard_map/ppermute | solution.py:1363
  570.4 13.5 %slice-start = ((s8[9437184]{0:T(1024)(128)(4,1)}), s8[1048576]{0:T(1024)(128)(4,1)S(1)}, s32[]{:S(2)}) async-start(s8[9437184]{0:T(1024)(128)(4,1)} %bitcast.67), calls=%async_computation.3 | async-start | bytes 2097152
  575.1 8.8 %slice-start.1 = ((s8[9437184]{0:T(1024)(128)(4,1)}), s8[4194304]{0:T(1024)(128)(4,1)S(1)}, s32[]{:S(2)}) async-start(s8[9437184]{0:T(1024)(128)(4,1)} %bitcast.67), calls=%async_computation.4 | async-start | bytes 8388608
  575.1 8.8 %slice-start.2 = ((s8[9437184]{0:T(1024)(128)(4,1)}), s8[4194304]{0:T(1024)(128)(4,1)S(1)}, s32[]{:S(2)}) async-start(s8[9437184]{0:T(1024)(128)(4,1)} %bitcast.67), calls=%async_computation.5 | async-start | bytes 8388608
  575.1 8.8 %copy-start.2 = (bf16[8,128,1536]{2,1,0:T(8,128)(2,1)S(1)}, bf16[8,128,1536]{2,1,0:T(8,128)(2,1)}, u32[]{:S(2)}) copy-start(bf16[8,128,1536]{2,1,0:T(8,128)(2,1)} %get-tuple-element.73) | copy-start | bytes 9437188
  575.1 8.8 %copy-start.10 = (bf16[16,96,1152]{2,1,0:T(8,128)(2,1)S(1)}, bf16[16,96,1152]{2,1,0:T(8,128)(2,1)}, u32[]{:S(2)}) copy-start(bf16[16,96,1152]{2,1,0:T(8,128)(2,1)} %get-tuple-element.58) | copy-start | bytes 10616836
  575.1 27.6 %slice-start.3 = ((s8[7077888]{0:T(1024)(128)(4,1)}), s8[4194304]{0:T(1024)(128)(4,1)S(1)}, s32[]{:S(2)}) async-start(s8[7077888]{0:T(1024)(128)(4,1)} %bitcast.80), calls=%async_computation.6 | async-start | bytes 8388608
  584.0 18.8 %slice-start.4 = ((s8[7077888]{0:T(1024)(128)(4,1)}), s8[2883584]{0:T(1024)(128)(4,1)S(1)}, s32[]{:S(2)}) async-start(s8[7077888]{0:T(1024)(128)(4,1)} %bitcast.80), calls=%async_computation.7 | async-start | bytes 5767168
  590.8 12.0 %copy-start.13 = (bf16[1024,1152]{1,0:T(8,128)(2,1)S(1)}, bf16[1024,1152]{1,0:T(8,128)(2,1)}, u32[]{:S(2)}) copy-start(bf16[1024,1152]{1,0:T(8,128)(2,1)} %get-tuple-element.100) | copy-start | bytes 7077892
  611.6 150.1 %copy-start.1 = (f32[128,1536]{1,0:T(8,128)S(1)}, f32[128,1536]{1,0:T(8,128)}, u32[]{:S(2)}) copy-start(f32[128,1536]{1,0:T(8,128)} %get-tuple-element.60.refs_6_) | copy-start | bytes 2359300
  611.6 150.1 %copy-start.8 = (f32[128,1536]{1,0:T(8,128)S(1)}, f32[128,1536]{1,0:T(8,128)}, u32[]{:S(2)}) copy-start(f32[128,1536]{1,0:T(8,128)} %get-tuple-element.72) | copy-start | bytes 2359300
  758.8 11.3 %copy-start.7 = (f32[128,1536]{1,0:T(8,128)S(1)}, f32[128,1536]{1,0:T(8,128)}, u32[]{:S(2)}) copy-start(f32[128,1536]{1,0:T(8,128)} %get-tuple-element.138) | copy-start | bytes 2359300
Sparse Core Ops, SparseCore 0:
  181.7 82.4 all-gather.1
  563.0 109.8 reduce-scatter.1

commit v8 on v7

--- a/solution.py
+++ b/solution.py
@@ -690,7 +690,9 @@
 
 def front_kernel(size, bits, block, half, layer, width, *refs):
     first = layer == 0
-    inputs, outs, refs = in_groups(refs, [11, 13 if first else 11, len(refs)])
+    inputs, far_rows, outs, refs = in_groups(
+        refs, [11, 1 if first else 0, 14 if first else 11, len(refs)]
+    )
     (x_ref, more_ref, ga_ref, gf_ref, bias_ref, cos_ref, sin_ref, mask_ref, at_ref, gu_ref, dn_ref) = inputs
     xf_out, gu_out, dn_out = outs[8:11]
     (w_ref, xf_ref, at_sem), pair, feed_sems, rows_sems, rest = in_groups(refs, [3, 4, 4, 4, len(refs)])
@@ -703,19 +705,26 @@
     )
     rows = Gather(size, ("t",), xf_ref, xf_out, *rows_sems)
     if first:
-        at_sems, next_sems = in_groups(rest, [4, 4])
+        at_sems, next_sems, side_sems = in_groups(rest, [4, 4, 4])
+        side = Gather(size, ("t",), far_rows[0], outs[13], *side_sems)
         attention = Gather(size, bits, at_ref, w_ref, *at_sems)
         ahead = Gather(size, bits, more_ref, outs[12], *next_sems)
         moved = pltpu.make_async_copy(w_ref, outs[11], at_sem)
         attention.begin()
+        side.begin()
         feed.begin()
         work.begin(x_ref[...].astype(F32))
         attention.step(1)
+        side.step(1)
         attention.step(2)
         attention.on_bits(0)
+        side.on_bits(0)
+        side.step(2)
+        feed.send(1)
         attention.step(3)
-        feed.send(1)
         attention.on_bits(1)
+        side.on_bits(1)
+        side.step(3)
         attention.on_bits(2)
         attention.on_bits(3)
         attention.settle()
@@ -724,7 +733,9 @@
         feed.sent(1)
         feed.send(3)
         feed.step(1)
-        steps = (attention, ahead)
+        side.on_bits(2)
+        side.on_bits(3)
+        steps = (attention, ahead, side)
     else:
         total_ref, *rest = rest
         side = Relay(size, ("t",), more_ref, total_ref, *rest)
@@ -784,7 +795,7 @@
         item.end()
 
 
-def front(x, more, gains, bias, tables, at, gu, dn, layer, size, bits, block, width, collective_id):
+def front(x, more, gains, bias, tables, at, gu, dn, late, layer, size, bits, block, width, collective_id):
     slots = size * 2 ** len(bits)
     count, model = x.shape
     few, half = dn.shape[1:]
@@ -795,7 +806,7 @@
     shape = jax.ShapeDtypeStruct
     weight = (slots, few, at.shape[-1])
     more_scratch = (
-        gather_semaphores(size, bits) * 2
+        [*gather_semaphores(size, bits) * 2, *gather_semaphores(size, ("t",))]
         if first
         else [pltpu.VMEM((count, model), F32), *scatter_scratch(size, ("t",), count, model)]
     )
@@ -814,9 +825,10 @@
             shape((slots, few, 2 * block), LOW),
             shape((slots, few, block), LOW),
             *([shape(weight, LOW)] * 2 if first else []),
+            *([shape((2 * size, count, model), LOW)] if first else []),
         ),
-        in_specs=[held, far] + [held] * 6 + [far] * 3,
-        out_specs=[held] * 8 + [far] * (5 if first else 3),
+        in_specs=[held, far] + [held] * 6 + [far] * (3 + len(late)),
+        out_specs=[held] * 8 + [far] * (6 if first else 3),
         scratch_shapes=[
             pltpu.VMEM(weight, LOW),
             pltpu.VMEM((count, model), LOW),
@@ -834,7 +846,7 @@
         ],
         compiler_params=comm_params(collective_id),
         cost_estimate=at_microseconds(150),
-    )(x, more, *gains, bias, *tables, at, gu, dn)
+    )(x, more, *gains, bias, *tables, at, gu, dn, *late)
 
 
 class AttendBack:
@@ -1317,14 +1329,13 @@
             start, more, weight = middle, in_slots(partial, 2 * LINE), attn_weights[layer]
         out = front(
             start, more, gains, bias_all[layer : layer + 1], tables, weight, w_gateup, w_down,
-            layer, LINE, bits, block, qkv_width, 8 + layer,
+            [cotangent] if layer == 0 else [], layer, LINE, bits, block, qkv_width, 8 + layer,
         )
         (state, middle, xa_all, query, key, value, log_total, attended) = out[:8]
         xf_all, gu_w, down_w = (item.reshape(-1, item.shape[2]) for item in out[8:11])
         if layer == 0:
-            attn_weights = out[11:]
-            xf_all, late = lax.optimization_barrier((xf_all, cotangent))
-            gm_all = lax.all_gather(late, ("z", "t"), axis=0, tiled=True)
+            attn_weights = out[11:13]
+            gm_all = out[13].reshape(-1, cotangent.shape[1])
         both_w = attn_weights[layer]
         gate_up = jnp.dot(xf_all, gu_w, preferred_element_type=F32)
         gate = gate_up[:, :block]

time: 789 us -> 788 us (level)
  matrix products: 116 us -> 103 us
  local copies, waits for them, and re-layouts: 22.6 us -> 30.6 us
    dot_general x4, matrix products: 46.5 us -> 35.2 us  [contract_first(): lax.dot_general(left, right, (((0,), (0,)), ((), ())), preferred_element_...]
    dot_general x2 -> x4, local copies, waits for them, and re-layouts: 9.5 us -> 17.5 us  [contract_first(): lax.dot_general(left, right, (((0,), (0,)), ((), ())), preferred_element_...]
  transfers between devices with their start and end apart: 5 -> 4, of which waited for: 0 -> 0; matrix products, arithmetic and copies ran while one was open for 10% -> 6% of each run, Pallas kernels for 40% -> 19%
where the time goes in v8:
time: 788 us; the launch traced here: 773 us
  Pallas kernels  604 us (77%)
  matrix products  103 us (13%)
  local copies, waits for them, and re-layouts  30.6 us (4%)
  between operations  17.1 us (2%)
  starting transfers between devices  9.55 us (1%)
  other arithmetic  8.8 us (1%)
    pallas_call x2, Pallas kernels, front(): pl.pallas_call(functools.partial(front_kernel, size, bits, block, half, l...  319 us
    pallas_call x2, Pallas kernels, back(): pl.pallas_call(functools.partial(back_kernel, size, bits, width, (top, bo...  278 us
    dot_general x4, matrix products, contract_first(): lax.dot_general(left, right, (((0,), (0,)), ((), ())), preferred_element_...  35.2 us
    dot_general x4, matrix products, contract_last(): lax.dot_general(left, right, (((1,), (1,)), ((), ())), preferred_element_...  29.6 us
    dot_general x2, matrix products, local(): gate_up = jnp.dot(xf_all, gu_w, preferred_element_type=F32)  22.3 us
    dot_general x4, local copies, waits for them, and re-layouts, contract_first(): lax.dot_general(left, right, (((0,), (0,)), ((), ())), preferred_element_...  17.5 us
  transfers between devices with their start and end apart: 4, of which 0 were waited for; matrix products, arithmetic and copies ran while one was open for 6% of the time, Pallas kernels for 19%

profile of v8, /device:TPU:26, one launch (start us, length us, event | category | flops | bytes accessed | tf_op | source)
XLA Modules:
  0.0 772.5 jit_solution(9222281090452268121)
XLA Ops:
  7.2 0.0 reduce-scatter.2.cloned.1.call-start
  7.3 1.4 fusion.28
  11.2 2.6 convert_add_fusion
  13.8 0.5 multiply_sine_fusion
  14.4 0.8 pad_maximum_fusion.2.refs_5_.refs_9_.refs_8_
  15.1 0.8 fusion.19.refs_7_.refs_11_.refs_10_
  16.0 1.0 slice_bitcast_fusion
  17.0 1.0 slice_bitcast_fusion.2
  18.0 1.4 fusion.27
  19.4 0.7 negate_select_fusion.refs_6_.refs_10_.refs_9_
  20.1 1.4 fusion.25
  21.5 0.9 pad_maximum_fusion
  22.4 179.5 %shard_map.169 = (f32[128,1536]{1,0:T(8,128)}, f32[128,1536]{1,0:T(8,128)}, bf16[2,128,1536]{2,1,0:T(8,128)(2,1)}, bf16[256,768]{1,0:T(8,128)(2,1)}, bf16[256,12...) custom-call(bf16[128,1536]{1,0:T(8,128)(2,1)} %refs_0_.1, ...), custom_call_target="tpu_custom_call" | custom-call | bytes 525000000 | tf_op jit(solution)/shard_map/pallas_call | solution.py:813
  201.9 4.8 copy.20
  206.7 9.5 %fusion.29 = f32[1024,2304]{1,0:T(8,128)S(1)} fusion(bf16[1024,1536]{1,0:T(8,128)(2,1)S(1)} %bitcast.81, bf16[1536,2304]{1,0:T(8,128)(2,1)} %bitcast.93), kind=kOutput, calls=%fused_computation.61 | convolution fusion | flops 7247757312 | bytes 19660800 | tf_op jit(solution)/shard_map/dot_general | solution.py:1340
  216.2 1.6 select_convert_fusion.5
  217.8 2.8 copy-done
  220.6 0.2 copy-done.14
  220.9 5.6 fusion.30.refs_1_
  226.5 139.2 %shard_map.170 = (f32[128,1536]{1,0:T(8,128)}, f32[128,1536]{1,0:T(8,128)}, bf16[2,128,1536]{2,1,0:T(8,128)(2,1)}, bf16[256,768]{1,0:T(8,128)(2,1)}, bf16[256,12...) custom-call(f32[128,1536]{1,0:T(8,128)} %get-tuple-element.53.refs_0, ...), custom_call_target="tpu_custom_call" | custom-call | bytes 525000000 | tf_op jit(solution)/shard_map/pallas_call | solution.py:813
  365.7 4.8 copy.19
  370.5 12.8 %fusion.31 = f32[1024,2304]{1,0:T(8,128)} fusion(bf16[1024,1536]{1,0:T(8,128)(2,1)S(1)} %bitcast.88, bf16[1536,2304]{1,0:T(8,128)(2,1)} %bitcast.97), kind=kOutput, calls=%fused_computation.63 | convolution fusion | flops 7247757312 | bytes 19660800 | tf_op jit(solution)/shard_map/dot_general | solution.py:1340
  383.3 8.8 %select_convert_fusion.4 = (bf16[1024,1152]{1,0:T(8,128)(2,1)S(1)}, bf16[1024,1152]{1,0:T(8,128)(2,1)S(1)}, bf16[1024,1152]{1,0:T(8,128)(2,1)S(1)}) fusion(f32[1024,2304]{1,0:T(8,128)} %fusion.31, pred[1152]{0:T(1024)(128)(4,1)S(1)} %iota_compare_fusion.1, bf16[1024,1536]{1,0:T(8,128)(2,1)S(1)} %bitcast.85, bf16[1536,1152]{1,0:T(8,128)(2,1)S(1)} %bitcast.103), kind=kOutput, calls=%fused_computation.20 | convolution fusion | flops 3646291968 | bytes 23200896 | tf_op jit(solution)/shard_map/dot_general | solution.py:1355
  392.1 5.7 fusion.16.refs_3_
  397.7 5.8 fusion.32.refs_1_
  403.6 9.6 %fusion.4.refs_2_ = bf16[16,96,2304]{2,1,0:T(8,128)(2,1)} fusion(bf16[16,96,1024]{2,1,0:T(8,128)(2,1)S(1)} %bitcast.89, bf16[1024,1152]{1,0:T(8,128)(2,1)S(1)} %get-tuple-element.100, bf16[1024,1152]{1,0:T(8,128)(2,1)S(1)} %get-tuple-element.99), kind=kOutput, calls=%fused_computation.5 | convolution fusion | flops 7257194496 | bytes 14942208 | tf_op jit(solution)/shard_map/dot_general | solution.py:50
  413.2 9.3 %fusion.refs_0_ = bf16[8,128,1536]{2,1,0:T(8,128)(2,1)} fusion(bf16[1536,2304,1]{1,0,2:T(8,128)(2,1)S(1)} %bitcast.100, bf16[8,128,1152]{2,1,0:T(8,128)(2,1)S(1)} %bitcast.106, bf16[8,128,1152]{2,1,0:T(8,128)(2,1)S(1)} %bitcast.105), kind=kOutput, calls=%fused_computation | convolution fusion | flops 7257194496 | bytes 14942208 | tf_op jit(solution)/shard_map/dot_general | solution.py:46
  422.5 128.9 %shard_map.171 = (f32[128,1536]{1,0:T(8,128)}, bf16[2,128,1536]{2,1,0:T(8,128)(2,1)}, bf16[2,128,1024]{2,1,0:T(8,128)(2,1)}, f32[1,1024]{1,0:T(1,128)}, f32[1,15...) custom-call(bf16[8,128,1536]{2,1,0:T(8,128)(2,1)} %fusion.refs_0_, ...), custom_call_target="tpu_custom_call" | custom-call | bytes 525000000 | tf_op jit(solution)/shard_map/pallas_call | solution.py:1184
  551.3 0.0 reduce-scatter.2.cloned.1.call-update
  551.4 2.2 collective-permute-start
  553.5 5.4 collective-permute-start.1
  558.9 2.0 collective-permute-start.2
  560.9 2.9 copy.22
  563.8 5.1 copy.21
  568.9 8.8 %fusion.14.refs_2_ = bf16[16,96,1152]{2,1,0:T(8,128)(2,1)} fusion(bf16[16,96,1024]{2,1,0:T(8,128)(2,1)} %bitcast.91, bf16[1024,1152]{1,0:T(8,128)(2,1)S(1)} %copy-done.11), kind=kOutput, calls=%fused_computation.24 | convolution fusion | flops 3623878656 | bytes 9043968 | tf_op jit(solution)/shard_map/dot_general | solution.py:50
  577.7 0.0 copy-start.9
  577.7 0.0 slice-start.3
  577.7 6.8 select_convert_fusion.1
  584.5 11.2 %fusion.11.refs_1_ = bf16[16,96,2304]{2,1,0:T(8,128)(2,1)} fusion(bf16[16,96,1024]{2,1,0:T(8,128)(2,1)S(1)} %bitcast.90, bf16[1024,1152]{1,0:T(8,128)(2,1)} %get-tuple-element.98, bf16[1024,1152]{1,0:T(8,128)(2,1)S(1)} %get-tuple-element.97), kind=kOutput, calls=%fused_computation.13 | convolution fusion | flops 7257194496 | bytes 14942208 | tf_op jit(solution)/shard_map/dot_general | solution.py:50
  595.8 8.9 %fusion.7.refs_0_ = bf16[8,128,1536]{2,1,0:T(8,128)(2,1)} fusion(bf16[1536,2304,1]{1,0,2:T(8,128)(2,1)S(1)} %bitcast.96, bf16[8,128,1152]{2,1,0:T(8,128)(2,1)S(1)} %bitcast.108, bf16[8,128,1152]{2,1,0:T(8,128)(2,1)S(1)} %bitcast.107), kind=kOutput, calls=%fused_computation.8 | convolution fusion | flops 7257194496 | bytes 14942208 | tf_op jit(solution)/shard_map/dot_general | solution.py:46
  604.7 148.6 %shard_map.172 = (f32[128,1536]{1,0:T(8,128)}, bf16[2,128,1536]{2,1,0:T(8,128)(2,1)}, bf16[2,128,1024]{2,1,0:T(8,128)(2,1)}, f32[1,1024]{1,0:T(1,128)}, f32[1,15...) custom-call(bf16[8,128,1536]{2,1,0:T(8,128)(2,1)} %fusion.7.refs_0_,, ...), custom_call_target="tpu_custom_call" | custom-call | bytes 17500000 | tf_op jit(solution)/shard_map/pallas_call | solution.py:1184
  753.3 1.5 fusion.24
  754.8 1.4 constant_dynamic-slice_fusion
  756.2 0.8 add_convert_fusion
  757.0 0.0 collective-permute-done.refs_1_
  757.0 0.0 reduce-scatter.2.cloned.1.call-done.refs_6_
  757.1 7.5 shard_map.173
  764.6 0.9 copy.24
  (54 shorter events, 0.1 us)
Async XLA Ops:
  7.2 749.9 %reduce-scatter.2.cloned.1.call-start = ((), (), s32[]{:S(2)}) async-start(), calls=%async_computation.1 | async-start | bytes 5849088 | tf_op jit(solution)/shard_map/reduce_scatter | solution.py:1386
  201.9 4.8 copy-start.2
  216.2 4.4 copy-start
  216.2 4.7 copy-start.14
  220.6 5.8 copy-start.10
  365.7 4.8 copy-start.7
  370.5 12.8 %copy-start.5 = (bf16[8,128,1536]{2,1,0:T(8,128)(2,1)S(1)}, bf16[8,128,1536]{2,1,0:T(8,128)(2,1)}, u32[]{:S(2)}) copy-start(bf16[8,128,1536]{2,1,0:T(8,128)(2,1)} %get-tuple-element.59) | copy-start | bytes 9437188
  370.5 12.8 %copy-start.16 = (bf16[16,96,1152]{2,1,0:T(8,128)(2,1)S(1)}, bf16[16,96,1152]{2,1,0:T(8,128)(2,1)}, u32[]{:S(2)}) copy-start(bf16[16,96,1152]{2,1,0:T(8,128)(2,1)} %get-tuple-element.60) | copy-start | bytes 10616836
  383.3 8.8 %copy-start.6 = (bf16[1536,1024]{1,0:T(8,128)(2,1)S(1)}, bf16[1536,1024]{1,0:T(8,128)(2,1)}, u32[]{:S(2)}) copy-start(bf16[1536,1024]{1,0:T(8,128)(2,1)} %copy.20) | copy-start | bytes 9437188
  397.7 5.8 copy-start.8
  397.7 15.4 %slice-start.5 = ((s8[7077888]{0:T(1024)(128)(4,1)}), s8[4194304]{0:T(1024)(128)(4,1)S(1)}, s32[]{:S(2)}) async-start(s8[7077888]{0:T(1024)(128)(4,1)} %bitcast.98), calls=%async_computation.7 | async-start | bytes 8388608
  403.6 9.6 %slice-start.6 = ((s8[7077888]{0:T(1024)(128)(4,1)}), s8[2883584]{0:T(1024)(128)(4,1)S(1)}, s32[]{:S(2)}) async-start(s8[7077888]{0:T(1024)(128)(4,1)} %bitcast.98), calls=%async_computation.8 | async-start | bytes 5767168
  551.3 9.6 %copy-start.3 = (bf16[8,128,1536]{2,1,0:T(8,128)(2,1)S(1)}, bf16[8,128,1536]{2,1,0:T(8,128)(2,1)}, u32[]{:S(2)}) copy-start(bf16[8,128,1536]{2,1,0:T(8,128)(2,1)} %get-tuple-element.71) | copy-start | bytes 9437188
  551.4 205.7 %collective-permute-start = (bf16[96,3456]{1,0:T(8,128)(2,1)}, bf16[96,3456]{1,0:T(8,128)(2,1)}, u32[]{:S(2)}, u32[]{:S(2)}) collective-permute-start(bf16[96,3456]{1,0:T(8,128)(2,1)} %get-tuple-element.87), channel_id=1, source_target_pairs={{0,8},{8,16},{16,24},{24,0},{1,9},{9,17},{17,25},{25,1},{2,10},{10... | collective-permute-start | bytes 1990664 | tf_op jit(solution)/shard_map/ppermute | solution.py:1374
  553.5 203.5 %collective-permute-start.1 = (bf16[96,3456]{1,0:T(8,128)(2,1)}, bf16[96,3456]{1,0:T(8,128)(2,1)}, u32[]{:S(2)}, u32[]{:S(2)}) collective-permute-start(bf16[96,3456]{1,0:T(8,128)(2,1)} %get-tuple-element.88), channel_id=1, source_target_pairs={{0,16},{8,24},{16,0},{24,8},{1,17},{9,25},{17,1},{25,9},{2,18},{10... | collective-permute-start | bytes 1990664 | tf_op jit(solution)/shard_map/ppermute | solution.py:1374
  558.9 198.1 %collective-permute-start.2 = (bf16[96,3456]{1,0:T(8,128)(2,1)}, bf16[96,3456]{1,0:T(8,128)(2,1)}, u32[]{:S(2)}, u32[]{:S(2)}) collective-permute-start(bf16[96,3456]{1,0:T(8,128)(2,1)} %get-tuple-element.89), channel_id=1, source_target_pairs={{0,24},{8,0},{16,8},{24,16},{1,25},{9,1},{17,9},{25,17},{2,26},{10... | collective-permute-start | bytes 1990664 | tf_op jit(solution)/shard_map/ppermute | solution.py:1374
  563.8 5.1 copy-start.11
  563.8 13.8 %slice-start = ((s8[9437184]{0:T(1024)(128)(4,1)}), s8[1048576]{0:T(1024)(128)(4,1)S(1)}, s32[]{:S(2)}) async-start(s8[9437184]{0:T(1024)(128)(4,1)} %bitcast.77), calls=%async_computation.2 | async-start | bytes 2097152
  568.8 8.8 %slice-start.1 = ((s8[9437184]{0:T(1024)(128)(4,1)}), s8[4194304]{0:T(1024)(128)(4,1)S(1)}, s32[]{:S(2)}) async-start(s8[9437184]{0:T(1024)(128)(4,1)} %bitcast.77), calls=%async_computation.3 | async-start | bytes 8388608
  568.8 8.8 %slice-start.2 = ((s8[9437184]{0:T(1024)(128)(4,1)}), s8[4194304]{0:T(1024)(128)(4,1)S(1)}, s32[]{:S(2)}) async-start(s8[9437184]{0:T(1024)(128)(4,1)} %bitcast.77), calls=%async_computation.4 | async-start | bytes 8388608
  568.9 8.8 %copy-start.4 = (bf16[8,128,1536]{2,1,0:T(8,128)(2,1)S(1)}, bf16[8,128,1536]{2,1,0:T(8,128)(2,1)}, u32[]{:S(2)}) copy-start(bf16[8,128,1536]{2,1,0:T(8,128)(2,1)} %get-tuple-element.71) | copy-start | bytes 9437188
  568.9 8.8 %copy-start.15 = (bf16[16,96,1152]{2,1,0:T(8,128)(2,1)S(1)}, bf16[16,96,1152]{2,1,0:T(8,128)(2,1)}, u32[]{:S(2)}) copy-start(bf16[16,96,1152]{2,1,0:T(8,128)(2,1)} %get-tuple-element.56) | copy-start | bytes 10616836
  577.7 6.9 copy-start.9
  577.7 18.1 %slice-start.3 = ((s8[7077888]{0:T(1024)(128)(4,1)}), s8[2883584]{0:T(1024)(128)(4,1)S(1)}, s32[]{:S(2)}) async-start(s8[7077888]{0:T(1024)(128)(4,1)} %bitcast.94), calls=%async_computation.5 | async-start | bytes 5767168
  584.5 11.2 %slice-start.4 = ((s8[7077888]{0:T(1024)(128)(4,1)}), s8[4194304]{0:T(1024)(128)(4,1)S(1)}, s32[]{:S(2)}) async-start(s8[7077888]{0:T(1024)(128)(4,1)} %bitcast.94), calls=%async_computation.6 | async-start | bytes 8388608
  584.5 11.2 %copy-start.17 = (bf16[1024,1152]{1,0:T(8,128)(2,1)S(1)}, bf16[1024,1152]{1,0:T(8,128)(2,1)}, u32[]{:S(2)}) copy-start(bf16[1024,1152]{1,0:T(8,128)(2,1)} %get-tuple-element.98) | copy-start | bytes 7077892
  604.6 151.5 %copy-start.1 = (f32[128,1536]{1,0:T(8,128)S(1)}, f32[128,1536]{1,0:T(8,128)}, u32[]{:S(2)}) copy-start(f32[128,1536]{1,0:T(8,128)} %get-tuple-element.58.refs_6_) | copy-start | bytes 2359300
  604.7 151.5 %copy-start.13 = (f32[128,1536]{1,0:T(8,128)S(1)}, f32[128,1536]{1,0:T(8,128)}, u32[]{:S(2)}) copy-start(f32[128,1536]{1,0:T(8,128)} %get-tuple-element.70) | copy-start | bytes 2359300
  753.3 11.3 %copy-start.12 = (f32[128,1536]{1,0:T(8,128)S(1)}, f32[128,1536]{1,0:T(8,128)}, u32[]{:S(2)}) copy-start(f32[128,1536]{1,0:T(8,128)} %get-tuple-element.136) | copy-start | bytes 2359300
Sparse Core Ops, SparseCore 0:
  551.5 111.6 reduce-scatter.1
